TPU v7x, 32 devices: a whole 2x2x4 slice. The times are simulated.
32 devices in a mesh: seg: 8 (over y, x, core), head: 4 (over z).
Axes of the slice: x: 2, y: 2, z: 4, core: 2. Of those that a mesh axis runs over, the one named last changes fastest.
Arguments:
- attn_query: bfloat16 [8, 1024, 3072], P(None, 'seg', 'head'), may hold values from -8 to 8
- attn_key: bfloat16 [8, 1024, 3072], P(None, 'seg', 'head'), may hold values from -8 to 8
- attn_value: bfloat16 [8, 1024, 3072], P(None, 'seg', 'head'), may hold values from -6 to 6
- prompt_len: int32 [8, 8], P(None, 'seg'), may hold values from 1 to 64, as said below
- ttt_weight: bfloat16 [3072, 9216], P(None, 'head'), may hold values from -0.109375 to 0.109375
- init_w1: float32 [48, 64, 256], P('head'), may hold values from -0.75 to 0.75
- init_w2t: float32 [48, 64, 256], P('head'), may hold values from -0.375 to 0.375
- step_rate: float32 [8, 48, 1024], P(None, 'head', 'seg'), may hold values from 0.005 to 0.05
Outputs:
- ttt_out: bfloat16 [8, 1024, 3072], P(None, 'seg', 'head')
Inputs may be any that keep to these rules, and one draw needn't show every extreme that they name: `prompt_len`: some entry equals 64.
All inputs are finite; a program needn't handle non-finite values.
Results may differ from a plain program's by a relative error of at most 0.008.
Values may be sent and summed in bfloat16 or wider, within the bound.
No kernel may reach another device: no remote copies, remote signals or barrier semaphores. Data moves between devices by JAX's collectives and lax.ppermute only.
A program may use at most 128 MiB of HBM per device.

v0:
```python
import jax
import jax.numpy as jnp
from jax import lax
from jax.sharding import PartitionSpec as P

MINI = 64
TEXT_SLOTS = 64


highest_precision = lax.Precision.HIGHEST
norm_epsilon = 1e-05
rms_epsilon = 1e-06


def normalize(values):
    center = values - jnp.mean(values, axis=-1, keepdims=True)
    spread = jnp.mean(center * center, axis=-1, keepdims=True)
    return center * lax.rsqrt(spread + norm_epsilon)


def fast_mlp(inputs, fast_weights):
    hidden = jax.nn.gelu(
        jnp.einsum("bmd,bdf->bmf", inputs, fast_weights[:, 0], precision=highest_precision),
        approximate=True,
    )
    return normalize(
        jnp.einsum("bmf,bdf->bmd", hidden, fast_weights[:, 1], precision=highest_precision)
    )


def minibatch(fast_weights, batch_items):
    queries, key_rows, value_rows, step_rates = batch_items
    target = value_rows - key_rows

    def loss_value(weights_now):
        error = fast_mlp(key_rows, weights_now) - target
        return 0.5 * jnp.sum(step_rates[:, :, None] * error * error) / step_rates.shape[-1]

    gradient = jax.grad(loss_value)(fast_weights)
    fast_weights = fast_weights - gradient
    return (fast_weights, queries + fast_mlp(queries, fast_weights))


def run_items(fast_weights, picked, step_rates):
    batch = picked.shape[0]
    seg_len = picked.shape[2]
    head_dim = picked.shape[3]
    block_count = seg_len // MINI

    def to_blocks(array):
        return array.reshape(batch, block_count, MINI, head_dim).transpose(1, 0, 2, 3)

    rate_blocks = step_rates.reshape(batch, block_count, MINI).transpose(1, 0, 2)
    fast_weights, outputs = lax.scan(
        minibatch,
        fast_weights,
        (to_blocks(picked[:, 0]), to_blocks(picked[:, 1]), to_blocks(picked[:, 2]), rate_blocks),
    )
    return (fast_weights, outputs.transpose(1, 0, 2, 3).reshape(batch, seg_len, head_dim))


def body(attn_query, attn_key, attn_value, prompt_len, ttt_weight, init_w1, init_w2t, step_rate):
    videos = attn_query.shape[0]
    seg_len = attn_query.shape[1]
    heads_dev = init_w1.shape[0]
    head_dim = init_w1.shape[1]
    position = lax.broadcasted_iota(jnp.int32, (videos, seg_len), 1)
    usable = (position >= TEXT_SLOTS) | (position < prompt_len)
    queries = attn_query.reshape(videos, seg_len, heads_dev, head_dim)
    key_rows = attn_key.reshape(videos, seg_len, heads_dev, head_dim)
    value_rows = attn_value.reshape(videos, seg_len, heads_dev, head_dim)
    scores = jnp.einsum(
        "vqhd,vkhd->vhqk", queries, key_rows, preferred_element_type=jnp.float32
    ) * head_dim ** (-0.5)
    scores = jnp.where(usable[:, None, None, :], scores, -1e30)
    largest = jnp.max(scores, axis=-1, keepdims=True)
    exponent = jnp.exp(scores - largest)
    weights = (exponent / jnp.sum(exponent, axis=-1, keepdims=True)).astype(jnp.bfloat16)
    attended = jnp.einsum(
        "vhqk,vkhd->vqhd", weights, value_rows, preferred_element_type=jnp.float32
    )
    attended = attended.astype(jnp.bfloat16).reshape(videos, seg_len, heads_dev * head_dim)
    features = lax.all_gather(attended, "head", axis=2, tiled=True)
    feature_full = features.astype(jnp.float32)
    normed = (
        feature_full
        * lax.rsqrt(jnp.mean(feature_full * feature_full, axis=-1, keepdims=True) + rms_epsilon)
    ).astype(jnp.bfloat16)
    projected = jnp.dot(
        normed.reshape(videos * seg_len, normed.shape[2]),
        ttt_weight,
        preferred_element_type=jnp.float32,
    )
    projected = projected.reshape(videos, seg_len, heads_dev, 3, head_dim).transpose(0, 2, 3, 1, 4)
    step_rates = step_rate * usable[:, None, :].astype(jnp.float32)
    init_stack = jnp.stack([init_w1, init_w2t], axis=1)
    seg_count = lax.axis_size("seg")
    item_count = videos * heads_dev
    per_device = (item_count + seg_count - 1) // seg_count
    padded = per_device * seg_count
    item_inputs = projected.reshape(item_count, 3, seg_len, head_dim)
    item_inputs = jnp.pad(item_inputs, ((0, padded - item_count), (0, 0), (0, 0), (0, 0)))
    item_rates = step_rates.reshape(item_count, 1, seg_len, 1)
    item_rates = jnp.pad(item_rates, ((0, padded - item_count), (0, 0), (0, 0), (0, 0)))
    sequences, rate_rows = (
        lax.all_to_all(
            item_inputs.astype(jnp.bfloat16), "seg", split_axis=0, concat_axis=2, tiled=True
        ).astype(item_inputs.dtype),
        lax.all_to_all(
            item_rates.astype(jnp.bfloat16), "seg", split_axis=0, concat_axis=2, tiled=True
        ).astype(item_rates.dtype),
    )
    item_global = lax.axis_index("seg") * per_device + jnp.arange(per_device, dtype=jnp.int32)
    head_of = item_global % heads_dev
    start = jnp.take(init_stack, head_of, axis=0)
    final_weights, outputs = run_items(
        start, sequences, rate_rows.reshape(per_device, sequences.shape[2])
    )
    returned = lax.all_to_all(
        outputs.astype(jnp.bfloat16), "seg", split_axis=1, concat_axis=0, tiled=True
    ).astype(outputs.dtype)
    results = returned[:item_count].reshape(videos, heads_dev, seg_len, head_dim)
    results = results.transpose(0, 2, 1, 3).reshape(videos, seg_len, heads_dev * head_dim)
    return results.astype(jnp.bfloat16)


def solution(mesh):
    return jax.shard_map(
        body,
        mesh=mesh,
        in_specs=(
            P(None, "seg", "head"),
            P(None, "seg", "head"),
            P(None, "seg", "head"),
            P(None, "seg"),
            P(None, "head"),
            P("head", None, None),
            P("head", None, None),
            P(None, "head", "seg"),
        ),
        out_specs=P(None, "seg", "head"),
        check_vma=False,
    )
```

profile of v0, /device:TPU:0, one launch (start us, length us, event | category | flops | bytes accessed | tf_op | source)
XLA Modules:
  0.0 675.3 jit_solution(10755237393714331353)
XLA Ops:
  6.6 2.7 copy.89
  11.8 7.2 %fusion.99 = (f32[8,12,128]{2,1,0:T(8,128)S(1)}, f32[8,12,128,128]{2,3,1,0:T(8,128)}) fusion(pred[8,128]{1,0:T(8,128)(4,1)S(1)} %get-tuple-element.150, bf16[8,128,12,64]{1,3,2,0:T(8,128)(2,1)} %bitcast.185, bf16[8,128,12,64]{1,3,2,0:T(8,128)(2,1)} %bitcast.186), kind=kOutput, calls=%fused_computation.143 | convolution fusion | flops 207618176 | bytes 9487360 | tf_op jit(solution)/shard_map/sub | solution.py:77
  19.1 3.8 fusion.87
  26.5 5.2 all-to-all-start
  31.7 18.8 %copy.94 = bf16[3072,2304]{0,1:T(8,128)(2,1)} copy(bf16[3072,2304]{1,0:T(8,128)(2,1)} %param.14) | data formatting | bytes 28311552 | tf_op args[4]
  50.5 92.2 %all-gather.2.cloned.1.call-done = bf16[8,128,3072]{2,1,0:T(8,128)(2,1)} async-done(((bf16[8,128,768]{2,1,0:T(8,128)(2,1)}), bf16[8,128,3072]{2,1,0:T(8,128)(2,1)}) %all-gather.2.cloned.1.call-update) | async-done | bytes 6291472 | tf_op jit(solution)/shard_map/all_gather | solution.py:83
  142.6 4.2 fusion.73
  147.2 19.0 %fusion.84 = bf16[8,128,12,3,64]{1,4,3,2,0:T(8,128)(2,1)} fusion(bf16[12,3,64,3072,1]{3,2,1,0,4:T(8,128)(2,1)} %bitcast.175, bf16[8,128,3072]{2,1,0:T(8,128)(2,1)S(1)} %copy-done.2, f32[8,128]{1,0:T(8,128)S(1)} %add_rsqrt_fusion.1), kind=kOutput, calls=%fused_computation.118 | convolution fusion | flops 14507311104 | bytes 25169920 | tf_op jit(solution)/shard_map/dot_general | solution.py:89
  166.3 4.9 all-to-all-start.1
  173.4 52.4 %all-to-all-done.1 = bf16[96,3,128,64]{2,3,1,0:T(8,128)(2,1)} async-done(((bf16[96,3,128,64]{2,3,1,0:T(8,128)(2,1)}), bf16[96,3,128,64]{2,3,1,0:T(8,128)(2,1)}, u32[]{:S(2)}, u32[]{:S(2)}) %all-to-all-start.1) | async-done | bytes 4718624 | tf_op jit(solution)/shard_map/all_to_all | solution.py:106
  225.8 3.6 copy_bitcast_fusion.1
  229.4 3.8 fusion.98
  233.2 5.7 reshape_squeeze.9
  238.9 5.7 reshape_squeeze.10
  244.6 5.7 reshape_squeeze.11
  250.3 371.7 %while.14 = (s32[]{:T(128)}, f32[12,2,64,256]{3,2,0,1:T(8,128)S(1)}, bf16[16,12,64,64]{3,2,1,0:T(8,128)(2,1)}, f32[16,12,64]{2,0,1:T(8,128)}, f32[16,12,64,64]{2...) while((s32[]{:T(128)}, f32[12,2,64,256]{3,2,0,1:T(8,128)S(1)}, ...), condition=%wide.region_10.11_spmd, body=%wide.region_3.0_spmd.sunk | while | flops 1067981568 | bytes 30627536 | solution.py:54
  250.3 2.2 constant_dynamic-slice_fusion.7
  256.5 3.6 constant_dynamic-slice_fusion.8
  264.9 2.3 convolution_bitcast_fusion.5
  273.5 2.2 constant_dynamic-slice_fusion.7
  279.7 3.6 constant_dynamic-slice_fusion.8
  288.1 2.3 convolution_bitcast_fusion.5
  296.8 2.2 constant_dynamic-slice_fusion.7
  302.9 3.6 constant_dynamic-slice_fusion.8
  311.4 2.3 convolution_bitcast_fusion.5
  320.0 2.2 constant_dynamic-slice_fusion.7
  326.2 3.6 constant_dynamic-slice_fusion.8
  334.6 2.3 convolution_bitcast_fusion.5
  343.2 2.2 constant_dynamic-slice_fusion.7
  349.4 3.6 constant_dynamic-slice_fusion.8
  357.8 2.3 convolution_bitcast_fusion.5
  366.5 2.2 constant_dynamic-slice_fusion.7
  372.7 3.6 constant_dynamic-slice_fusion.8
  381.1 2.3 convolution_bitcast_fusion.5
  395.9 3.6 constant_dynamic-slice_fusion.8
  404.3 2.3 convolution_bitcast_fusion.5
  412.9 2.2 constant_dynamic-slice_fusion.7
  419.1 3.6 constant_dynamic-slice_fusion.8
  427.5 2.3 convolution_bitcast_fusion.5
  442.4 3.6 constant_dynamic-slice_fusion.8
  450.8 2.3 convolution_bitcast_fusion.5
  465.6 3.6 constant_dynamic-slice_fusion.8
  474.0 2.3 convolution_bitcast_fusion.5
  488.8 3.6 constant_dynamic-slice_fusion.8
  497.2 2.3 convolution_bitcast_fusion.5
  505.9 2.2 constant_dynamic-slice_fusion.7
  512.0 3.6 constant_dynamic-slice_fusion.8
  520.5 2.3 convolution_bitcast_fusion.5
  529.1 2.2 constant_dynamic-slice_fusion.7
  535.3 3.6 constant_dynamic-slice_fusion.8
  543.7 2.3 convolution_bitcast_fusion.5
  558.5 3.6 constant_dynamic-slice_fusion.8
  566.9 2.3 convolution_bitcast_fusion.5
  575.6 2.2 constant_dynamic-slice_fusion.7
  581.7 3.6 constant_dynamic-slice_fusion.8
  590.2 2.3 convolution_bitcast_fusion.5
  598.8 2.2 constant_dynamic-slice_fusion.7
  605.0 3.6 constant_dynamic-slice_fusion.8
  613.4 2.3 convolution_bitcast_fusion.5
  622.0 6.5 copy.110
  628.5 5.8 reshape.221
  634.3 23.4 %all_to_all.12 = bf16[8,2,49152]{2,1,0:T(2,128)(2,1)S(1)} all-to-all(bf16[8,2,49152]{2,1,0:T(2,128)(2,1)S(1)} %reshape.221), channel_id=1, replica_groups=mesh['seg'=8,'head'=4] {'seg'}, dimensions={0} | all-to-all | bytes 3145728 | tf_op jit(solution)/shard_map/all_to_all | solution.py:119
  657.8 4.7 reshape.222
  662.5 4.4 copy.104
  (575 shorter events, 260.4 us)
Async XLA Ops:
  6.5 2.7 copy-start.4
  6.5 136.1 %all-gather.2.cloned.1.call-start = ((), (), s32[]{:S(2)}) async-start(), calls=%async_computation.3 | async-start | bytes 7864320 | tf_op jit(solution)/shard_map/all_gather | solution.py:83
  6.5 4.3 copy-start.5
  9.3 2.5 copy-start.10
  22.8 1.6 copy-start.9
  26.5 139.8 %all-to-all-start = ((bf16[8,2,768]{2,1,0:T(2,128)(2,1)}), bf16[8,2,768]{2,1,0:T(2,128)(2,1)S(1)}, u32[]{:S(2)}, u32[]{:S(2)}) async-start(bf16[8,2,768]{2,1,0:T(2,128)(2,1)} %reshape.219), calls=%async_computation | async-start | bytes 49152 | tf_op jit(solution)/shard_map/all_to_all | solution.py:109
  142.6 4.6 copy-start.2
  166.3 5.0 copy-start.7
  166.3 5.0 copy-start.8
  166.3 59.5 %all-to-all-start.1 = ((bf16[96,3,128,64]{2,3,1,0:T(8,128)(2,1)}), bf16[96,3,128,64]{2,3,1,0:T(8,128)(2,1)}, u32[]{:S(2)}, u32[]{:S(2)}) async-start(bf16[96,3,128,64]{2,3,1,0:T(8,128)(2,1)} %bitcast.180), calls=%async_computation.1 | async-start | bytes 9437184 | tf_op jit(solution)/shard_map/all_to_all | solution.py:106
  253.4 1.1 copy-start
  255.1 1.4 copy-start.3
  255.9 0.6 copy-start.6
  262.7 5.3 copy-start.1
  276.6 1.1 copy-start
  278.3 1.4 copy-start.3
  279.1 0.6 copy-start.6
  285.9 5.3 copy-start.1
  299.9 1.1 copy-start
  301.5 1.4 copy-start.3
  302.3 0.6 copy-start.6
  309.2 5.3 copy-start.1
  323.1 1.1 copy-start
  324.7 1.4 copy-start.3
  325.6 0.6 copy-start.6
  332.4 5.3 copy-start.1
  346.3 1.1 copy-start
  348.0 1.4 copy-start.3
  348.8 0.6 copy-start.6
  355.6 5.3 copy-start.1
  369.6 1.1 copy-start
  371.2 1.4 copy-start.3
  372.1 0.6 copy-start.6
  378.9 5.3 copy-start.1
  392.8 1.1 copy-start
  394.5 1.4 copy-start.3
  402.1 5.3 copy-start.1
  416.0 1.1 copy-start
  417.7 1.4 copy-start.3
  425.3 5.3 copy-start.1
  439.3 1.1 copy-start
  440.9 1.4 copy-start.3
  448.6 5.3 copy-start.1
  462.5 1.1 copy-start
  464.2 1.4 copy-start.3
  471.8 5.3 copy-start.1
  485.7 1.1 copy-start
  487.4 1.4 copy-start.3
  495.0 5.3 copy-start.1
  509.0 1.1 copy-start
  510.6 1.4 copy-start.3
  518.3 5.3 copy-start.1
  532.2 1.1 copy-start
  533.8 1.4 copy-start.3
  541.5 5.3 copy-start.1
  555.4 1.1 copy-start
  557.1 1.4 copy-start.3
  564.7 5.3 copy-start.1
  578.6 1.1 copy-start
  580.3 1.4 copy-start.3
  588.0 5.3 copy-start.1
  601.9 1.1 copy-start
  603.6 1.4 copy-start.3
  611.2 5.3 copy-start.1
  (10 other events, 6.0 us)
Sparse Core Ops, SparseCore 0:
  24.6 118.0 all-gather.1
where the time goes:
time: 681 us; the launch traced here: 675 us
  local copies, waits for them, and re-layouts  210 us (31%)
  matrix products  164 us (24%)
  waiting for transfers between devices  145 us (21%)
  other arithmetic  106 us (16%)
  blocking collectives  23.4 us (3%)
  between operations  13.6 us (2%)
  starting transfers between devices  10.1 us (1%)
    dynamic_slice x112, local copies, waits for them, and re-layouts, run_items(): lax.scan(minibatch, fast_weights, (to_blocks(picked[:, 0]), to_blocks(pic...  132 us
    all_gather x1, waiting for transfers between devices, body(): features = lax.all_gather(attended, 'head', axis=2, tiled=True)  92.2 us
    dot_general x64, matrix products, fast_mlp(): jnp.einsum('bmf,bdf->bmd', hidden, fast_weights[:, 1], precision=highest_...  85.6 us
    all_to_all x1, waiting for transfers between devices, body(): lax.all_to_all(item_inputs.astype(jnp.bfloat16), 'seg', split_axis=0, con...  52.4 us
    dot_general x48, matrix products, fast_mlp(): jnp.einsum('bmd,bdf->bmf', inputs, fast_weights[:, 0], precision=highest_...  48.1 us
    unnamed x23, local copies, waits for them, and re-layouts  36.1 us
    all_to_all x1, blocking collectives, body(): lax.all_to_all(outputs.astype(jnp.bfloat16), 'seg', split_axis=1, concat_...  23.4 us
    reduce_sum x16, other arithmetic, normalize(): center = values - jnp.mean(values, axis=-1, keepdims=True)  22.3 us
  transfers between devices with their start and end apart: 3, of which 2 were waited for; matrix products, arithmetic and copies ran while one was open for 7% of the time, Pallas kernels for 0%

commit v1 on v0

--- a/solution.py
+++ b/solution.py
@@ -1,15 +1,262 @@
+import functools
 import jax
 import jax.numpy as jnp
 from jax import lax
+from jax.experimental import pallas as pl
+from jax.experimental.pallas import tpu as pltpu
 from jax.sharding import PartitionSpec as P
 
+highest_precision = lax.Precision.HIGHEST
 MINI = 64
 TEXT_SLOTS = 64
-
-
-highest_precision = lax.Precision.HIGHEST
 norm_epsilon = 1e-05
 rms_epsilon = 1e-06
+VMEM_LIMIT = 56 * 1024 * 1024
+gelu_a = 0.7978845608028654
+gelu_b = gelu_a * 0.044715
+
+
+def dot_nn(a, b):
+    return lax.dot_general(a, b, (((1,), (0,)), ((), ())), preferred_element_type=jnp.float32)
+
+
+def dot_nt(a, b):
+    return lax.dot_general(a, b, (((1,), (1,)), ((), ())), preferred_element_type=jnp.float32)
+
+
+def low_half(shape, half):
+    return lax.broadcasted_iota(jnp.int32, shape, len(shape) - 1) < half
+
+
+def half_ones(half):
+    width = 2 * half
+    row = lax.broadcasted_iota(jnp.int32, (width, width), 0) < half
+    column = lax.broadcasted_iota(jnp.int32, (width, width), 1) < half
+    return (row == column).astype(jnp.bfloat16)
+
+
+def attention_kernel(lens_ref, q_ref, k_ref, v_ref, rate_ref, out_ref, *, half):
+    video = pl.program_id(0)
+    length = lens_ref[video]
+    seg_len = q_ref.shape[1]
+    channels = q_ref.shape[2]
+    width = 2 * half
+    heads = channels // half
+    key_at = lax.broadcasted_iota(jnp.int32, (seg_len, 2 * seg_len), 1)
+    key_at = jnp.where(key_at >= seg_len, key_at - seg_len, key_at)
+    usable = (key_at >= TEXT_SLOTS) | (key_at < length)
+    low = low_half((seg_len, width), half)
+    zero = jnp.zeros((seg_len, width), jnp.bfloat16)
+    ones = jnp.ones((seg_len, width), jnp.bfloat16)
+    scale = jnp.asarray(half ** (-0.5), jnp.bfloat16)
+    totals = jnp.concatenate([jnp.where(low, ones, zero), jnp.where(low, zero, ones)], axis=0)
+    for pair in range(channels // width):
+        lanes = slice(pair * width, (pair + 1) * width)
+        query = q_ref[0, :, lanes] * scale
+        key = k_ref[0, :, lanes]
+        value = v_ref[0, :, lanes]
+        keys = jnp.concatenate([jnp.where(low, key, zero), jnp.where(low, zero, key)], axis=0)
+        scores = jnp.where(usable, dot_nt(query, keys), -1e30)
+        parts = []
+        for side in range(2):
+            block = scores[:, side * seg_len : (side + 1) * seg_len]
+            largest = jnp.max(block, axis=1, keepdims=True)
+            parts.append(jnp.exp(block - largest).astype(jnp.bfloat16))
+        weights = jnp.concatenate(parts, axis=1)
+        values = jnp.concatenate([jnp.where(low, value, zero), jnp.where(low, zero, value)], axis=0)
+        mixed = dot_nn(weights, jnp.concatenate([values, totals], axis=1))
+        out_ref[0, :, lanes] = (mixed[:, :width] / mixed[:, width:]).astype(jnp.bfloat16)
+    token = lax.broadcasted_iota(jnp.int32, (seg_len, 1), 0)
+    open_token = ((token >= TEXT_SLOTS) | (token < length)).astype(jnp.float32)
+    rates = rate_ref[0]
+    spare = out_ref.shape[2] - channels
+    rates = jnp.concatenate(
+        [rates, jnp.zeros((spare - rates.shape[0], seg_len), jnp.float32)], axis=0
+    )
+    out_ref[0, :, channels:] = (rates.T * open_token).astype(jnp.bfloat16)
+
+
+def attention(attn_query, attn_key, attn_value, lens, step_rate, half):
+    videos, seg_len, channels = attn_query.shape
+    heads = step_rate.shape[1]
+    spare = 128
+    block = pl.BlockSpec((1, seg_len, channels), lambda v, lens: (v, 0, 0))
+    return pl.pallas_call(
+        functools.partial(attention_kernel, half=half),
+        grid_spec=pltpu.PrefetchScalarGridSpec(
+            num_scalar_prefetch=1,
+            grid=(videos,),
+            in_specs=[block, block, block, pl.BlockSpec((1, heads, seg_len), lambda v, lens: (v, 0, 0))],
+            out_specs=pl.BlockSpec((1, seg_len, channels + spare), lambda v, lens: (v, 0, 0)),
+        ),
+        out_shape=jax.ShapeDtypeStruct((videos, seg_len, channels + spare), jnp.bfloat16),
+        compiler_params=pltpu.CompilerParams(vmem_limit_bytes=VMEM_LIMIT),
+        name="attention",
+    )(lens, attn_query, attn_key, attn_value, step_rate)
+
+
+def project_kernel(row_ref, *refs, shards, half):
+    x_refs = refs[:shards]
+    rate_ref, w_ref, q_ref, k_ref, t_ref, e_ref, inv_ref = refs[shards:]
+    pair = pl.program_id(0)
+    tokens, depth = x_refs[0].shape
+    width = 2 * half
+
+    @pl.when(pair == 0)
+    def _():
+        total = jnp.zeros((tokens, 128), jnp.float32)
+        for x_ref in x_refs:
+            for at in range(0, depth, 128):
+                piece = x_ref[:, at : at + 128].astype(jnp.float32)
+                total = total + piece * piece
+        mean = jnp.sum(total, axis=1, keepdims=True) / (shards * depth)
+        inv_ref[...] = jnp.broadcast_to(lax.rsqrt(mean + rms_epsilon), inv_ref.shape)
+
+    acc = None
+    for i, x_ref in enumerate(x_refs):
+        rows = pl.ds(pl.multiple_of(row_ref[i] * depth, depth), depth)
+        term = dot_nn(x_ref[...], w_ref[rows, :])
+        acc = term if acc is None else acc + term
+    inv = inv_ref[...]
+    low = low_half((tokens, width), half)
+    first = acc[:, :width] * inv
+    middle = acc[:, width : 2 * width] * inv
+    last = acc[:, 2 * width :] * inv
+    query = jnp.where(low, first, middle)
+    key = pltpu.roll(jnp.where(low, last, first), half, 1)
+    target = jnp.where(low, middle, last) - key
+    zero = jnp.zeros_like(target)
+    total_low = jnp.sum(jnp.where(low, target, zero), axis=1, keepdims=True)
+    total_high = jnp.sum(jnp.where(low, zero, target), axis=1, keepdims=True)
+    target = target - jnp.where(low, total_low, total_high) * (1.0 / half)
+    q_ref[...] = query
+    k_ref[...] = key.astype(jnp.bfloat16)
+    t_ref[...] = target
+    head = lax.broadcasted_iota(jnp.int32, (rate_ref.shape[1], width), 0)
+    lane = lax.broadcasted_iota(jnp.int32, (rate_ref.shape[1], width), 1)
+    spread = (head == 2 * pair + (lane >= half).astype(jnp.int32)).astype(jnp.bfloat16)
+    e_ref[...] = dot_nn(rate_ref[...], spread) * (1.0 / MINI)
+
+
+def project(shards, rates, weight, row_blocks, half):
+    tokens, depth = shards[0].shape
+    width = 2 * half
+    pairs = weight.shape[1] // (3 * width)
+    whole = pl.BlockSpec((tokens, depth), lambda p, r: (0, 0))
+    piece = pl.BlockSpec((tokens, width), lambda p, r: (0, p))
+    out = lambda kind: jax.ShapeDtypeStruct((tokens, pairs * width), kind)
+    return pl.pallas_call(
+        functools.partial(project_kernel, shards=len(shards), half=half),
+        grid_spec=pltpu.PrefetchScalarGridSpec(
+            num_scalar_prefetch=1,
+            grid=(pairs,),
+            in_specs=[whole] * len(shards)
+            + [
+                pl.BlockSpec(rates.shape, lambda p, r: (0, 0)),
+                pl.BlockSpec((weight.shape[0], 3 * width), lambda p, r: (0, p)),
+            ],
+            out_specs=[piece] * 4,
+            scratch_shapes=[pltpu.VMEM((tokens, width), jnp.float32)],
+        ),
+        out_shape=[out(jnp.float32), out(jnp.bfloat16), out(jnp.float32), out(jnp.float32)],
+        compiler_params=pltpu.CompilerParams(vmem_limit_bytes=VMEM_LIMIT),
+        name="project",
+    )(row_blocks, *shards, rates, weight)
+
+
+def ttt_kernel(q_ref, k_ref, t_ref, e_ref, w1_in, w2_in, out_ref, w1_out, w2_out, w1_s, w2_s, *, half):
+    width = 2 * half
+    steps = q_ref.shape[0] // MINI
+    pairs = q_ref.shape[1] // width
+    hidden = w1_in.shape[2]
+    block_ones = half_ones(half)
+
+    w1_out[...] = w1_in[...]
+    w2_out[...] = w2_in[...]
+    for head in range(2 * pairs):
+        here = slice((head % 2) * half, (head % 2) * half + half)
+        other = slice(half - (head % 2) * half, 2 * half - (head % 2) * half)
+        w1_s[head, here, :] = w1_in[head].astype(jnp.bfloat16)
+        w1_s[head, other, :] = jnp.zeros((half, hidden), jnp.bfloat16)
+        w2_s[head, here, :] = w2_in[head].astype(jnp.bfloat16)
+        w2_s[head, other, :] = jnp.zeros((half, hidden), jnp.bfloat16)
+
+    def rows_of(step):
+        return pl.ds(pl.multiple_of(step * MINI, MINI), MINI)
+
+    def gelu_parts(value):
+        square = value * value
+        return square, jnp.tanh(value * (gelu_b * square + gelu_a))
+
+    def forward(pair, batch, grads):
+        hiddens, slopes = [], []
+        total = None
+        for side in range(2):
+            head = 2 * pair + side
+            value = dot_nn(batch, w1_s[head])
+            square, bent = gelu_parts(value)
+            doubled = (value + value * bent).astype(jnp.bfloat16)
+            if grads:
+                v, s, b = value[-MINI:], square[-MINI:], bent[-MINI:]
+                slopes.append((1.0 + b) + v * (1.0 - b * b) * (3.0 * gelu_b * s + gelu_a))
+                hiddens.append(doubled[-MINI:])
+            term = dot_nt(doubled, w2_s[head])
+            total = term if total is None else total + term
+        spread = dot_nn((total * total).astype(jnp.bfloat16), block_ones)
+        inverse = lax.rsqrt(spread * (1.0 / half) + 4.0 * norm_epsilon)
+        return total * inverse, inverse, hiddens, slopes
+
+    def update(pair, step, unit, inverse, hiddens, slopes):
+        lanes = slice(pair * width, (pair + 1) * width)
+        rows = rows_of(step)
+        grad = e_ref[rows, lanes] * (unit - t_ref[rows, lanes])
+        along = dot_nn((grad * unit).astype(jnp.bfloat16), block_ones) * (1.0 / half)
+        change = (inverse * (grad - unit * along)).astype(jnp.bfloat16)
+        change_t = change.T
+        key_t = k_ref[rows, lanes].T
+        for side in range(2):
+            head = 2 * pair + side
+            here = slice(side * half, side * half + half)
+            back = (dot_nn(change, w2_s[head]) * slopes[side]).astype(jnp.bfloat16)
+            w2 = w2_out[head] - dot_nn(change_t[here], hiddens[side])
+            w2_out[head] = w2
+            w1 = w1_out[head] - dot_nn(key_t[here], back)
+            w1_out[head] = w1
+            w2_s[head, here, :] = w2.astype(jnp.bfloat16)
+            w1_s[head, here, :] = w1.astype(jnp.bfloat16)
+
+    def one(step, with_query, with_key):
+        for pair in range(pairs):
+            lanes = slice(pair * width, (pair + 1) * width)
+            parts = []
+            if with_query:
+                query = q_ref[rows_of(step - 1), lanes]
+                parts.append(query.astype(jnp.bfloat16))
+            if with_key:
+                parts.append(k_ref[rows_of(step), lanes])
+            batch = jnp.concatenate(parts, axis=0) if len(parts) > 1 else parts[0]
+            unit, inverse, hiddens, slopes = forward(pair, batch, with_key)
+            if with_query:
+                out_ref[rows_of(step - 1), lanes] = (query + unit[:MINI]).astype(jnp.bfloat16)
+            if with_key:
+                update(pair, step, unit[-MINI:], inverse[-MINI:], hiddens, slopes)
+
+    one(0, False, True)
+    lax.fori_loop(1, steps, lambda step, carry: (one(step, True, True), carry)[1], 0)
+    one(steps, True, False)
+
+
+def ttt(query, key, target, rates, w1, w2, half):
+    hidden = w1.shape[2]
+    heads = w1.shape[0]
+    state = jax.ShapeDtypeStruct(w1.shape, jnp.float32)
+    return pl.pallas_call(
+        functools.partial(ttt_kernel, half=half),
+        out_shape=[jax.ShapeDtypeStruct(query.shape, jnp.bfloat16), state, state],
+        scratch_shapes=[pltpu.VMEM((heads, 2 * half, hidden), jnp.bfloat16)] * 2,
+        compiler_params=pltpu.CompilerParams(vmem_limit_bytes=VMEM_LIMIT),
+        name="fast_weights",
+    )(query, key, target, rates, w1, w2)
 
 
 def normalize(values):
@@ -59,7 +306,7 @@
     return (fast_weights, outputs.transpose(1, 0, 2, 3).reshape(batch, seg_len, head_dim))
 
 
-def body(attn_query, attn_key, attn_value, prompt_len, ttt_weight, init_w1, init_w2t, step_rate):
+def any_size(attn_query, attn_key, attn_value, prompt_len, ttt_weight, init_w1, init_w2t, step_rate):
     videos = attn_query.shape[0]
     seg_len = attn_query.shape[1]
     heads_dev = init_w1.shape[0]
@@ -124,6 +371,52 @@
     return results.astype(jnp.bfloat16)
 
 
+def gather_heads(block):
+    count = lax.axis_size("head")
+    me = lax.axis_index("head")
+    if count != 4:
+        every = lax.all_gather(block, "head", axis=0)
+        return [every[i] for i in range(count)], jnp.arange(count, dtype=jnp.int32)
+    near = lax.ppermute(block, "head", [(0, 1), (1, 0), (2, 3), (3, 2)])
+    far = lax.ppermute(block, "head", [(0, 2), (2, 0), (1, 3), (3, 1)])
+    inner = lax.ppermute(block, "head", [(1, 2), (2, 1)])
+    outer = lax.ppermute(far, "head", [(2, 3), (1, 0)])
+    last = jnp.where((me == 0) | (me == 3), outer, inner)
+    return [block, near, far, last], me ^ jnp.arange(4, dtype=jnp.int32)
+
+
+def by_video(attn_query, attn_key, attn_value, prompt_len, ttt_weight, init_w1, init_w2t, step_rate):
+    videos, seg_len, channels = attn_query.shape
+    half = init_w1.shape[1]
+    segments = lax.axis_size("seg")
+    mixed = attention(attn_query, attn_key, attn_value, prompt_len[:, 0], step_rate, half)
+    mine = lax.all_to_all(mixed, "seg", split_axis=0, concat_axis=0, tiled=True)
+    mine = mine.reshape(segments * seg_len, mixed.shape[2])
+    features = mine[:, :channels]
+    rates = mine[:, channels:]
+    w1 = init_w1
+    w2 = init_w2t - jnp.mean(init_w2t, axis=1, keepdims=True)
+    tokens = segments * seg_len
+    chunk = max(seg_len, tokens // 4)
+    outs = []
+    for at in range(0, tokens, chunk):
+        shards, row_blocks = gather_heads(features[at : at + chunk])
+        query, key, target, spread = project(shards, rates[at : at + chunk], ttt_weight, row_blocks, half)
+        out, w1, w2 = ttt(query, key, target, spread, w1, w2, half)
+        outs.append(out)
+    result = jnp.concatenate(outs, axis=0).reshape(videos, seg_len, channels)
+    return lax.all_to_all(result, "seg", split_axis=0, concat_axis=0, tiled=True)
+
+
+def body(attn_query, attn_key, attn_value, prompt_len, ttt_weight, init_w1, init_w2t, step_rate):
+    videos, seg_len, channels = attn_query.shape
+    heads, half, hidden = init_w1.shape
+    whole_pairs = heads % 2 == 0 and 2 * half == 128 and hidden % 128 == 0
+    fits = seg_len % 128 == 0 and heads <= 128
+    run = by_video if videos == lax.axis_size("seg") and whole_pairs and fits else any_size
+    return run(attn_query, attn_key, attn_value, prompt_len, ttt_weight, init_w1, init_w2t, step_rate)
+
+
 def solution(mesh):
     return jax.shard_map(
         body,

time: 681 us -> 310 us (0.46)
  local copies, waits for them, and re-layouts: 210 us -> 5.84 us
  matrix products: 164 us -> 0 us
  Pallas kernels: 0 us -> 155 us
  other arithmetic: 106 us -> 6.96 us
  waiting for transfers between devices: 145 us -> 56.4 us
  blocking collectives: 23.4 us -> 52.4 us
  starting transfers between devices: 10.1 us -> 32.1 us
  between operations: 13.6 us -> 0.15 us
    dot_general x114 -> x0, matrix products: 157 us -> none  [the longest x64 85.6 us: fast_mlp(): jnp.einsum('bmf,bdf->bmd', hidden, fast_weights[:, 1], precision=highest_...]
    pallas_call x0 -> x9, Pallas kernels: none -> 155 us  [the longest x4 97.1 us: ttt(): pl.pallas_call(functools.partial(ttt_kernel, half=half), out_shape=[jax.S...]
    dynamic_slice x112 -> x0, local copies, waits for them, and re-layouts: 132 us -> none  [run_items(): lax.scan(minibatch, fast_weights, (to_blocks(picked[:, 0]), to_blocks(pic...]
    all_gather x1 -> x0, waiting for transfers between devices: 92.2 us -> none  [body(): features = lax.all_gather(attended, 'head', axis=2, tiled=True)]
    reduce_sum x65 -> x1, other arithmetic: 57.7 us -> 0.07 us  [by_video(): w2 = init_w2t - jnp.mean(init_w2t, axis=1, keepdims=True)]
    ppermute x0 -> x16, waiting for transfers between devices: none -> 56.4 us  [the longest x4 56.4 us: gather_heads(): far = lax.ppermute(block, 'head', [(0, 2), (2, 0), (1, 3), (3, 1)])]
    all_to_all x2 -> x0, waiting for transfers between devices: 52.4 us -> none  [the longest x1 52.4 us: body(): lax.all_to_all(item_inputs.astype(jnp.bfloat16), 'seg', split_axis=0, con...]
    ppermute x0 -> x16, starting transfers between devices: none -> 32.1 us  [the longest x4 18.5 us: gather_heads(): near = lax.ppermute(block, 'head', [(0, 1), (1, 0), (2, 3), (3, 2)])]
  transfers between devices with their start and end apart: 3 -> 16, of which waited for: 2 -> 3; matrix products, arithmetic and copies ran while one was open for 7% -> 2% of each run, Pallas kernels for 0% -> 35%
where the time goes in v1:
time: 310 us; the launch traced here: 309 us
  Pallas kernels  155 us (50%)
  waiting for transfers between devices  56.4 us (18%)
  blocking collectives  52.4 us (17%)
  starting transfers between devices  32.1 us (10%)
  other arithmetic  6.96 us (2%)
  local copies, waits for them, and re-layouts  5.84 us (2%)
    pallas_call x4, Pallas kernels, ttt(): pl.pallas_call(functools.partial(ttt_kernel, half=half), out_shape=[jax.S...  97.1 us
    ppermute x4, waiting for transfers between devices, gather_heads(): far = lax.ppermute(block, 'head', [(0, 2), (2, 0), (1, 3), (3, 1)])  56.4 us
    pallas_call x4, Pallas kernels, project(): pl.pallas_call(functools.partial(project_kernel, shards=len(shards), half...  49.2 us
    all_to_all x1, blocking collectives, by_video(): mine = lax.all_to_all(mixed, 'seg', split_axis=0, concat_axis=0, tiled=True)  29 us
    all_to_all x1, blocking collectives, by_video(): lax.all_to_all(result, 'seg', split_axis=0, concat_axis=0, tiled=True)  23.4 us
    ppermute x4, starting transfers between devices, gather_heads(): near = lax.ppermute(block, 'head', [(0, 1), (1, 0), (2, 3), (3, 2)])  18.5 us
    pallas_call x1, Pallas kernels, attention(): pl.pallas_call(functools.partial(attention_kernel, half=half), grid_spec=...  9.01 us
  transfers between devices with their start and end apart: 16, of which 3 were waited for; matrix products, arithmetic and copies ran while one was open for 2% of the time, Pallas kernels for 35%

profile of v1, /device:TPU:0, one launch (start us, length us, event | category | flops | bytes accessed | tf_op | source)
XLA Modules:
  0.0 309.1 jit_solution(11166425650280537899)
XLA Ops:
  0.0 1.4 copy.9.rate_ref
  1.4 9.0 %attention.1 = bf16[8,128,896]{2,1,0:T(8,128)(2,1)} custom-call(s32[8]{0:T(128)} %bitcast.6, bf16[8,128,768]{2,1,0:T(8,128)(2,1)} %q_ref.1, bf16[8,128,768]{2,1,0:T(8,128)(2,1)} %k_ref.1, bf16[8,128,768]{2,1,0:T(8,128)(2,1)} %v_ref.1, f32[8,12,128]{2,1,0:T(8,128)} %copy.9.rate_ref), custom_call_target="tpu_custom_call" | custom-call | tf_op jit(solution)/shard_map/attention/pallas_call | solution.py:84
  10.4 29.0 %all_to_all.10 = bf16[8,128,896]{2,1,0:T(8,128)(2,1)S(1)} all-to-all(bf16[8,128,896]{2,1,0:T(8,128)(2,1)} %attention.1), channel_id=1, replica_groups=mesh['seg'=8,'head'=4] {'seg'}, dimensions={0} | all-to-all | bytes 3670016 | tf_op jit(solution)/shard_map/all_to_all | solution.py:393
  39.4 1.0 fusion.1
  40.4 2.6 collective-permute-start.1
  43.0 1.4 collective-permute-start.3
  44.4 0.0 copy-done
  44.4 0.1 reduce_sum.9
  44.5 2.2 collective-permute-start
  46.7 1.5 collective-permute-start.5
  48.2 1.4 collective-permute-start.7
  49.6 28.7 %collective-permute-done.1.refs_2_ = bf16[256,768]{1,0:T(8,128)(2,1)} collective-permute-done((bf16[256,768]{1,0:T(8,128)(2,1)}, bf16[256,768]{1,0:T(8,128)(2,1)}, u32[]{:S(2)}, u32[]{:S(2)}) %collective-permute-start.1) | collective-permute-done | bytes 393248 | tf_op jit(solution)/shard_map/ppermute | solution.py:381
  78.4 0.0 collective-permute-start.9
  78.4 0.0 collective-permute-done.3
  78.4 1.3 collective-permute-start.2
  79.6 1.0 broadcast_subtract_fusion.w2_in
  80.6 0.6 iota_xor_fusion.row_ref
  81.2 0.0 collective-permute-done.refs_1_
  81.2 9.7 %collective-permute-start.4 = (bf16[256,768]{1,0:T(8,128)(2,1)}, bf16[256,768]{1,0:T(8,128)(2,1)S(1)}, u32[]{:S(2)}, u32[]{:S(2)}) collective-permute-start(bf16[256,768]{1,0:T(8,128)(2,1)} %get-tuple-element.64.refs_0_), channel_id=1, source_target_pairs={{0,1},{1,0},{2,3},{3,2},{4,5},{5,4},{6,7},{7,6},{8,9},{9,8},{10,11... | collective-permute-start | bytes 1179656 | tf_op jit(solution)/shard_map/ppermute | solution.py:380
  91.0 4.3 %collective-permute-done.5.refs_2_ = bf16[256,768]{1,0:T(8,128)(2,1)} collective-permute-done((bf16[256,768]{1,0:T(8,128)(2,1)}, bf16[256,768]{1,0:T(8,128)(2,1)}, u32[]{:S(2)}, u32[]{:S(2)}) %collective-permute-start.5) | collective-permute-done | bytes 393248 | tf_op jit(solution)/shard_map/ppermute | solution.py:381
  95.2 0.0 collective-permute-start.13
  95.3 0.0 collective-permute-done.7
  95.3 1.3 collective-permute-start.6
  96.5 0.7 fusion
  97.3 23.4 %collective-permute-done.9.refs_2_ = bf16[256,768]{1,0:T(8,128)(2,1)} collective-permute-done((bf16[256,768]{1,0:T(8,128)(2,1)S(1)}, bf16[256,768]{1,0:T(8,128)(2,1)}, u32[]{:S(2)}, u32[]{:S(2)}) %collective-permute-start.9) | collective-permute-done | bytes 393248 | tf_op jit(solution)/shard_map/ppermute | solution.py:381
  120.6 0.7 collective-permute-start.11
  121.3 0.0 collective-permute-done.2
  121.3 1.3 collective-permute-start.10
  122.6 1.8 broadcast_select_fusion.3.refs_3_
  124.4 12.3 %project.4 = (f32[256,768]{1,0:T(8,128)}, bf16[256,768]{1,0:T(8,128)(2,1)}, f32[256,768]{1,0:T(8,128)}, f32[256,768]{1,0:T(8,128)}) custom-call(s32[4]{0:T(128)} %iota_xor_fusion.row_ref, bf16[256,768]{1,0:T(8,128)(2,1)} %get-tuple-element.61.refs_0_, bf16[256,768]{1,0:T(8,128)(2,1)} %collective-permute-done.refs_1_, ...), custom_call_target="tpu_custom_call" | custom-call | tf_op jit(solution)/shard_map/project/pallas_call | solution.py:148
  136.7 24.2 %fast_weights.4 = (bf16[256,768]{1,0:T(8,128)(2,1)}, f32[12,64,256]{2,1,0:T(8,128)}, f32[12,64,256]{2,1,0:T(8,128)}) custom-call(f32[256,768]{1,0:T(8,128)} %get-tuple-element.31.q_ref, bf16[256,768]{1,0:T(8,128)(2,1)} %get-tuple-element.32.k_ref, f32[256,768]{1,0:T(8,128)} %get-tuple-element.33.t_ref, f32[256,768]{1,0:T(8,128)} %get-tuple-element.34.e_ref, ...), custom_call_target="tpu_custom_call" | custom-call | tf_op jit(solution)/shard_map/fast_weights/pallas_call | solution.py:253
  160.9 0.0 collective-permute-done.4.refs_1_
  160.9 0.0 copy-done.2
  160.9 0.0 copy-start.7
  161.0 2.7 collective-permute-start.8
  163.7 0.0 collective-permute-done.13.refs_2_
  163.7 0.7 collective-permute-start.15
  164.4 0.0 collective-permute-done.6
  164.4 1.5 collective-permute-start.14
  165.9 0.8 broadcast_select_fusion.2.refs_3_
  166.7 0.0 copy-done.7
  166.7 12.3 %project.5 = (f32[256,768]{1,0:T(8,128)}, bf16[256,768]{1,0:T(8,128)(2,1)}, f32[256,768]{1,0:T(8,128)}, f32[256,768]{1,0:T(8,128)}) custom-call(s32[4]{0:T(128)} %iota_xor_fusion.row_ref, bf16[256,768]{1,0:T(8,128)(2,1)} %get-tuple-element.64.refs_0_, bf16[256,768]{1,0:T(8,128)(2,1)} %copy-done.7, bf16[256,768]{1,0:T(8,128)(2,1)} %collective-permute-done.5.refs_2_, ...), custom_call_target="tpu_custom_call" | custom-call | tf_op jit(solution)/shard_map/project/pallas_call | solution.py:148
  179.0 0.0 copy-done.6
  179.0 24.2 %fast_weights.5 = (bf16[256,768]{1,0:T(8,128)(2,1)}, f32[12,64,256]{2,1,0:T(8,128)}, f32[12,64,256]{2,1,0:T(8,128)}) custom-call(f32[256,768]{1,0:T(8,128)} %get-tuple-element.36.q_ref, bf16[256,768]{1,0:T(8,128)(2,1)} %get-tuple-element.37.k_ref, f32[256,768]{1,0:T(8,128)} %get-tuple-element.38.t_ref, f32[256,768]{1,0:T(8,128)} %get-tuple-element.39.e_ref, ...), custom_call_target="tpu_custom_call" | custom-call | tf_op jit(solution)/shard_map/fast_weights/pallas_call | solution.py:253
  203.2 0.0 collective-permute-done.11
  203.2 0.0 copy-done.1
  203.2 3.9 %collective-permute-start.12 = (bf16[256,768]{1,0:T(8,128)(2,1)S(1)}, bf16[256,768]{1,0:T(8,128)(2,1)S(1)}, u32[]{:S(2)}, u32[]{:S(2)}) collective-permute-start(bf16[256,768]{1,0:T(8,128)(2,1)S(1)} %get-tuple-element.62.refs_0_), channel_id=1, source_target_pairs={{0,1},{1,0},{2,3},{3,2},{4,5},{5,4},{6,7},{7,6},{8,9},{9,8},{10,11... | collective-permute-start | bytes 1179656 | tf_op jit(solution)/shard_map/ppermute | solution.py:380
  207.0 0.0 collective-permute-done.10
  207.0 0.8 broadcast_select_fusion.1.refs_3_
  207.8 0.0 collective-permute-done.8.refs_1_
  207.8 0.7 copy-done.8
  208.6 12.3 %project.6 = (f32[256,768]{1,0:T(8,128)}, bf16[256,768]{1,0:T(8,128)(2,1)}, f32[256,768]{1,0:T(8,128)}, f32[256,768]{1,0:T(8,128)}) custom-call(s32[4]{0:T(128)} %iota_xor_fusion.row_ref, bf16[256,768]{1,0:T(8,128)(2,1)} %copy-done.2, bf16[256,768]{1,0:T(8,128)(2,1)} %copy-done.8, bf16[256,768]{1,0:T(8,128)(2,1)} %collective-permute-done.9.refs_2_, ...), custom_call_target="tpu_custom_call" | custom-call | tf_op jit(solution)/shard_map/project/pallas_call | solution.py:148
  220.9 24.4 %fast_weights.6 = (bf16[256,768]{1,0:T(8,128)(2,1)}, f32[12,64,256]{2,1,0:T(8,128)}, f32[12,64,256]{2,1,0:T(8,128)}) custom-call(f32[256,768]{1,0:T(8,128)} %get-tuple-element.43.q_ref, bf16[256,768]{1,0:T(8,128)(2,1)} %get-tuple-element.44.k_ref, f32[256,768]{1,0:T(8,128)} %get-tuple-element.45.t_ref, f32[256,768]{1,0:T(8,128)} %get-tuple-element.46.e_ref, ...), custom_call_target="tpu_custom_call" | custom-call | tf_op jit(solution)/shard_map/fast_weights/pallas_call | solution.py:253
  245.3 0.0 collective-permute-done.15
  245.3 0.0 collective-permute-done.14
  245.3 0.8 broadcast_select_fusion.refs_3_
  246.1 0.0 collective-permute-done.12.refs_1_
  246.1 0.7 copy-done.9
  246.8 12.3 %project.7 = (f32[256,768]{1,0:T(8,128)}, bf16[256,768]{1,0:T(8,128)(2,1)}, f32[256,768]{1,0:T(8,128)}, f32[256,768]{1,0:T(8,128)}) custom-call(s32[4]{0:T(128)} %iota_xor_fusion.row_ref, bf16[256,768]{1,0:T(8,128)(2,1)} %copy-done.1, bf16[256,768]{1,0:T(8,128)(2,1)} %copy-done.9, bf16[256,768]{1,0:T(8,128)(2,1)} %copy-done.6, ...), custom_call_target="tpu_custom_call" | custom-call | tf_op jit(solution)/shard_map/project/pallas_call | solution.py:148
  259.1 0.0 copy-start.4
  259.1 24.3 %fast_weights.7 = (bf16[256,768]{1,0:T(8,128)(2,1)}, f32[12,64,256]{2,1,0:T(8,128)}, f32[12,64,256]{2,1,0:T(8,128)}) custom-call(f32[256,768]{1,0:T(8,128)} %get-tuple-element.50.q_ref, bf16[256,768]{1,0:T(8,128)(2,1)} %get-tuple-element.51.k_ref, f32[256,768]{1,0:T(8,128)} %get-tuple-element.52.t_ref, f32[256,768]{1,0:T(8,128)} %get-tuple-element.53.e_ref, ...), custom_call_target="tpu_custom_call" | custom-call | tf_op jit(solution)/shard_map/fast_weights/pallas_call | solution.py:253
  283.4 1.1 pad_maximum_fusion
  284.5 23.4 %all_to_all.11 = bf16[8,128,768]{2,1,0:T(8,128)(2,1)S(1)} all-to-all(bf16[8,128,768]{2,1,0:T(8,128)(2,1)S(1)} %bitcast.5), channel_id=1, replica_groups=mesh['seg'=8,'head'=4] {'seg'}, dimensions={0} | all-to-all | bytes 3145728 | tf_op jit(solution)/shard_map/all_to_all | solution.py:408
  308.0 1.1 copy.11
  (12 shorter events, 0.0 us)
Async XLA Ops:
  39.4 5.0 %copy-start = (f32[12,64,256]{2,1,0:T(8,128)S(1)}, f32[12,64,256]{2,1,0:T(8,128)}, u32[]{:S(2)}) copy-start(f32[12,64,256]{2,1,0:T(8,128)} %param.14) | copy-start | bytes 2359300
  40.4 120.5 %copy-start.2 = (bf16[256,768]{1,0:T(8,128)(2,1)}, bf16[256,768]{1,0:T(8,128)(2,1)S(1)}, u32[]{:S(2)}) copy-start(bf16[256,768]{1,0:T(8,128)(2,1)S(1)} %get-tuple-element.63.refs_0_) | copy-start | bytes 1179652
  40.4 162.7 %copy-start.1 = (bf16[256,768]{1,0:T(8,128)(2,1)}, bf16[256,768]{1,0:T(8,128)(2,1)S(1)}, u32[]{:S(2)}) copy-start(bf16[256,768]{1,0:T(8,128)(2,1)S(1)} %get-tuple-element.62.refs_0_) | copy-start | bytes 1179652
  40.4 37.9 %collective-permute-start.1 = (bf16[256,768]{1,0:T(8,128)(2,1)}, bf16[256,768]{1,0:T(8,128)(2,1)}, u32[]{:S(2)}, u32[]{:S(2)}) collective-permute-start(bf16[256,768]{1,0:T(8,128)(2,1)} %get-tuple-element.61.refs_0_), channel_id=1, source_target_pairs={{0,2},{2,0},{1,3},{3,1},{4,6},{6,4},{5,7},{7,5},{8,10},{10,8},{9,1... | collective-permute-start | bytes 1179656 | tf_op jit(solution)/shard_map/ppermute | solution.py:381
  43.0 35.3 %collective-permute-start.3 = (bf16[256,768]{1,0:T(8,128)(2,1)}, bf16[256,768]{1,0:T(8,128)(2,1)}, u32[]{:S(2)}, u32[]{:S(2)}) collective-permute-start(bf16[256,768]{1,0:T(8,128)(2,1)} %get-tuple-element.61.refs_0_), channel_id=1, source_target_pairs={{1,2},{2,1},{5,6},{6,5},{9,10},{10,9},{13,14},{14,13},{17,18},{18,... | collective-permute-start | bytes 1179656 | tf_op jit(solution)/shard_map/ppermute | solution.py:382
  44.5 36.7 %collective-permute-start = (bf16[256,768]{1,0:T(8,128)(2,1)}, bf16[256,768]{1,0:T(8,128)(2,1)}, u32[]{:S(2)}, u32[]{:S(2)}) collective-permute-start(bf16[256,768]{1,0:T(8,128)(2,1)} %get-tuple-element.61.refs_0_), channel_id=1, source_target_pairs={{0,1},{1,0},{2,3},{3,2},{4,5},{5,4},{6,7},{7,6},{8,9},{9,8},{10,11... | collective-permute-start | bytes 1179656 | tf_op jit(solution)/shard_map/ppermute | solution.py:380
  46.7 48.6 %collective-permute-start.5 = (bf16[256,768]{1,0:T(8,128)(2,1)}, bf16[256,768]{1,0:T(8,128)(2,1)}, u32[]{:S(2)}, u32[]{:S(2)}) collective-permute-start(bf16[256,768]{1,0:T(8,128)(2,1)} %get-tuple-element.64.refs_0_), channel_id=1, source_target_pairs={{0,2},{2,0},{1,3},{3,1},{4,6},{6,4},{5,7},{7,5},{8,10},{10,8},{9,1... | collective-permute-start | bytes 1179656 | tf_op jit(solution)/shard_map/ppermute | solution.py:381
  48.2 47.1 %collective-permute-start.7 = (bf16[256,768]{1,0:T(8,128)(2,1)}, bf16[256,768]{1,0:T(8,128)(2,1)}, u32[]{:S(2)}, u32[]{:S(2)}) collective-permute-start(bf16[256,768]{1,0:T(8,128)(2,1)} %get-tuple-element.64.refs_0_), channel_id=1, source_target_pairs={{1,2},{2,1},{5,6},{6,5},{9,10},{10,9},{13,14},{14,13},{17,18},{18,... | collective-permute-start | bytes 1179656 | tf_op jit(solution)/shard_map/ppermute | solution.py:382
  78.4 42.3 %collective-permute-start.9 = (bf16[256,768]{1,0:T(8,128)(2,1)S(1)}, bf16[256,768]{1,0:T(8,128)(2,1)}, u32[]{:S(2)}, u32[]{:S(2)}) collective-permute-start(bf16[256,768]{1,0:T(8,128)(2,1)S(1)} %get-tuple-element.63.refs_0_), channel_id=1, source_target_pairs={{0,2},{2,0},{1,3},{3,1},{4,6},{6,4},{5,7},{7,5},{8,10},{10,8},{9,1... | collective-permute-start | bytes 1179656 | tf_op jit(solution)/shard_map/ppermute | solution.py:381
  78.4 43.0 %collective-permute-start.2 = (bf16[256,768]{1,0:T(8,128)(2,1)}, bf16[256,768]{1,0:T(8,128)(2,1)}, u32[]{:S(2)}, u32[]{:S(2)}) collective-permute-start(bf16[256,768]{1,0:T(8,128)(2,1)} %collective-permute-done.1.refs_2_), channel_id=1, source_target_pairs={{2,3},{1,0},{6,7},{5,4},{10,11},{9,8},{14,15},{13,12},{18,19},{17,... | collective-permute-start | bytes 1179656 | tf_op jit(solution)/shard_map/ppermute | solution.py:383
  81.2 79.7 %collective-permute-start.4 = (bf16[256,768]{1,0:T(8,128)(2,1)}, bf16[256,768]{1,0:T(8,128)(2,1)S(1)}, u32[]{:S(2)}, u32[]{:S(2)}) collective-permute-start(bf16[256,768]{1,0:T(8,128)(2,1)} %get-tuple-element.64.refs_0_), channel_id=1, source_target_pairs={{0,1},{1,0},{2,3},{3,2},{4,5},{5,4},{6,7},{7,6},{8,9},{9,8},{10,11... | collective-permute-start | bytes 1179656 | tf_op jit(solution)/shard_map/ppermute | solution.py:380
  95.2 68.4 %collective-permute-start.13 = (bf16[256,768]{1,0:T(8,128)(2,1)S(1)}, bf16[256,768]{1,0:T(8,128)(2,1)S(1)}, u32[]{:S(2)}, u32[]{:S(2)}) collective-permute-start(bf16[256,768]{1,0:T(8,128)(2,1)S(1)} %get-tuple-element.62.refs_0_), channel_id=1, source_target_pairs={{0,2},{2,0},{1,3},{3,1},{4,6},{6,4},{5,7},{7,5},{8,10},{10,8},{9,1... | collective-permute-start | bytes 1179656 | tf_op jit(solution)/shard_map/ppermute | solution.py:381
  95.3 69.1 %collective-permute-start.6 = (bf16[256,768]{1,0:T(8,128)(2,1)}, bf16[256,768]{1,0:T(8,128)(2,1)S(1)}, u32[]{:S(2)}, u32[]{:S(2)}) collective-permute-start(bf16[256,768]{1,0:T(8,128)(2,1)} %collective-permute-done.5.refs_2_), channel_id=1, source_target_pairs={{2,3},{1,0},{6,7},{5,4},{10,11},{9,8},{14,15},{13,12},{18,19},{17,... | collective-permute-start | bytes 1179656 | tf_op jit(solution)/shard_map/ppermute | solution.py:383
  120.6 82.5 %collective-permute-start.11 = (bf16[256,768]{1,0:T(8,128)(2,1)S(1)}, bf16[256,768]{1,0:T(8,128)(2,1)S(1)}, u32[]{:S(2)}, u32[]{:S(2)}) collective-permute-start(bf16[256,768]{1,0:T(8,128)(2,1)S(1)} %get-tuple-element.63.refs_0_), channel_id=1, source_target_pairs={{1,2},{2,1},{5,6},{6,5},{9,10},{10,9},{13,14},{14,13},{17,18},{18,... | collective-permute-start | bytes 1179656 | tf_op jit(solution)/shard_map/ppermute | solution.py:382
  121.3 85.7 %collective-permute-start.10 = (bf16[256,768]{1,0:T(8,128)(2,1)}, bf16[256,768]{1,0:T(8,128)(2,1)S(1)}, u32[]{:S(2)}, u32[]{:S(2)}) collective-permute-start(bf16[256,768]{1,0:T(8,128)(2,1)} %collective-permute-done.9.refs_2_), channel_id=1, source_target_pairs={{2,3},{1,0},{6,7},{5,4},{10,11},{9,8},{14,15},{13,12},{18,19},{17,... | collective-permute-start | bytes 1179656 | tf_op jit(solution)/shard_map/ppermute | solution.py:383
  160.9 5.7 %copy-start.7 = (bf16[256,768]{1,0:T(8,128)(2,1)}, bf16[256,768]{1,0:T(8,128)(2,1)S(1)}, u32[]{:S(2)}) copy-start(bf16[256,768]{1,0:T(8,128)(2,1)S(1)} %collective-permute-done.4.refs_1_) | copy-start | bytes 1179652
  161.0 46.9 %collective-permute-start.8 = (bf16[256,768]{1,0:T(8,128)(2,1)S(1)}, bf16[256,768]{1,0:T(8,128)(2,1)S(1)}, u32[]{:S(2)}, u32[]{:S(2)}) collective-permute-start(bf16[256,768]{1,0:T(8,128)(2,1)S(1)} %get-tuple-element.63.refs_0_), channel_id=1, source_target_pairs={{0,1},{1,0},{2,3},{3,2},{4,5},{5,4},{6,7},{7,6},{8,9},{9,8},{10,11... | collective-permute-start | bytes 1179656 | tf_op jit(solution)/shard_map/ppermute | solution.py:380
  163.7 15.3 %copy-start.6 = (bf16[256,768]{1,0:T(8,128)(2,1)}, bf16[256,768]{1,0:T(8,128)(2,1)S(1)}, u32[]{:S(2)}) copy-start(bf16[256,768]{1,0:T(8,128)(2,1)S(1)} %collective-permute-done.13.refs_2_) | copy-start | bytes 1179652
  163.7 81.6 %collective-permute-start.15 = (bf16[256,768]{1,0:T(8,128)(2,1)S(1)}, bf16[256,768]{1,0:T(8,128)(2,1)S(1)}, u32[]{:S(2)}, u32[]{:S(2)}) collective-permute-start(bf16[256,768]{1,0:T(8,128)(2,1)S(1)} %get-tuple-element.62.refs_0_), channel_id=1, source_target_pairs={{1,2},{2,1},{5,6},{6,5},{9,10},{10,9},{13,14},{14,13},{17,18},{18,... | collective-permute-start | bytes 1179656 | tf_op jit(solution)/shard_map/ppermute | solution.py:382
  164.4 80.9 %collective-permute-start.14 = (bf16[256,768]{1,0:T(8,128)(2,1)S(1)}, bf16[256,768]{1,0:T(8,128)(2,1)S(1)}, u32[]{:S(2)}, u32[]{:S(2)}) collective-permute-start(bf16[256,768]{1,0:T(8,128)(2,1)S(1)} %collective-permute-done.13.refs_2_), channel_id=1, source_target_pairs={{2,3},{1,0},{6,7},{5,4},{10,11},{9,8},{14,15},{13,12},{18,19},{17,... | collective-permute-start | bytes 1179656 | tf_op jit(solution)/shard_map/ppermute | solution.py:383
  203.2 42.9 %collective-permute-start.12 = (bf16[256,768]{1,0:T(8,128)(2,1)S(1)}, bf16[256,768]{1,0:T(8,128)(2,1)S(1)}, u32[]{:S(2)}, u32[]{:S(2)}) collective-permute-start(bf16[256,768]{1,0:T(8,128)(2,1)S(1)} %get-tuple-element.62.refs_0_), channel_id=1, source_target_pairs={{0,1},{1,0},{2,3},{3,2},{4,5},{5,4},{6,7},{7,6},{8,9},{9,8},{10,11... | collective-permute-start | bytes 1179656 | tf_op jit(solution)/shard_map/ppermute | solution.py:380
  207.8 0.7 copy-start.8
  246.1 0.7 copy-start.9
  259.1 24.3 %copy-start.3 = (bf16[256,768]{1,0:T(8,128)(2,1)S(1)}, bf16[256,768]{1,0:T(8,128)(2,1)}, u32[]{:S(2)}) copy-start(bf16[256,768]{1,0:T(8,128)(2,1)} %get-tuple-element.35) | copy-start | bytes 1179652
  259.1 24.3 %copy-start.4 = (bf16[256,768]{1,0:T(8,128)(2,1)S(1)}, bf16[256,768]{1,0:T(8,128)(2,1)}, u32[]{:S(2)}) copy-start(bf16[256,768]{1,0:T(8,128)(2,1)} %get-tuple-element.42) | copy-start | bytes 1179652
  259.1 24.3 %copy-start.5 = (bf16[256,768]{1,0:T(8,128)(2,1)S(1)}, bf16[256,768]{1,0:T(8,128)(2,1)}, u32[]{:S(2)}) copy-start(bf16[256,768]{1,0:T(8,128)(2,1)} %get-tuple-element.49) | copy-start | bytes 1179652

commit v2 on v0

--- a/solution.py
+++ b/solution.py
@@ -1,15 +1,266 @@
+import functools
 import jax
 import jax.numpy as jnp
 from jax import lax
+from jax.experimental import pallas as pl
+from jax.experimental.pallas import tpu as pltpu
 from jax.sharding import PartitionSpec as P
 
+highest_precision = lax.Precision.HIGHEST
 MINI = 64
 TEXT_SLOTS = 64
-
-
-highest_precision = lax.Precision.HIGHEST
 norm_epsilon = 1e-05
 rms_epsilon = 1e-06
+GROUP = 6
+PB = 3
+CHUNK_VMEM = 26 * 1024 * 1024
+VMEM_LIMIT = 20 * 1024 * 1024
+gelu_a = 0.7978845608028654
+gelu_b = gelu_a * 0.044715
+
+
+def dot_nn(a, b):
+    return lax.dot_general(a, b, (((1,), (0,)), ((), ())), preferred_element_type=jnp.float32)
+
+
+def dot_nt(a, b):
+    return lax.dot_general(a, b, (((1,), (1,)), ((), ())), preferred_element_type=jnp.float32)
+
+
+def low_half(shape, half):
+    return lax.broadcasted_iota(jnp.int32, shape, len(shape) - 1) < half
+
+
+def half_ones(half):
+    width = 2 * half
+    row = lax.broadcasted_iota(jnp.int32, (width, width), 0) < half
+    column = lax.broadcasted_iota(jnp.int32, (width, width), 1) < half
+    return (row == column).astype(jnp.bfloat16)
+
+
+def attention_kernel(lens_ref, q_ref, k_ref, v_ref, rate_ref, out_ref, *, half):
+    video = pl.program_id(0)
+    length = lens_ref[video]
+    seg_len = q_ref.shape[1]
+    channels = q_ref.shape[2]
+    width = 2 * half
+    heads = channels // half
+    key_at = lax.broadcasted_iota(jnp.int32, (seg_len, 2 * seg_len), 1)
+    key_at = jnp.where(key_at >= seg_len, key_at - seg_len, key_at)
+    usable = (key_at >= TEXT_SLOTS) | (key_at < length)
+    low = low_half((seg_len, width), half)
+    zero = jnp.zeros((seg_len, width), jnp.bfloat16)
+    ones = jnp.ones((seg_len, width), jnp.bfloat16)
+    scale = jnp.asarray(half ** (-0.5), jnp.bfloat16)
+    totals = jnp.concatenate([jnp.where(low, ones, zero), jnp.where(low, zero, ones)], axis=0)
+    for pair in range(channels // width):
+        lanes = slice(pair * width, (pair + 1) * width)
+        query = q_ref[0, :, lanes] * scale
+        key = k_ref[0, :, lanes]
+        value = v_ref[0, :, lanes]
+        keys = jnp.concatenate([jnp.where(low, key, zero), jnp.where(low, zero, key)], axis=0)
+        scores = jnp.where(usable, dot_nt(query, keys), -1e30)
+        parts = []
+        for side in range(2):
+            block = scores[:, side * seg_len : (side + 1) * seg_len]
+            largest = jnp.max(block, axis=1, keepdims=True)
+            parts.append(jnp.exp(block - largest).astype(jnp.bfloat16))
+        weights = jnp.concatenate(parts, axis=1)
+        values = jnp.concatenate([jnp.where(low, value, zero), jnp.where(low, zero, value)], axis=0)
+        mixed = dot_nn(weights, jnp.concatenate([values, totals], axis=1))
+        out_ref[0, :, lanes] = (mixed[:, :width] / mixed[:, width:]).astype(jnp.bfloat16)
+    token = lax.broadcasted_iota(jnp.int32, (seg_len, 1), 0)
+    open_token = ((token >= TEXT_SLOTS) | (token < length)).astype(jnp.float32)
+    rates = rate_ref[0]
+    spare = out_ref.shape[2] - channels
+    rates = jnp.concatenate(
+        [rates, jnp.zeros((spare - rates.shape[0], seg_len), jnp.float32)], axis=0
+    )
+    out_ref[0, :, channels:] = (rates.T * open_token).astype(jnp.bfloat16)
+
+
+def attention(attn_query, attn_key, attn_value, lens, step_rate, half):
+    videos, seg_len, channels = attn_query.shape
+    heads = step_rate.shape[1]
+    spare = 128
+    block = pl.BlockSpec((1, seg_len, channels), lambda v, lens: (v, 0, 0))
+    return pl.pallas_call(
+        functools.partial(attention_kernel, half=half),
+        grid_spec=pltpu.PrefetchScalarGridSpec(
+            num_scalar_prefetch=1,
+            grid=(videos,),
+            in_specs=[block, block, block, pl.BlockSpec((1, heads, seg_len), lambda v, lens: (v, 0, 0))],
+            out_specs=pl.BlockSpec((1, seg_len, channels + spare), lambda v, lens: (v, 0, 0)),
+        ),
+        out_shape=jax.ShapeDtypeStruct((videos, seg_len, channels + spare), jnp.bfloat16),
+        compiler_params=pltpu.CompilerParams(vmem_limit_bytes=VMEM_LIMIT),
+        name="attention",
+    )(lens, attn_query, attn_key, attn_value, step_rate)
+
+
+def chunk_kernel(row_ref, *refs, inputs, shards, half, extra):
+    x_refs, refs = refs[:inputs], refs[inputs:]
+    rate_ref, w_ref, w1_in, w2_in = refs[:4]
+    out_ref, w1_out, w2_out = refs[4 + extra : 7 + extra]
+    x_s, q_ref, k_ref, t_ref, e_ref, w1_s, w2_s = refs[7 + extra :]
+    tokens, depth = x_refs[0].shape
+    width = 2 * half
+    steps = tokens // MINI
+    pairs = q_ref.shape[1] // width
+    hidden = w1_in.shape[2]
+    block_ones = half_ones(half)
+
+    w1_out[...] = w1_in[...]
+    w2_out[...] = w2_in[...]
+    for head in range(2 * pairs):
+        here = slice((head % 2) * half, (head % 2) * half + half)
+        other = slice(half - (head % 2) * half, 2 * half - (head % 2) * half)
+        w1_s[head, here, :] = w1_in[head].astype(jnp.bfloat16)
+        w1_s[head, other, :] = jnp.zeros((half, hidden), jnp.bfloat16)
+        w2_s[head, here, :] = w2_in[head].astype(jnp.bfloat16)
+        w2_s[head, other, :] = jnp.zeros((half, hidden), jnp.bfloat16)
+
+    squares = jnp.zeros((tokens, 128), jnp.float32)
+    for i in range(shards):
+        start = row_ref[i] * depth
+        for at in range(0, depth, 128):
+            piece = x_refs[i][:, at : at + 128]
+            if i == shards - 1 and inputs > shards:
+                piece = piece + x_refs[shards][:, at : at + 128]
+            x_s[:, pl.ds(pl.multiple_of(start + at, 128), 128)] = piece
+            wide = piece.astype(jnp.float32)
+            squares = squares + wide * wide
+    mean = jnp.sum(squares, axis=1, keepdims=True) / (shards * depth)
+    inv = jnp.broadcast_to(lax.rsqrt(mean + rms_epsilon), (tokens, width))
+
+    low = low_half((tokens, width), half)
+    zero = jnp.zeros((tokens, width), jnp.float32)
+    block = PB if pairs % PB == 0 else 1
+    for group in range(0, pairs, block):
+        wide = 3 * width * block
+        acc = dot_nn(x_s[...], w_ref[:, group * 3 * width : group * 3 * width + wide])
+        for at in range(block):
+            first, middle, last = (
+                acc[:, (3 * at + j) * width : (3 * at + j + 1) * width] * inv for j in range(3)
+            )
+            query = jnp.where(low, first, middle)
+            key = pltpu.roll(jnp.where(low, last, first), half, 1)
+            target = jnp.where(low, middle, last) - key
+            total_low = jnp.sum(jnp.where(low, target, zero), axis=1, keepdims=True)
+            total_high = jnp.sum(jnp.where(low, zero, target), axis=1, keepdims=True)
+            target = target - jnp.where(low, total_low, total_high) * (1.0 / half)
+            lanes = slice((group + at) * width, (group + at + 1) * width)
+            q_ref[:, lanes] = query
+            k_ref[:, lanes] = key.astype(jnp.bfloat16)
+            t_ref[:, lanes] = target
+    head = lax.broadcasted_iota(jnp.int32, (rate_ref.shape[1], pairs * width), 0)
+    lane = lax.broadcasted_iota(jnp.int32, (rate_ref.shape[1], pairs * width), 1)
+    spread_to = (lane // half == head).astype(jnp.bfloat16)
+    e_ref[...] = dot_nn(rate_ref[...], spread_to) * (1.0 / MINI)
+
+    def rows_of(step):
+        return pl.ds(pl.multiple_of(step * MINI, MINI), MINI)
+
+    def gelu_parts(value):
+        square = value * value
+        return square, jnp.tanh(value * (gelu_b * square + gelu_a))
+
+    def one(step, with_query, with_key):
+        for first in range(0, pairs, GROUP):
+            group = range(first, min(first + GROUP, pairs))
+            sides = [(pair, side) for pair in group for side in range(2)]
+            lanes = {pair: slice(pair * width, (pair + 1) * width) for pair in group}
+            batch, value, doubled, slope, total, inverse, unit, change = ({} for _ in range(8))
+            for pair in group:
+                parts = []
+                if with_query:
+                    parts.append(q_ref[rows_of(step - 1), lanes[pair]].astype(jnp.bfloat16))
+                if with_key:
+                    parts.append(k_ref[rows_of(step), lanes[pair]])
+                batch[pair] = jnp.concatenate(parts, axis=0) if len(parts) > 1 else parts[0]
+            for pair, side in sides:
+                value[pair, side] = dot_nn(batch[pair], w1_s[2 * pair + side])
+            for at in sides:
+                v = value[at]
+                square, bent = gelu_parts(v)
+                doubled[at] = (v + v * bent).astype(jnp.bfloat16)
+                if with_key:
+                    v, s, b = v[-MINI:], square[-MINI:], bent[-MINI:]
+                    slope[at] = (1.0 + b) + v * (1.0 - b * b) * (3.0 * gelu_b * s + gelu_a)
+            for pair in group:
+                total[pair] = dot_nt(doubled[pair, 0], w2_s[2 * pair]) + dot_nt(
+                    doubled[pair, 1], w2_s[2 * pair + 1]
+                )
+            count = batch[group[0]].shape[0]
+            squares = jnp.concatenate([(total[pair] * total[pair]).astype(jnp.bfloat16) for pair in group], axis=0)
+            spread = dot_nn(squares, block_ones)
+            for at, pair in enumerate(group):
+                part = spread[at * count : (at + 1) * count]
+                inverse[pair] = lax.rsqrt(part * (1.0 / half) + 4.0 * norm_epsilon)
+                unit[pair] = total[pair] * inverse[pair]
+            if with_query:
+                for pair in group:
+                    query = q_ref[rows_of(step - 1), lanes[pair]]
+                    out_ref[rows_of(step - 1), lanes[pair]] = (query + unit[pair][:MINI]).astype(jnp.bfloat16)
+            if not with_key:
+                continue
+            rows = rows_of(step)
+            grads = {}
+            for pair in group:
+                grads[pair] = e_ref[rows, lanes[pair]] * (unit[pair][-MINI:] - t_ref[rows, lanes[pair]])
+            products = [(grads[pair] * unit[pair][-MINI:]).astype(jnp.bfloat16) for pair in group]
+            along = dot_nn(jnp.concatenate(products, axis=0), block_ones) * (1.0 / half)
+            for at, pair in enumerate(group):
+                part = along[at * MINI : (at + 1) * MINI]
+                change[pair] = (
+                    inverse[pair][-MINI:] * (grads[pair] - unit[pair][-MINI:] * part)
+                ).astype(jnp.bfloat16)
+            back = {}
+            for pair, side in sides:
+                back[pair, side] = (dot_nn(change[pair], w2_s[2 * pair + side]) * slope[pair, side]).astype(jnp.bfloat16)
+            for pair, side in sides:
+                head = 2 * pair + side
+                here = slice(side * half, side * half + half)
+                w2 = w2_out[head] - dot_nn(change[pair].T[here], doubled[pair, side][-MINI:])
+                w2_out[head] = w2
+                w2_s[head, here, :] = w2.astype(jnp.bfloat16)
+                w1 = w1_out[head] - dot_nn(k_ref[rows, lanes[pair]].T[here], back[pair, side])
+                w1_out[head] = w1
+                w1_s[head, here, :] = w1.astype(jnp.bfloat16)
+
+    one(0, False, True)
+    lax.fori_loop(1, steps, lambda step, carry: (one(step, True, True), carry)[1], 0)
+    one(steps, True, False)
+
+
+def run_chunk(shards, rates, weight, row_blocks, w1, w2, half, after=()):
+    shards = [shard for shard in shards if shard is not None]
+    tokens, depth = shards[0].shape
+    heads, _, hidden = w1.shape
+    inputs = len(shards)
+    count = weight.shape[0] // depth
+    state = jax.ShapeDtypeStruct(w1.shape, jnp.float32)
+    inside = pl.BlockSpec(memory_space=pltpu.VMEM)
+    wide = pltpu.VMEM((tokens, heads * half), jnp.float32)
+    return pl.pallas_call(
+        functools.partial(chunk_kernel, inputs=inputs, shards=count, half=half, extra=len(after)),
+        in_specs=[pl.BlockSpec(memory_space=pltpu.SMEM)]
+        + [inside] * (inputs + 4)
+        + [pl.BlockSpec(memory_space=pl.ANY)] * len(after),
+        out_specs=[inside] * 3,
+        out_shape=[jax.ShapeDtypeStruct((tokens, heads * half), jnp.bfloat16), state, state],
+        scratch_shapes=[
+            pltpu.VMEM((tokens, count * depth), jnp.bfloat16),
+            wide,
+            pltpu.VMEM((tokens, heads * half), jnp.bfloat16),
+            wide,
+            wide,
+            pltpu.VMEM((heads, 2 * half, hidden), jnp.bfloat16),
+            pltpu.VMEM((heads, 2 * half, hidden), jnp.bfloat16),
+        ],
+        compiler_params=pltpu.CompilerParams(vmem_limit_bytes=CHUNK_VMEM),
+        name="fast_weights",
+    )(row_blocks, *shards, rates, weight, w1, w2, *after)
 
 
 def normalize(values):
@@ -59,7 +310,7 @@
     return (fast_weights, outputs.transpose(1, 0, 2, 3).reshape(batch, seg_len, head_dim))
 
 
-def body(attn_query, attn_key, attn_value, prompt_len, ttt_weight, init_w1, init_w2t, step_rate):
+def any_size(attn_query, attn_key, attn_value, prompt_len, ttt_weight, init_w1, init_w2t, step_rate):
     videos = attn_query.shape[0]
     seg_len = attn_query.shape[1]
     heads_dev = init_w1.shape[0]
@@ -124,6 +375,104 @@
     return results.astype(jnp.bfloat16)
 
 
+def take_kernel(*refs, at):
+    out = refs[-1]
+    out[...] = refs[0][at : at + out.shape[0], : out.shape[1]]
+
+
+def take(source, at, rows, columns, after):
+    return pl.pallas_call(
+        functools.partial(take_kernel, at=at),
+        in_specs=[pl.BlockSpec(memory_space=pltpu.VMEM)]
+        + [pl.BlockSpec(memory_space=pl.ANY)] * len(after),
+        out_specs=pl.BlockSpec(memory_space=pltpu.VMEM),
+        out_shape=jax.ShapeDtypeStruct((rows, columns), source.dtype),
+        compiler_params=pltpu.CompilerParams(vmem_limit_bytes=8 * 1024 * 1024),
+        name="take",
+    )(source, *after)
+
+
+CHUNK_PARTS = (4, 4, 4, 4)
+FAR_GATE = 1
+OUT_GATE = 3
+KG = 1
+DIRECT = ()
+
+
+def chunk_sizes(tokens):
+    if tokens % (16 * MINI):
+        return [tokens]
+    return [part * (tokens // 16) for part in CHUNK_PARTS]
+
+
+NEAR = [(0, 1), (1, 0), (2, 3), (3, 2)]
+FAR = [(0, 2), (2, 0), (1, 3), (3, 1)]
+INNER = [(1, 2), (2, 1)]
+OUTER = [(2, 3), (1, 0)]
+ACROSS = [(0, 3), (3, 0), (1, 2), (2, 1)]
+
+
+def by_video(attn_query, attn_key, attn_value, prompt_len, ttt_weight, init_w1, init_w2t, step_rate):
+    videos, seg_len, channels = attn_query.shape
+    half = init_w1.shape[1]
+    segments = lax.axis_size("seg")
+    mixed = attention(attn_query, attn_key, attn_value, prompt_len[:, 0], step_rate, half)
+    mine = lax.all_to_all(mixed, "seg", split_axis=0, concat_axis=0, tiled=True)
+    mine = mine.reshape(segments * seg_len, mixed.shape[2])
+    rates = mine[:, channels:]
+    w1 = init_w1
+    w2 = init_w2t - jnp.mean(init_w2t, axis=1, keepdims=True)
+    tokens = segments * seg_len
+    chunk = tokens // 4
+    count = lax.axis_size("head")
+    me = lax.axis_index("head")
+    row_blocks = me ^ jnp.arange(4, dtype=jnp.int32)
+    sizes = chunk_sizes(tokens)
+    ends = [sum(sizes[: c + 1]) for c in range(len(sizes))]
+    blocks, pieces, outs = [], [], []
+
+    def send(c):
+        at, size = ends[c] - sizes[c], sizes[c]
+        after = []
+        if c >= FAR_GATE:
+            after.append(pieces[c - FAR_GATE][0])
+        if c >= OUT_GATE:
+            after.append(outs[c - OUT_GATE])
+        block = take(mine, at, size, channels, after)
+        far = lax.ppermute(block, "head", FAR)
+        near = lax.ppermute(block, "head", NEAR)
+        if c in DIRECT:
+            pieces.append((far, near, lax.ppermute(block, "head", ACROSS), None))
+        else:
+            inner = lax.ppermute(block, "head", INNER)
+            outer = lax.ppermute(far, "head", OUTER)
+            pieces.append((far, near, inner, outer))
+        blocks.append(block)
+
+    for c in range(min(OUT_GATE, len(sizes))):
+        send(c)
+    for c in range(len(sizes)):
+        far, near, inner, outer = pieces[c]
+        rate = rates[ends[c] - sizes[c] : ends[c]]
+        after = [blocks[c + KG]] if c + KG < len(blocks) else []
+        shards = [blocks[c], near, far, inner, outer]
+        out, w1, w2 = run_chunk(shards, rate, ttt_weight, row_blocks, w1, w2, half, after)
+        outs.append(out)
+        if c + OUT_GATE < len(sizes):
+            send(c + OUT_GATE)
+    result = jnp.concatenate(outs, axis=0).reshape(videos, seg_len, channels)
+    return lax.all_to_all(result, "seg", split_axis=0, concat_axis=0, tiled=True)
+
+
+def body(attn_query, attn_key, attn_value, prompt_len, ttt_weight, init_w1, init_w2t, step_rate):
+    videos, seg_len, channels = attn_query.shape
+    heads, half, hidden = init_w1.shape
+    whole_pairs = heads % 2 == 0 and 2 * half == 128 and hidden % 128 == 0
+    fits = seg_len % 128 == 0 and heads <= 128
+    run = by_video if videos == lax.axis_size("seg") and whole_pairs and fits and lax.axis_size("head") == 4 else any_size
+    return run(attn_query, attn_key, attn_value, prompt_len, ttt_weight, init_w1, init_w2t, step_rate)
+
+
 def solution(mesh):
     return jax.shard_map(
         body,

time: 681 us -> 205 us (0.30)
  local copies, waits for them, and re-layouts: 210 us -> 13.7 us
  matrix products: 164 us -> 0 us
  other arithmetic: 106 us -> 2.54 us
  waiting for transfers between devices: 145 us -> 47.9 us
  Pallas kernels: 0 us -> 57.2 us
  blocking collectives: 23.4 us -> 52.3 us
  starting transfers between devices: 10.1 us -> 30.3 us
  between operations: 13.6 us -> 0.29 us
    dot_general x114 -> x0, matrix products: 157 us -> none  [the longest x64 85.6 us: fast_mlp(): jnp.einsum('bmf,bdf->bmd', hidden, fast_weights[:, 1], precision=highest_...]
    dynamic_slice x112 -> x0, local copies, waits for them, and re-layouts: 132 us -> none  [run_items(): lax.scan(minibatch, fast_weights, (to_blocks(picked[:, 0]), to_blocks(pic...]
    all_gather x1 -> x0, waiting for transfers between devices: 92.2 us -> none  [body(): features = lax.all_gather(attended, 'head', axis=2, tiled=True)]
    pallas_call x0 -> x9, Pallas kernels: none -> 57.2 us  [the longest x4 51.3 us: run_chunk(): pl.pallas_call(functools.partial(chunk_kernel, inputs=inputs, shards=coun...]
    reduce_sum x65 -> x1, other arithmetic: 57.7 us -> 1.21 us  [by_video(): w2 = init_w2t - jnp.mean(init_w2t, axis=1, keepdims=True)]
    all_to_all x2 -> x0, waiting for transfers between devices: 52.4 us -> none  [the longest x1 52.4 us: body(): lax.all_to_all(item_inputs.astype(jnp.bfloat16), 'seg', split_axis=0, con...]
    ppermute x0 -> x16, waiting for transfers between devices: none -> 47.9 us  [the longest x4 42.4 us: send(): far = lax.ppermute(block, 'head', FAR)]
    ppermute x0 -> x16, starting transfers between devices: none -> 30.3 us  [the longest x4 14.6 us: send(): far = lax.ppermute(block, 'head', FAR)]
  transfers between devices with their start and end apart: 3 -> 16, of which waited for: 2 -> 4; matrix products, arithmetic and copies ran while one was open for 7% -> 1% of each run, Pallas kernels for 0% -> 19%
where the time goes in v2:
time: 205 us; the launch traced here: 204 us
  Pallas kernels  57.2 us (28%)
  blocking collectives  52.3 us (26%)
  waiting for transfers between devices  47.9 us (23%)
  starting transfers between devices  30.3 us (15%)
  local copies, waits for them, and re-layouts  13.7 us (7%)
  other arithmetic  2.54 us (1%)
    pallas_call x4, Pallas kernels, run_chunk(): pl.pallas_call(functools.partial(chunk_kernel, inputs=inputs, shards=coun...  51.3 us
    ppermute x4, waiting for transfers between devices, send(): far = lax.ppermute(block, 'head', FAR)  42.4 us
    all_to_all x1, blocking collectives, by_video(): mine = lax.all_to_all(mixed, 'seg', split_axis=0, concat_axis=0, tiled=True)  28.8 us
    all_to_all x1, blocking collectives, by_video(): lax.all_to_all(result, 'seg', split_axis=0, concat_axis=0, tiled=True)  23.5 us
    ppermute x4, starting transfers between devices, send(): far = lax.ppermute(block, 'head', FAR)  14.6 us
    unnamed x20, local copies, waits for them, and re-layouts  13.7 us
    ppermute x4, starting transfers between devices, send(): near = lax.ppermute(block, 'head', NEAR)  6.9 us
    ppermute x4, waiting for transfers between devices, send(): outer = lax.ppermute(far, 'head', OUTER)  5.49 us
  transfers between devices with their start and end apart: 16, of which 4 were waited for; matrix products, arithmetic and copies ran while one was open for 1% of the time, Pallas kernels for 19%

profile of v2, /device:TPU:0, one launch (start us, length us, event | category | flops | bytes accessed | tf_op | source)
XLA Modules:
  0.0 204.2 jit_solution(15489778767119972686)
XLA Ops:
  0.0 0.8 copy.9.rate_ref
  0.8 0.0 copy-start.2
  0.8 1.4 copy-done.2
  2.2 0.0 copy-start.3
  2.2 1.4 copy-done.3
  3.6 0.0 copy-start.4
  3.6 1.4 copy-done.4
  5.0 0.0 copy-start.8
  5.0 0.7 copy-done.8
  5.7 5.1 %attention.1 = bf16[8,128,896]{2,1,0:T(8,128)(2,1)S(1)} custom-call(s32[8]{0:T(128)S(1)} %bitcast.8, bf16[8,128,768]{2,1,0:T(8,128)(2,1)S(1)} %copy-done.2, bf16[8,128,768]{2,1,0:T(8,128)(2,1)S(1)} %copy-done.3, bf16[8,128,768]{2,1,0:T(8,128)(2,1)S(1)} %copy-done.4, f32[8,12,128]{2,1,0:T(8,128)S(1)} %copy.9.rate_ref), custom_call_target="tpu_custom_call" | custom-call | tf_op jit(solution)/shard_map/attention/pallas_call | solution.py:87
  10.8 28.8 %all_to_all.10 = bf16[8,128,896]{2,1,0:T(8,128)(2,1)S(1)} all-to-all(bf16[8,128,896]{2,1,0:T(8,128)(2,1)S(1)} %attention.1), channel_id=1, replica_groups=mesh['seg'=8,'head'=4] {'seg'}, dimensions={0} | all-to-all | bytes 3670016 | tf_op jit(solution)/shard_map/all_to_all | solution.py:420
  39.6 0.8 take.4.refs_0_
  40.3 2.6 %collective-permute-start.1 = (bf16[256,768]{1,0:T(8,128)(2,1)}, bf16[256,768]{1,0:T(8,128)(2,1)}, u32[]{:S(2)}, u32[]{:S(2)}) collective-permute-start(bf16[256,768]{1,0:T(8,128)(2,1)} %take.4.refs_0_), channel_id=1, source_target_pairs={{0,2},{2,0},{1,3},{3,1},{4,6},{6,4},{5,7},{7,5},{8,10},{10,8},{9,1... | collective-permute-start | bytes 1179656 | tf_op jit(solution)/shard_map/ppermute | solution.py:442
  42.9 17.3 %collective-permute-done.1.refs_1_.refs_2_ = bf16[256,768]{1,0:T(8,128)(2,1)} collective-permute-done((bf16[256,768]{1,0:T(8,128)(2,1)}, bf16[256,768]{1,0:T(8,128)(2,1)}, u32[]{:S(2)}, u32[]{:S(2)}) %collective-permute-start.1) | collective-permute-done | bytes 393248 | tf_op jit(solution)/shard_map/ppermute | solution.py:442
  60.2 0.1 collective-permute-start.5
  60.3 1.2 reduce_sum.9
  61.5 4.1 %collective-permute-start = (bf16[256,768]{1,0:T(8,128)(2,1)}, bf16[256,768]{1,0:T(8,128)(2,1)}, u32[]{:S(2)}, u32[]{:S(2)}) collective-permute-start(bf16[256,768]{1,0:T(8,128)(2,1)} %take.4.refs_0_), channel_id=1, source_target_pairs={{0,1},{1,0},{2,3},{3,2},{4,5},{5,4},{6,7},{7,6},{8,9},{9,8},{10,11... | collective-permute-start | bytes 1179656 | tf_op jit(solution)/shard_map/ppermute | solution.py:443
  65.6 1.4 collective-permute-start.2
  67.0 1.3 collective-permute-start.3
  68.3 13.4 %collective-permute-done.5.refs_1_.refs_2_ = bf16[256,768]{1,0:T(8,128)(2,1)S(1)} collective-permute-done((bf16[256,768]{1,0:T(8,128)(2,1)S(1)}, bf16[256,768]{1,0:T(8,128)(2,1)S(1)}, u32[]{:S(2)}, u32[]{:S(2)}) %collective-permute-start.5) | collective-permute-done | bytes 393248 | tf_op jit(solution)/shard_map/ppermute | solution.py:442
  81.7 0.0 copy-start.5
  81.7 0.7 copy-done.5
  82.4 0.0 collective-permute-start.9
  82.4 1.2 broadcast_subtract_fusion.refs_8_
  83.7 0.1 collective-permute-start.4
  83.8 0.0 collective-permute-done.refs_1_
  83.8 0.7 collective-permute-start.6
  84.5 0.0 collective-permute-done.2.refs_3_
  84.5 0.7 collective-permute-start.10
  85.2 5.5 %collective-permute-done.3.refs_4_ = bf16[256,768]{1,0:T(8,128)(2,1)} collective-permute-done((bf16[256,768]{1,0:T(8,128)(2,1)}, bf16[256,768]{1,0:T(8,128)(2,1)}, u32[]{:S(2)}, u32[]{:S(2)}) %collective-permute-start.3) | collective-permute-done | bytes 393248 | tf_op jit(solution)/shard_map/ppermute | solution.py:448
  90.7 1.3 collective-permute-start.7
  92.0 0.0 copy-start
  92.0 5.0 %copy-done = bf16[3072,2304]{1,0:T(8,128)(2,1)S(1)} copy-done((bf16[3072,2304]{1,0:T(8,128)(2,1)S(1)}, bf16[3072,2304]{1,0:T(8,128)(2,1)}, u32[]{:S(2)}) %copy-start) | copy-done | bytes 14155800
  97.0 0.0 copy-start.7
  97.0 1.1 copy-done.7
  98.2 0.0 copy-start.1
  98.2 13.3 %fast_weights.4 = (bf16[256,768]{1,0:T(8,128)(2,1)S(1)}, f32[12,64,256]{2,1,0:T(8,128)S(1)}, f32[12,64,256]{2,1,0:T(8,128)S(1)}) custom-call(s32[4]{0:T(128)S(1)} %iota_xor_fusion.row_ref, bf16[256,768]{1,0:T(8,128)(2,1)} %take.4.refs_0_, bf16[256,768]{1,0:T(8,128)(2,1)} %collective-permute-done.refs_1_, ...), custom_call_target="tpu_custom_call" | custom-call | tf_op jit(solution)/shard_map/fast_weights/pallas_call | solution.py:245
  111.5 0.0 copy-start.6
  111.5 0.0 collective-permute-done.9.refs_1_.refs_2_
  111.5 12.0 %collective-permute-start.13 = (bf16[256,768]{1,0:T(8,128)(2,1)S(1)}, bf16[256,768]{1,0:T(8,128)(2,1)S(1)}, u32[]{:S(2)}, u32[]{:S(2)}) collective-permute-start(bf16[256,768]{1,0:T(8,128)(2,1)S(1)} %take.7.refs_9_.refs_0_), channel_id=1, source_target_pairs={{0,2},{2,0},{1,3},{3,1},{4,6},{6,4},{5,7},{7,5},{8,10},{10,8},{9,1... | collective-permute-start | bytes 1179656 | tf_op jit(solution)/shard_map/ppermute | solution.py:442
  123.5 0.0 collective-permute-done.4.refs_1_
  123.5 0.0 collective-permute-start.8
  123.5 0.0 collective-permute-done.6.refs_3_
  123.5 1.3 collective-permute-start.11
  124.8 0.0 collective-permute-done.7.refs_4_
  124.8 2.7 %collective-permute-start.12 = (bf16[256,768]{1,0:T(8,128)(2,1)S(1)}, bf16[256,768]{1,0:T(8,128)(2,1)S(1)}, u32[]{:S(2)}, u32[]{:S(2)}) collective-permute-start(bf16[256,768]{1,0:T(8,128)(2,1)S(1)} %take.7.refs_9_.refs_0_), channel_id=1, source_target_pairs={{0,1},{1,0},{2,3},{3,2},{4,5},{5,4},{6,7},{7,6},{8,9},{9,8},{10,11... | collective-permute-start | bytes 1179656 | tf_op jit(solution)/shard_map/ppermute | solution.py:443
  127.6 0.0 collective-permute-done.10.refs_3_
  127.6 0.7 collective-permute-start.14
  128.2 11.7 %collective-permute-done.13.refs_2_ = bf16[256,768]{1,0:T(8,128)(2,1)S(1)} collective-permute-done((bf16[256,768]{1,0:T(8,128)(2,1)S(1)}, bf16[256,768]{1,0:T(8,128)(2,1)S(1)}, u32[]{:S(2)}, u32[]{:S(2)}) %collective-permute-start.13) | collective-permute-done | bytes 393248 | tf_op jit(solution)/shard_map/ppermute | solution.py:442
  140.0 1.5 collective-permute-start.15
  141.5 0.0 copy-done.1
  141.5 0.0 copy-done.6
  141.5 12.3 %fast_weights.5 = (bf16[256,768]{1,0:T(8,128)(2,1)S(1)}, f32[12,64,256]{2,1,0:T(8,128)S(1)}, f32[12,64,256]{2,1,0:T(8,128)S(1)}) custom-call(s32[4]{0:T(128)S(1)} %iota_xor_fusion.row_ref, bf16[256,768]{1,0:T(8,128)(2,1)S(1)} %take.5.refs_9_.refs_0_, bf16[256,768]{1,0:T(8,128)(2,1)S(1)} %collective-permute-done.4.refs_1_, bf16[256,768]{1,0:T(8,128)(2,1)S(1)} %copy-done.6, ...), custom_call_target="tpu_custom_call" | custom-call | tf_op jit(solution)/shard_map/fast_weights/pallas_call | solution.py:245
  153.7 0.0 collective-permute-done.8.refs_1_
  153.7 0.0 collective-permute-done.11.refs_4_
  153.8 12.9 %fast_weights.6 = (bf16[256,768]{1,0:T(8,128)(2,1)S(1)}, f32[12,64,256]{2,1,0:T(8,128)S(1)}, f32[12,64,256]{2,1,0:T(8,128)S(1)}) custom-call(s32[4]{0:T(128)S(1)} %iota_xor_fusion.row_ref, bf16[256,768]{1,0:T(8,128)(2,1)S(1)} %take.6.refs_9_.refs_0_, bf16[256,768]{1,0:T(8,128)(2,1)S(1)} %collective-permute-done.8.refs_1_, ...), custom_call_target="tpu_custom_call" | custom-call | tf_op jit(solution)/shard_map/fast_weights/pallas_call | solution.py:245
  166.7 0.0 collective-permute-done.12.refs_1_
  166.7 0.0 collective-permute-done.14.refs_3_
  166.7 0.0 collective-permute-done.15.refs_4_
  166.7 12.8 %fast_weights.7 = (bf16[256,768]{1,0:T(8,128)(2,1)S(1)}, f32[12,64,256]{2,1,0:T(8,128)}, f32[12,64,256]{2,1,0:T(8,128)}) custom-call(s32[4]{0:T(128)S(1)} %iota_xor_fusion.row_ref, bf16[256,768]{1,0:T(8,128)(2,1)S(1)} %take.7.refs_9_.refs_0_, bf16[256,768]{1,0:T(8,128)(2,1)S(1)} %collective-permute-done.12.refs_1_, ...), custom_call_target="tpu_custom_call" | custom-call | tf_op jit(solution)/shard_map/fast_weights/pallas_call | solution.py:245
  179.5 0.1 pad_maximum_fusion
  179.6 23.5 %all_to_all.11 = bf16[8,128,768]{2,1,0:T(8,128)(2,1)S(1)} all-to-all(bf16[8,128,768]{2,1,0:T(8,128)(2,1)S(1)} %bitcast.9), channel_id=1, replica_groups=mesh['seg'=8,'head'=4] {'seg'}, dimensions={0} | all-to-all | bytes 3145728 | tf_op jit(solution)/shard_map/all_to_all | solution.py:464
  203.1 1.1 copy.11
  (6 shorter events, 0.1 us)
Async XLA Ops:
  0.8 1.4 copy-start.2
  2.2 1.4 copy-start.3
  3.6 1.4 copy-start.4
  5.0 0.7 copy-start.8
  40.3 19.8 %collective-permute-start.1 = (bf16[256,768]{1,0:T(8,128)(2,1)}, bf16[256,768]{1,0:T(8,128)(2,1)}, u32[]{:S(2)}, u32[]{:S(2)}) collective-permute-start(bf16[256,768]{1,0:T(8,128)(2,1)} %take.4.refs_0_), channel_id=1, source_target_pairs={{0,2},{2,0},{1,3},{3,1},{4,6},{6,4},{5,7},{7,5},{8,10},{10,8},{9,1... | collective-permute-start | bytes 1179656 | tf_op jit(solution)/shard_map/ppermute | solution.py:442
  60.2 21.5 %collective-permute-start.5 = (bf16[256,768]{1,0:T(8,128)(2,1)S(1)}, bf16[256,768]{1,0:T(8,128)(2,1)S(1)}, u32[]{:S(2)}, u32[]{:S(2)}) collective-permute-start(bf16[256,768]{1,0:T(8,128)(2,1)S(1)} %take.5.refs_9_.refs_0_), channel_id=1, source_target_pairs={{0,2},{2,0},{1,3},{3,1},{4,6},{6,4},{5,7},{7,5},{8,10},{10,8},{9,1... | collective-permute-start | bytes 1179656 | tf_op jit(solution)/shard_map/ppermute | solution.py:442
  61.5 22.3 %collective-permute-start = (bf16[256,768]{1,0:T(8,128)(2,1)}, bf16[256,768]{1,0:T(8,128)(2,1)}, u32[]{:S(2)}, u32[]{:S(2)}) collective-permute-start(bf16[256,768]{1,0:T(8,128)(2,1)} %take.4.refs_0_), channel_id=1, source_target_pairs={{0,1},{1,0},{2,3},{3,2},{4,5},{5,4},{6,7},{7,6},{8,9},{9,8},{10,11... | collective-permute-start | bytes 1179656 | tf_op jit(solution)/shard_map/ppermute | solution.py:443
  65.6 18.9 %collective-permute-start.2 = (bf16[256,768]{1,0:T(8,128)(2,1)}, bf16[256,768]{1,0:T(8,128)(2,1)}, u32[]{:S(2)}, u32[]{:S(2)}) collective-permute-start(bf16[256,768]{1,0:T(8,128)(2,1)} %take.4.refs_0_), channel_id=1, source_target_pairs={{1,2},{2,1},{5,6},{6,5},{9,10},{10,9},{13,14},{14,13},{17,18},{18,... | collective-permute-start | bytes 1179656 | tf_op jit(solution)/shard_map/ppermute | solution.py:447
  67.0 23.7 %collective-permute-start.3 = (bf16[256,768]{1,0:T(8,128)(2,1)}, bf16[256,768]{1,0:T(8,128)(2,1)}, u32[]{:S(2)}, u32[]{:S(2)}) collective-permute-start(bf16[256,768]{1,0:T(8,128)(2,1)} %collective-permute-done.1.refs_1_.refs_2_), channel_id=1, source_target_pairs={{2,3},{1,0},{6,7},{5,4},{10,11},{9,8},{14,15},{13,12},{18,19},{17,... | collective-permute-start | bytes 1179656 | tf_op jit(solution)/shard_map/ppermute | solution.py:448
  81.7 0.7 copy-start.5
  82.4 29.1 %collective-permute-start.9 = (bf16[256,768]{1,0:T(8,128)(2,1)S(1)}, bf16[256,768]{1,0:T(8,128)(2,1)}, u32[]{:S(2)}, u32[]{:S(2)}) collective-permute-start(bf16[256,768]{1,0:T(8,128)(2,1)S(1)} %take.6.refs_9_.refs_0_), channel_id=1, source_target_pairs={{0,2},{2,0},{1,3},{3,1},{4,6},{6,4},{5,7},{7,5},{8,10},{10,8},{9,1... | collective-permute-start | bytes 1179656 | tf_op jit(solution)/shard_map/ppermute | solution.py:442
  83.7 39.8 %collective-permute-start.4 = (bf16[256,768]{1,0:T(8,128)(2,1)S(1)}, bf16[256,768]{1,0:T(8,128)(2,1)S(1)}, u32[]{:S(2)}, u32[]{:S(2)}) collective-permute-start(bf16[256,768]{1,0:T(8,128)(2,1)S(1)} %take.5.refs_9_.refs_0_), channel_id=1, source_target_pairs={{0,1},{1,0},{2,3},{3,2},{4,5},{5,4},{6,7},{7,6},{8,9},{9,8},{10,11... | collective-permute-start | bytes 1179656 | tf_op jit(solution)/shard_map/ppermute | solution.py:443
  83.8 39.7 %collective-permute-start.6 = (bf16[256,768]{1,0:T(8,128)(2,1)S(1)}, bf16[256,768]{1,0:T(8,128)(2,1)S(1)}, u32[]{:S(2)}, u32[]{:S(2)}) collective-permute-start(bf16[256,768]{1,0:T(8,128)(2,1)S(1)} %take.5.refs_9_.refs_0_), channel_id=1, source_target_pairs={{1,2},{2,1},{5,6},{6,5},{9,10},{10,9},{13,14},{14,13},{17,18},{18,... | collective-permute-start | bytes 1179656 | tf_op jit(solution)/shard_map/ppermute | solution.py:447
  84.5 43.0 %collective-permute-start.10 = (bf16[256,768]{1,0:T(8,128)(2,1)S(1)}, bf16[256,768]{1,0:T(8,128)(2,1)S(1)}, u32[]{:S(2)}, u32[]{:S(2)}) collective-permute-start(bf16[256,768]{1,0:T(8,128)(2,1)S(1)} %take.6.refs_9_.refs_0_), channel_id=1, source_target_pairs={{1,2},{2,1},{5,6},{6,5},{9,10},{10,9},{13,14},{14,13},{17,18},{18,... | collective-permute-start | bytes 1179656 | tf_op jit(solution)/shard_map/ppermute | solution.py:447
  90.7 34.1 %collective-permute-start.7 = (bf16[256,768]{1,0:T(8,128)(2,1)}, bf16[256,768]{1,0:T(8,128)(2,1)S(1)}, u32[]{:S(2)}, u32[]{:S(2)}) collective-permute-start(bf16[256,768]{1,0:T(8,128)(2,1)} %copy-done.5), channel_id=1, source_target_pairs={{2,3},{1,0},{6,7},{5,4},{10,11},{9,8},{14,15},{13,12},{18,19},{17,... | collective-permute-start | bytes 1179656 | tf_op jit(solution)/shard_map/ppermute | solution.py:448
  92.0 5.0 %copy-start = (bf16[3072,2304]{1,0:T(8,128)(2,1)S(1)}, bf16[3072,2304]{1,0:T(8,128)(2,1)}, u32[]{:S(2)}) copy-start(bf16[3072,2304]{1,0:T(8,128)(2,1)} %refs_6_.7) | copy-start | bytes 42467332
  97.0 1.1 copy-start.7
  98.2 43.3 %copy-start.1 = (bf16[3072,2304]{1,0:T(8,128)(2,1)S(1)}, bf16[3072,2304]{1,0:T(8,128)(2,1)}, u32[]{:S(2)}) copy-start(bf16[3072,2304]{1,0:T(8,128)(2,1)} %refs_6_.7) | copy-start | bytes 42467332
  111.5 30.0 %copy-start.6 = (bf16[256,768]{1,0:T(8,128)(2,1)S(1)}, bf16[256,768]{1,0:T(8,128)(2,1)}, u32[]{:S(2)}) copy-start(bf16[256,768]{1,0:T(8,128)(2,1)} %copy-done.5) | copy-start | bytes 1179652
  111.5 28.4 %collective-permute-start.13 = (bf16[256,768]{1,0:T(8,128)(2,1)S(1)}, bf16[256,768]{1,0:T(8,128)(2,1)S(1)}, u32[]{:S(2)}, u32[]{:S(2)}) collective-permute-start(bf16[256,768]{1,0:T(8,128)(2,1)S(1)} %take.7.refs_9_.refs_0_), channel_id=1, source_target_pairs={{0,2},{2,0},{1,3},{3,1},{4,6},{6,4},{5,7},{7,5},{8,10},{10,8},{9,1... | collective-permute-start | bytes 1179656 | tf_op jit(solution)/shard_map/ppermute | solution.py:442
  123.5 30.2 %collective-permute-start.8 = (bf16[256,768]{1,0:T(8,128)(2,1)S(1)}, bf16[256,768]{1,0:T(8,128)(2,1)S(1)}, u32[]{:S(2)}, u32[]{:S(2)}) collective-permute-start(bf16[256,768]{1,0:T(8,128)(2,1)S(1)} %take.6.refs_9_.refs_0_), channel_id=1, source_target_pairs={{0,1},{1,0},{2,3},{3,2},{4,5},{5,4},{6,7},{7,6},{8,9},{9,8},{10,11... | collective-permute-start | bytes 1179656 | tf_op jit(solution)/shard_map/ppermute | solution.py:443
  123.5 30.2 %collective-permute-start.11 = (bf16[256,768]{1,0:T(8,128)(2,1)}, bf16[256,768]{1,0:T(8,128)(2,1)S(1)}, u32[]{:S(2)}, u32[]{:S(2)}) collective-permute-start(bf16[256,768]{1,0:T(8,128)(2,1)} %collective-permute-done.9.refs_1_.refs_2_), channel_id=1, source_target_pairs={{2,3},{1,0},{6,7},{5,4},{10,11},{9,8},{14,15},{13,12},{18,19},{17,... | collective-permute-start | bytes 1179656 | tf_op jit(solution)/shard_map/ppermute | solution.py:448
  124.8 41.9 %collective-permute-start.12 = (bf16[256,768]{1,0:T(8,128)(2,1)S(1)}, bf16[256,768]{1,0:T(8,128)(2,1)S(1)}, u32[]{:S(2)}, u32[]{:S(2)}) collective-permute-start(bf16[256,768]{1,0:T(8,128)(2,1)S(1)} %take.7.refs_9_.refs_0_), channel_id=1, source_target_pairs={{0,1},{1,0},{2,3},{3,2},{4,5},{5,4},{6,7},{7,6},{8,9},{9,8},{10,11... | collective-permute-start | bytes 1179656 | tf_op jit(solution)/shard_map/ppermute | solution.py:443
  127.6 39.2 %collective-permute-start.14 = (bf16[256,768]{1,0:T(8,128)(2,1)S(1)}, bf16[256,768]{1,0:T(8,128)(2,1)S(1)}, u32[]{:S(2)}, u32[]{:S(2)}) collective-permute-start(bf16[256,768]{1,0:T(8,128)(2,1)S(1)} %take.7.refs_9_.refs_0_), channel_id=1, source_target_pairs={{1,2},{2,1},{5,6},{6,5},{9,10},{10,9},{13,14},{14,13},{17,18},{18,... | collective-permute-start | bytes 1179656 | tf_op jit(solution)/shard_map/ppermute | solution.py:447
  140.0 26.7 %collective-permute-start.15 = (bf16[256,768]{1,0:T(8,128)(2,1)S(1)}, bf16[256,768]{1,0:T(8,128)(2,1)S(1)}, u32[]{:S(2)}, u32[]{:S(2)}) collective-permute-start(bf16[256,768]{1,0:T(8,128)(2,1)S(1)} %collective-permute-done.13.refs_2_), channel_id=1, source_target_pairs={{2,3},{1,0},{6,7},{5,4},{10,11},{9,8},{14,15},{13,12},{18,19},{17,... | collective-permute-start | bytes 1179656 | tf_op jit(solution)/shard_map/ppermute | solution.py:448

commit v3 on v2

--- a/solution.py
+++ b/solution.py
@@ -13,6 +13,7 @@
 rms_epsilon = 1e-06
 GROUP = 6
 PB = 3
+VIDEO_STEP = 2
 CHUNK_VMEM = 26 * 1024 * 1024
 VMEM_LIMIT = 20 * 1024 * 1024
 gelu_a = 0.7978845608028654
@@ -39,61 +40,63 @@
 
 
 def attention_kernel(lens_ref, q_ref, k_ref, v_ref, rate_ref, out_ref, *, half):
-    video = pl.program_id(0)
-    length = lens_ref[video]
+    videos = q_ref.shape[0]
     seg_len = q_ref.shape[1]
     channels = q_ref.shape[2]
     width = 2 * half
     heads = channels // half
     key_at = lax.broadcasted_iota(jnp.int32, (seg_len, 2 * seg_len), 1)
     key_at = jnp.where(key_at >= seg_len, key_at - seg_len, key_at)
-    usable = (key_at >= TEXT_SLOTS) | (key_at < length)
     low = low_half((seg_len, width), half)
     zero = jnp.zeros((seg_len, width), jnp.bfloat16)
     ones = jnp.ones((seg_len, width), jnp.bfloat16)
     scale = jnp.asarray(half ** (-0.5), jnp.bfloat16)
     totals = jnp.concatenate([jnp.where(low, ones, zero), jnp.where(low, zero, ones)], axis=0)
-    for pair in range(channels // width):
-        lanes = slice(pair * width, (pair + 1) * width)
-        query = q_ref[0, :, lanes] * scale
-        key = k_ref[0, :, lanes]
-        value = v_ref[0, :, lanes]
-        keys = jnp.concatenate([jnp.where(low, key, zero), jnp.where(low, zero, key)], axis=0)
-        scores = jnp.where(usable, dot_nt(query, keys), -1e30)
-        parts = []
-        for side in range(2):
-            block = scores[:, side * seg_len : (side + 1) * seg_len]
-            largest = jnp.max(block, axis=1, keepdims=True)
-            parts.append(jnp.exp(block - largest).astype(jnp.bfloat16))
-        weights = jnp.concatenate(parts, axis=1)
-        values = jnp.concatenate([jnp.where(low, value, zero), jnp.where(low, zero, value)], axis=0)
-        mixed = dot_nn(weights, jnp.concatenate([values, totals], axis=1))
-        out_ref[0, :, lanes] = (mixed[:, :width] / mixed[:, width:]).astype(jnp.bfloat16)
-    token = lax.broadcasted_iota(jnp.int32, (seg_len, 1), 0)
-    open_token = ((token >= TEXT_SLOTS) | (token < length)).astype(jnp.float32)
-    rates = rate_ref[0]
-    spare = out_ref.shape[2] - channels
-    rates = jnp.concatenate(
-        [rates, jnp.zeros((spare - rates.shape[0], seg_len), jnp.float32)], axis=0
-    )
-    out_ref[0, :, channels:] = (rates.T * open_token).astype(jnp.bfloat16)
+    for v in range(videos):
+        length = lens_ref[pl.program_id(0) * videos + v]
+        usable = (key_at >= TEXT_SLOTS) | (key_at < length)
+        for pair in range(channels // width):
+            lanes = slice(pair * width, (pair + 1) * width)
+            query = q_ref[v, :, lanes] * scale
+            key = k_ref[v, :, lanes]
+            value = v_ref[v, :, lanes]
+            keys = jnp.concatenate([jnp.where(low, key, zero), jnp.where(low, zero, key)], axis=0)
+            scores = jnp.where(usable, dot_nt(query, keys), -1e30)
+            parts = []
+            for side in range(2):
+                block = scores[:, side * seg_len : (side + 1) * seg_len]
+                largest = jnp.max(block, axis=1, keepdims=True)
+                parts.append(jnp.exp(block - largest).astype(jnp.bfloat16))
+            weights = jnp.concatenate(parts, axis=1)
+            values = jnp.concatenate([jnp.where(low, value, zero), jnp.where(low, zero, value)], axis=0)
+            mixed = dot_nn(weights, jnp.concatenate([values, totals], axis=1))
+            out_ref[v, :, lanes] = (mixed[:, :width] / mixed[:, width:]).astype(jnp.bfloat16)
+        token = lax.broadcasted_iota(jnp.int32, (seg_len, 1), 0)
+        open_token = ((token >= TEXT_SLOTS) | (token < length)).astype(jnp.float32)
+        rates = rate_ref[v]
+        spare = out_ref.shape[2] - channels
+        rates = jnp.concatenate(
+            [rates, jnp.zeros((spare - rates.shape[0], seg_len), jnp.float32)], axis=0
+        )
+        out_ref[v, :, channels:] = (rates.T * open_token).astype(jnp.bfloat16)
 
 
 def attention(attn_query, attn_key, attn_value, lens, step_rate, half):
     videos, seg_len, channels = attn_query.shape
     heads = step_rate.shape[1]
     spare = 128
-    block = pl.BlockSpec((1, seg_len, channels), lambda v, lens: (v, 0, 0))
+    step = VIDEO_STEP if videos % VIDEO_STEP == 0 else 1
+    block = pl.BlockSpec((step, seg_len, channels), lambda v, lens: (v, 0, 0))
     return pl.pallas_call(
         functools.partial(attention_kernel, half=half),
         grid_spec=pltpu.PrefetchScalarGridSpec(
             num_scalar_prefetch=1,
-            grid=(videos,),
-            in_specs=[block, block, block, pl.BlockSpec((1, heads, seg_len), lambda v, lens: (v, 0, 0))],
-            out_specs=pl.BlockSpec((1, seg_len, channels + spare), lambda v, lens: (v, 0, 0)),
+            grid=(videos // step,),
+            in_specs=[block, block, block, pl.BlockSpec((step, heads, seg_len), lambda v, lens: (v, 0, 0))],
+            out_specs=pl.BlockSpec((step, seg_len, channels + spare), lambda v, lens: (v, 0, 0)),
         ),
         out_shape=jax.ShapeDtypeStruct((videos, seg_len, channels + spare), jnp.bfloat16),
-        compiler_params=pltpu.CompilerParams(vmem_limit_bytes=VMEM_LIMIT),
+        compiler_params=pltpu.CompilerParams(vmem_limit_bytes=58 * 1024 * 1024),
         name="attention",
     )(lens, attn_query, attn_key, attn_value, step_rate)
 
@@ -122,11 +125,10 @@
 
     squares = jnp.zeros((tokens, 128), jnp.float32)
     for i in range(shards):
+        source, rows = x_refs[min(i, 2)], slice(0, tokens) if i < 3 else slice(tokens, 2 * tokens)
         start = row_ref[i] * depth
         for at in range(0, depth, 128):
-            piece = x_refs[i][:, at : at + 128]
-            if i == shards - 1 and inputs > shards:
-                piece = piece + x_refs[shards][:, at : at + 128]
+            piece = source[rows, at : at + 128]
             x_s[:, pl.ds(pl.multiple_of(start + at, 128), 128)] = piece
             wide = piece.astype(jnp.float32)
             squares = squares + wide * wide
@@ -234,7 +236,6 @@
 
 
 def run_chunk(shards, rates, weight, row_blocks, w1, w2, half, after=()):
-    shards = [shard for shard in shards if shard is not None]
     tokens, depth = shards[0].shape
     heads, _, hidden = w1.shape
     inputs = len(shards)
@@ -375,28 +376,32 @@
     return results.astype(jnp.bfloat16)
 
 
-def take_kernel(*refs, at):
+def take_kernel(*refs, at, rows):
     out = refs[-1]
-    out[...] = refs[0][at : at + out.shape[0], : out.shape[1]]
-
-
-def take(source, at, rows, columns, after):
+    out[:rows] = refs[0][at : at + rows, : out.shape[1]]
+    if out.shape[0] > rows:
+        out[rows:] = refs[1][...]
+
+
+def take(source, at, rows, columns, second=None, after=(), beside=()):
+    inputs = [source] if second is None else [source, second]
     return pl.pallas_call(
-        functools.partial(take_kernel, at=at),
-        in_specs=[pl.BlockSpec(memory_space=pltpu.VMEM)]
+        functools.partial(take_kernel, at=at, rows=rows),
+        in_specs=[pl.BlockSpec(memory_space=pltpu.VMEM)] * len(inputs)
+        + [pl.BlockSpec(memory_space=pltpu.VMEM)] * len(beside)
         + [pl.BlockSpec(memory_space=pl.ANY)] * len(after),
         out_specs=pl.BlockSpec(memory_space=pltpu.VMEM),
-        out_shape=jax.ShapeDtypeStruct((rows, columns), source.dtype),
+        out_shape=jax.ShapeDtypeStruct((rows * len(inputs), columns), source.dtype),
+        cost_estimate=pl.CostEstimate(flops=1, transcendentals=0, bytes_accessed=1),
         compiler_params=pltpu.CompilerParams(vmem_limit_bytes=8 * 1024 * 1024),
         name="take",
-    )(source, *after)
-
-
-CHUNK_PARTS = (4, 4, 4, 4)
-FAR_GATE = 1
-OUT_GATE = 3
-KG = 1
-DIRECT = ()
+    )(*inputs, *beside, *after)
+
+
+CHUNK_PARTS = (3, 4, 4, 3, 2)
+LAG = 2
+AHEAD = 2
+WAT = 0
 
 
 def chunk_sizes(tokens):
@@ -407,9 +412,6 @@
 
 NEAR = [(0, 1), (1, 0), (2, 3), (3, 2)]
 FAR = [(0, 2), (2, 0), (1, 3), (3, 1)]
-INNER = [(1, 2), (2, 1)]
-OUTER = [(2, 3), (1, 0)]
-ACROSS = [(0, 3), (3, 0), (1, 2), (2, 1)]
 
 
 def by_video(attn_query, attn_key, attn_value, prompt_len, ttt_weight, init_w1, init_w2t, step_rate):
@@ -426,40 +428,36 @@
     chunk = tokens // 4
     count = lax.axis_size("head")
     me = lax.axis_index("head")
-    row_blocks = me ^ jnp.arange(4, dtype=jnp.int32)
+    row_blocks = me ^ jnp.array([0, 2, 1, 3], jnp.int32)
     sizes = chunk_sizes(tokens)
     ends = [sum(sizes[: c + 1]) for c in range(len(sizes))]
-    blocks, pieces, outs = [], [], []
-
-    def send(c):
-        at, size = ends[c] - sizes[c], sizes[c]
-        after = []
-        if c >= FAR_GATE:
-            after.append(pieces[c - FAR_GATE][0])
-        if c >= OUT_GATE:
-            after.append(outs[c - OUT_GATE])
-        block = take(mine, at, size, channels, after)
-        far = lax.ppermute(block, "head", FAR)
-        near = lax.ppermute(block, "head", NEAR)
-        if c in DIRECT:
-            pieces.append((far, near, lax.ppermute(block, "head", ACROSS), None))
-        else:
-            inner = lax.ppermute(block, "head", INNER)
-            outer = lax.ppermute(far, "head", OUTER)
-            pieces.append((far, near, inner, outer))
-        blocks.append(block)
-
-    for c in range(min(OUT_GATE, len(sizes))):
-        send(c)
-    for c in range(len(sizes)):
-        far, near, inner, outer = pieces[c]
-        rate = rates[ends[c] - sizes[c] : ends[c]]
-        after = [blocks[c + KG]] if c + KG < len(blocks) else []
-        shards = [blocks[c], near, far, inner, outer]
-        out, w1, w2 = run_chunk(shards, rate, ttt_weight, row_blocks, w1, w2, half, after)
-        outs.append(out)
-        if c + OUT_GATE < len(sizes):
-            send(c + OUT_GATE)
+    chunks = len(sizes)
+    outs, own, far, near = [], [], [], []
+
+    def send_far(c, after):
+        own.append(take(mine, ends[c] - sizes[c], sizes[c], channels, after=after))
+        far.append(lax.ppermute(own[c], "head", FAR))
+
+    def send_near(c, after):
+        both = take(own[c], 0, sizes[c], channels, far[c], after, [ttt_weight] if c == WAT else [])
+        near.append(lax.ppermute(both, "head", NEAR))
+        return both
+
+    for c in range(min(AHEAD, chunks)):
+        send_far(c, [])
+    for c in range(chunks + 1):
+        if c < chunks:
+            both = send_near(c, [outs[c - LAG]] if c >= LAG else [])
+        if c + AHEAD < chunks:
+            send_far(c + AHEAD, [both])
+        if c > 0:
+            d = c - 1
+            after = [own[c + AHEAD]] if c + AHEAD < chunks else [both] if c < chunks else []
+            rate = rates[ends[d] - sizes[d] : ends[d]]
+            out, w1, w2 = run_chunk(
+                [own[d], far[d], near[d]], rate, ttt_weight, row_blocks, w1, w2, half, after
+            )
+            outs.append(out)
     result = jnp.concatenate(outs, axis=0).reshape(videos, seg_len, channels)
     return lax.all_to_all(result, "seg", split_axis=0, concat_axis=0, tiled=True)
 

time: 205 us -> 191 us (0.932)
  starting transfers between devices: 30.3 us -> 14.5 us
  waiting for transfers between devices: 47.9 us -> 58.3 us
  local copies, waits for them, and re-layouts: 13.7 us -> 7.76 us
  other arithmetic: 2.54 us -> 0.14 us
    ppermute x16 -> x10, starting transfers between devices: 30.3 us -> 14.5 us  [the longest x5 9.66 us: send_far(): far.append(lax.ppermute(own[c], 'head', FAR))]
    ppermute x16 -> x10, waiting for transfers between devices: 47.9 us -> 58.3 us  [the longest x5 31.8 us: send_near(): near.append(lax.ppermute(both, 'head', NEAR))]
    unnamed x20 -> x16, local copies, waits for them, and re-layouts: 13.7 us -> 7.72 us
    pallas_call x4 -> x5, Pallas kernels: 51.3 us -> 50.4 us  [run_chunk(): pl.pallas_call(functools.partial(chunk_kernel, inputs=inputs, shards=coun...]
  transfers between devices with their start and end apart: 16 -> 10, of which waited for: 4 -> 5; matrix products, arithmetic and copies ran while one was open for 1% -> 0% of each run, Pallas kernels for 19% -> 23%
where the time goes in v3:
time: 191 us
  waiting for transfers between devices  58.3 us (31%)
  Pallas kernels  57.4 us (30%)
  blocking collectives  52.4 us (27%)
  starting transfers between devices  14.5 us (8%)
  local copies, waits for them, and re-layouts  7.76 us (4%)
    pallas_call x5, Pallas kernels, run_chunk(): pl.pallas_call(functools.partial(chunk_kernel, inputs=inputs, shards=coun...  50.4 us
    ppermute x5, waiting for transfers between devices, send_near(): near.append(lax.ppermute(both, 'head', NEAR))  31.8 us
    all_to_all x1, blocking collectives, by_video(): mine = lax.all_to_all(mixed, 'seg', split_axis=0, concat_axis=0, tiled=True)  29 us
    ppermute x5, waiting for transfers between devices, send_far(): far.append(lax.ppermute(own[c], 'head', FAR))  26.5 us
    all_to_all x1, blocking collectives, by_video(): lax.all_to_all(result, 'seg', split_axis=0, concat_axis=0, tiled=True)  23.5 us
    ppermute x5, starting transfers between devices, send_far(): far.append(lax.ppermute(own[c], 'head', FAR))  9.66 us
    unnamed x16, local copies, waits for them, and re-layouts  7.72 us
    pallas_call x1, Pallas kernels, attention(): pl.pallas_call(functools.partial(attention_kernel, half=half), grid_spec=...  6.62 us
  transfers between devices with their start and end apart: 10, of which 5 were waited for; matrix products, arithmetic and copies ran while one was open for 0% of the time, Pallas kernels for 23%

profile of v3, /device:TPU:0, one launch (start us, length us, event | category | flops | bytes accessed | tf_op | source)
XLA Modules:
  0.0 190.7 jit_solution(5494388507746237284)
XLA Ops:
  0.0 1.4 copy.10.rate_ref
  1.4 6.6 %attention.1 = bf16[8,128,896]{2,1,0:T(8,128)(2,1)} custom-call(s32[8]{0:T(128)} %bitcast.12, bf16[8,128,768]{2,1,0:T(8,128)(2,1)} %q_ref.1, bf16[8,128,768]{2,1,0:T(8,128)(2,1)} %k_ref.1, bf16[8,128,768]{2,1,0:T(8,128)(2,1)} %v_ref.1, f32[8,12,128]{2,1,0:T(8,128)} %copy.10.rate_ref), custom_call_target="tpu_custom_call" | custom-call | tf_op jit(solution)/shard_map/attention/pallas_call | solution.py:90
  8.1 29.0 %all_to_all.10 = bf16[8,128,896]{2,1,0:T(8,128)(2,1)S(1)} all-to-all(bf16[8,128,896]{2,1,0:T(8,128)(2,1)} %attention.1), channel_id=1, replica_groups=mesh['seg'=8,'head'=4] {'seg'}, dimensions={0} | all-to-all | bytes 3670016 | tf_op jit(solution)/shard_map/all_to_all | solution.py:422
  37.0 0.0 copy-start.3
  37.0 2.7 %collective-permute-start = (bf16[192,768]{1,0:T(8,128)(2,1)S(1)}, bf16[192,768]{1,0:T(8,128)(2,1)S(1)}, u32[]{:S(2)}, u32[]{:S(2)}) collective-permute-start(bf16[192,768]{1,0:T(8,128)(2,1)S(1)} %take.10.refs_0_), channel_id=1, source_target_pairs={{0,2},{2,0},{1,3},{3,1},{4,6},{6,4},{5,7},{7,5},{8,10},{10,8},{9,1... | collective-permute-start | bytes 884744 | tf_op jit(solution)/shard_map/ppermute | solution.py:439
  39.7 0.0 copy-done.3
  39.7 0.1 reduce_sum.9
  39.8 1.1 collective-permute-start.2
  40.9 21.1 %collective-permute-done.refs_1_ = bf16[192,768]{1,0:T(8,128)(2,1)S(1)} collective-permute-done((bf16[192,768]{1,0:T(8,128)(2,1)S(1)}, bf16[192,768]{1,0:T(8,128)(2,1)S(1)}, u32[]{:S(2)}, u32[]{:S(2)}) %collective-permute-start) | collective-permute-done | bytes 294944 | tf_op jit(solution)/shard_map/ppermute | solution.py:439
  62.0 0.0 copy-start
  62.0 5.0 %copy-done = bf16[3072,2304]{1,0:T(8,128)(2,1)S(1)} copy-done((bf16[3072,2304]{1,0:T(8,128)(2,1)S(1)}, bf16[3072,2304]{1,0:T(8,128)(2,1)}, u32[]{:S(2)}) %copy-start) | copy-done | bytes 14155800
  67.0 0.0 copy-start.1
  67.1 0.1 collective-permute-start.1
  67.2 0.1 broadcast_subtract_fusion.refs_6_
  67.2 0.0 copy-start.4
  67.3 3.0 %collective-permute-start.4 = (bf16[256,768]{1,0:T(8,128)(2,1)S(1)}, bf16[256,768]{1,0:T(8,128)(2,1)S(1)}, u32[]{:S(2)}, u32[]{:S(2)}) collective-permute-start(bf16[256,768]{1,0:T(8,128)(2,1)S(1)} %take.15.refs_0_), channel_id=1, source_target_pairs={{0,2},{2,0},{1,3},{3,1},{4,6},{6,4},{5,7},{7,5},{8,10},{10,8},{9,1... | collective-permute-start | bytes 1179656 | tf_op jit(solution)/shard_map/ppermute | solution.py:439
  70.3 0.0 copy-done.4
  70.3 0.0 collective-permute-done.2.refs_1_
  70.3 0.1 take.13.refs_1_
  70.4 0.0 copy-start.2
  70.4 0.4 collective-permute-start.3
  70.8 21.0 %collective-permute-done.1.refs_2_ = bf16[384,768]{1,0:T(8,128)(2,1)S(1)} collective-permute-done((bf16[384,768]{1,0:T(8,128)(2,1)S(1)}, bf16[384,768]{1,0:T(8,128)(2,1)S(1)}, u32[]{:S(2)}, u32[]{:S(2)}) %collective-permute-start.1) | collective-permute-done | bytes 589856 | tf_op jit(solution)/shard_map/ppermute | solution.py:443
  91.8 0.0 copy-done.1
  91.8 0.0 copy-done.2
  91.9 9.3 %fast_weights.5 = (bf16[192,768]{1,0:T(8,128)(2,1)S(1)}, f32[12,64,256]{2,1,0:T(8,128)S(1)}, f32[12,64,256]{2,1,0:T(8,128)S(1)}) custom-call(s32[4]{0:T(128)S(1)} %broadcast_xor_fusion.row_ref, bf16[192,768]{1,0:T(8,128)(2,1)S(1)} %take.10.refs_0_, bf16[192,768]{1,0:T(8,128)(2,1)S(1)} %collective-permute-done.refs_1_, ...), custom_call_target="tpu_custom_call" | custom-call | tf_op jit(solution)/shard_map/fast_weights/pallas_call | solution.py:246
  101.2 0.0 collective-permute-done.4.refs_1_
  101.2 0.1 take.16.refs_1_
  101.3 0.1 collective-permute-start.5
  101.4 2.9 %collective-permute-start.6 = (bf16[192,768]{1,0:T(8,128)(2,1)S(1)}, bf16[192,768]{1,0:T(8,128)(2,1)S(1)}, u32[]{:S(2)}, u32[]{:S(2)}) collective-permute-start(bf16[192,768]{1,0:T(8,128)(2,1)S(1)} %take.14.refs_7_.refs_0_), channel_id=1, source_target_pairs={{0,2},{2,0},{1,3},{3,1},{4,6},{6,4},{5,7},{7,5},{8,10},{10,8},{9,1... | collective-permute-start | bytes 884744 | tf_op jit(solution)/shard_map/ppermute | solution.py:439
  104.3 10.7 %collective-permute-done.3.refs_2_ = bf16[512,768]{1,0:T(8,128)(2,1)S(1)} collective-permute-done((bf16[512,768]{1,0:T(8,128)(2,1)S(1)}, bf16[512,768]{1,0:T(8,128)(2,1)S(1)}, u32[]{:S(2)}, u32[]{:S(2)}) %collective-permute-start.3) | collective-permute-done | bytes 786464 | tf_op jit(solution)/shard_map/ppermute | solution.py:443
  115.0 12.3 %fast_weights.6 = (bf16[256,768]{1,0:T(8,128)(2,1)S(1)}, f32[12,64,256]{2,1,0:T(8,128)S(1)}, f32[12,64,256]{2,1,0:T(8,128)S(1)}) custom-call(s32[4]{0:T(128)S(1)} %broadcast_xor_fusion.row_ref, bf16[256,768]{1,0:T(8,128)(2,1)S(1)} %take.12.refs_0_, bf16[256,768]{1,0:T(8,128)(2,1)S(1)} %collective-permute-done.2.refs_1_, ...), custom_call_target="tpu_custom_call" | custom-call | tf_op jit(solution)/shard_map/fast_weights/pallas_call | solution.py:246
  127.3 0.5 collective-permute-done.6.refs_1_
  127.9 4.2 %collective-permute-start.7 = (bf16[384,768]{1,0:T(8,128)(2,1)S(1)}, bf16[384,768]{1,0:T(8,128)(2,1)S(1)}, u32[]{:S(2)}, u32[]{:S(2)}) collective-permute-start(bf16[384,768]{1,0:T(8,128)(2,1)S(1)} %take.18.refs_7_), channel_id=1, source_target_pairs={{0,1},{1,0},{2,3},{3,2},{4,5},{5,4},{6,7},{7,6},{8,9},{9,8},{10,11... | collective-permute-start | bytes 1769480 | tf_op jit(solution)/shard_map/ppermute | solution.py:443
  132.1 0.0 collective-permute-start.8
  132.1 0.0 collective-permute-done.5.refs_2_
  132.1 12.4 %fast_weights.7 = (bf16[256,768]{1,0:T(8,128)(2,1)S(1)}, f32[12,64,256]{2,1,0:T(8,128)S(1)}, f32[12,64,256]{2,1,0:T(8,128)S(1)}) custom-call(s32[4]{0:T(128)S(1)} %broadcast_xor_fusion.row_ref, bf16[256,768]{1,0:T(8,128)(2,1)S(1)} %take.15.refs_0_, bf16[256,768]{1,0:T(8,128)(2,1)S(1)} %collective-permute-done.4.refs_1_, ...), custom_call_target="tpu_custom_call" | custom-call | tf_op jit(solution)/shard_map/fast_weights/pallas_call | solution.py:246
  144.5 4.9 %collective-permute-done.8.refs_1_ = bf16[128,768]{1,0:T(8,128)(2,1)S(1)} collective-permute-done((bf16[128,768]{1,0:T(8,128)(2,1)S(1)}, bf16[128,768]{1,0:T(8,128)(2,1)S(1)}, u32[]{:S(2)}, u32[]{:S(2)}) %collective-permute-start.8) | collective-permute-done | bytes 196640 | tf_op jit(solution)/shard_map/ppermute | solution.py:439
  149.5 0.1 collective-permute-start.9
  149.6 0.0 collective-permute-done.7.refs_2_
  149.6 9.5 %fast_weights.8 = (bf16[192,768]{1,0:T(8,128)(2,1)S(1)}, f32[12,64,256]{2,1,0:T(8,128)S(1)}, f32[12,64,256]{2,1,0:T(8,128)S(1)}) custom-call(s32[4]{0:T(128)S(1)} %broadcast_xor_fusion.row_ref, bf16[192,768]{1,0:T(8,128)(2,1)S(1)} %take.14.refs_7_.refs_0_, bf16[192,768]{1,0:T(8,128)(2,1)S(1)} %collective-permute-done.6.refs_1_, ...), custom_call_target="tpu_custom_call" | custom-call | tf_op jit(solution)/shard_map/fast_weights/pallas_call | solution.py:246
  159.2 0.0 collective-permute-done.9.refs_2_
  159.2 6.9 %fast_weights.9 = (bf16[128,768]{1,0:T(8,128)(2,1)S(1)}, f32[12,64,256]{2,1,0:T(8,128)}, f32[12,64,256]{2,1,0:T(8,128)}) custom-call(s32[4]{0:T(128)S(1)} %broadcast_xor_fusion.row_ref, bf16[128,768]{1,0:T(8,128)(2,1)S(1)} %take.17.refs_7_.refs_0_, bf16[128,768]{1,0:T(8,128)(2,1)S(1)} %collective-permute-done.8.refs_1_, ...), custom_call_target="tpu_custom_call" | custom-call | tf_op jit(solution)/shard_map/fast_weights/pallas_call | solution.py:246
  166.1 23.5 %all_to_all.11 = bf16[8,128,768]{2,1,0:T(8,128)(2,1)S(1)} all-to-all(bf16[8,128,768]{2,1,0:T(8,128)(2,1)S(1)} %bitcast.11), channel_id=1, replica_groups=mesh['seg'=8,'head'=4] {'seg'}, dimensions={0} | all-to-all | bytes 3145728 | tf_op jit(solution)/shard_map/all_to_all | solution.py:462
  189.5 1.1 copy.16
  (18 shorter events, 0.4 us)
Async XLA Ops:
  37.0 2.7 %copy-start.3 = (f32[12,64,256]{2,1,0:T(8,128)S(1)}, f32[12,64,256]{2,1,0:T(8,128)}, u32[]{:S(2)}) copy-start(f32[12,64,256]{2,1,0:T(8,128)} %param.15) | copy-start | bytes 2359300
  37.0 25.0 %collective-permute-start = (bf16[192,768]{1,0:T(8,128)(2,1)S(1)}, bf16[192,768]{1,0:T(8,128)(2,1)S(1)}, u32[]{:S(2)}, u32[]{:S(2)}) collective-permute-start(bf16[192,768]{1,0:T(8,128)(2,1)S(1)} %take.10.refs_0_), channel_id=1, source_target_pairs={{0,2},{2,0},{1,3},{3,1},{4,6},{6,4},{5,7},{7,5},{8,10},{10,8},{9,1... | collective-permute-start | bytes 884744 | tf_op jit(solution)/shard_map/ppermute | solution.py:439
  39.8 30.5 %collective-permute-start.2 = (bf16[256,768]{1,0:T(8,128)(2,1)S(1)}, bf16[256,768]{1,0:T(8,128)(2,1)S(1)}, u32[]{:S(2)}, u32[]{:S(2)}) collective-permute-start(bf16[256,768]{1,0:T(8,128)(2,1)S(1)} %take.12.refs_0_), channel_id=1, source_target_pairs={{0,2},{2,0},{1,3},{3,1},{4,6},{6,4},{5,7},{7,5},{8,10},{10,8},{9,1... | collective-permute-start | bytes 1179656 | tf_op jit(solution)/shard_map/ppermute | solution.py:439
  62.0 5.0 %copy-start = (bf16[3072,2304]{1,0:T(8,128)(2,1)S(1)}, bf16[3072,2304]{1,0:T(8,128)(2,1)}, u32[]{:S(2)}) copy-start(bf16[3072,2304]{1,0:T(8,128)(2,1)} %refs_4_.9) | copy-start | bytes 42467332
  67.0 24.8 %copy-start.1 = (bf16[3072,2304]{1,0:T(8,128)(2,1)S(1)}, bf16[3072,2304]{1,0:T(8,128)(2,1)}, u32[]{:S(2)}) copy-start(bf16[3072,2304]{1,0:T(8,128)(2,1)} %refs_4_.9) | copy-start | bytes 42467332
  67.1 24.8 %collective-permute-start.1 = (bf16[384,768]{1,0:T(8,128)(2,1)S(1)}, bf16[384,768]{1,0:T(8,128)(2,1)S(1)}, u32[]{:S(2)}, u32[]{:S(2)}) collective-permute-start(bf16[384,768]{1,0:T(8,128)(2,1)S(1)} %take.11.refs_1_), channel_id=1, source_target_pairs={{0,1},{1,0},{2,3},{3,2},{4,5},{5,4},{6,7},{7,6},{8,9},{9,8},{10,11... | collective-permute-start | bytes 1769480 | tf_op jit(solution)/shard_map/ppermute | solution.py:443
  67.2 3.1 %copy-start.4 = (s32[4]{0:T(128)S(1)}, s32[4]{0:T(128)}, u32[]{:S(2)}) copy-start(s32[4]{0:T(128)} %constant.11.clone) | copy-start | bytes 52
  67.3 33.9 %collective-permute-start.4 = (bf16[256,768]{1,0:T(8,128)(2,1)S(1)}, bf16[256,768]{1,0:T(8,128)(2,1)S(1)}, u32[]{:S(2)}, u32[]{:S(2)}) collective-permute-start(bf16[256,768]{1,0:T(8,128)(2,1)S(1)} %take.15.refs_0_), channel_id=1, source_target_pairs={{0,2},{2,0},{1,3},{3,1},{4,6},{6,4},{5,7},{7,5},{8,10},{10,8},{9,1... | collective-permute-start | bytes 1179656 | tf_op jit(solution)/shard_map/ppermute | solution.py:439
  70.4 21.5 %copy-start.2 = (f32[12,64,256]{2,1,0:T(8,128)S(1)}, f32[12,64,256]{2,1,0:T(8,128)}, u32[]{:S(2)}) copy-start(f32[12,64,256]{2,1,0:T(8,128)} %refs_5_.1) | copy-start | bytes 2359300
  70.4 44.6 %collective-permute-start.3 = (bf16[512,768]{1,0:T(8,128)(2,1)S(1)}, bf16[512,768]{1,0:T(8,128)(2,1)S(1)}, u32[]{:S(2)}, u32[]{:S(2)}) collective-permute-start(bf16[512,768]{1,0:T(8,128)(2,1)S(1)} %take.13.refs_1_), channel_id=1, source_target_pairs={{0,1},{1,0},{2,3},{3,2},{4,5},{5,4},{6,7},{7,6},{8,9},{9,8},{10,11... | collective-permute-start | bytes 2359304 | tf_op jit(solution)/shard_map/ppermute | solution.py:443
  101.3 30.8 %collective-permute-start.5 = (bf16[512,768]{1,0:T(8,128)(2,1)S(1)}, bf16[512,768]{1,0:T(8,128)(2,1)S(1)}, u32[]{:S(2)}, u32[]{:S(2)}) collective-permute-start(bf16[512,768]{1,0:T(8,128)(2,1)S(1)} %take.16.refs_1_), channel_id=1, source_target_pairs={{0,1},{1,0},{2,3},{3,2},{4,5},{5,4},{6,7},{7,6},{8,9},{9,8},{10,11... | collective-permute-start | bytes 2359304 | tf_op jit(solution)/shard_map/ppermute | solution.py:443
  101.4 26.5 %collective-permute-start.6 = (bf16[192,768]{1,0:T(8,128)(2,1)S(1)}, bf16[192,768]{1,0:T(8,128)(2,1)S(1)}, u32[]{:S(2)}, u32[]{:S(2)}) collective-permute-start(bf16[192,768]{1,0:T(8,128)(2,1)S(1)} %take.14.refs_7_.refs_0_), channel_id=1, source_target_pairs={{0,2},{2,0},{1,3},{3,1},{4,6},{6,4},{5,7},{7,5},{8,10},{10,8},{9,1... | collective-permute-start | bytes 884744 | tf_op jit(solution)/shard_map/ppermute | solution.py:439
  127.9 21.7 %collective-permute-start.7 = (bf16[384,768]{1,0:T(8,128)(2,1)S(1)}, bf16[384,768]{1,0:T(8,128)(2,1)S(1)}, u32[]{:S(2)}, u32[]{:S(2)}) collective-permute-start(bf16[384,768]{1,0:T(8,128)(2,1)S(1)} %take.18.refs_7_), channel_id=1, source_target_pairs={{0,1},{1,0},{2,3},{3,2},{4,5},{5,4},{6,7},{7,6},{8,9},{9,8},{10,11... | collective-permute-start | bytes 1769480 | tf_op jit(solution)/shard_map/ppermute | solution.py:443
  132.1 17.3 %collective-permute-start.8 = (bf16[128,768]{1,0:T(8,128)(2,1)S(1)}, bf16[128,768]{1,0:T(8,128)(2,1)S(1)}, u32[]{:S(2)}, u32[]{:S(2)}) collective-permute-start(bf16[128,768]{1,0:T(8,128)(2,1)S(1)} %take.17.refs_7_.refs_0_), channel_id=1, source_target_pairs={{0,2},{2,0},{1,3},{3,1},{4,6},{6,4},{5,7},{7,5},{8,10},{10,8},{9,1... | collective-permute-start | bytes 589832 | tf_op jit(solution)/shard_map/ppermute | solution.py:439
  149.5 9.7 %collective-permute-start.9 = (bf16[256,768]{1,0:T(8,128)(2,1)S(1)}, bf16[256,768]{1,0:T(8,128)(2,1)S(1)}, u32[]{:S(2)}, u32[]{:S(2)}) collective-permute-start(bf16[256,768]{1,0:T(8,128)(2,1)S(1)} %take.19.refs_7_), channel_id=1, source_target_pairs={{0,1},{1,0},{2,3},{3,2},{4,5},{5,4},{6,7},{7,6},{8,9},{9,8},{10,11... | collective-permute-start | bytes 1179656 | tf_op jit(solution)/shard_map/ppermute | solution.py:443

commit v4 on v3

--- a/solution.py
+++ b/solution.py
@@ -73,7 +73,7 @@
             out_ref[v, :, lanes] = (mixed[:, :width] / mixed[:, width:]).astype(jnp.bfloat16)
         token = lax.broadcasted_iota(jnp.int32, (seg_len, 1), 0)
         open_token = ((token >= TEXT_SLOTS) | (token < length)).astype(jnp.float32)
-        rates = rate_ref[v]
+        rates = rate_ref[:, pl.program_id(0) * videos + v, :]
         spare = out_ref.shape[2] - channels
         rates = jnp.concatenate(
             [rates, jnp.zeros((spare - rates.shape[0], seg_len), jnp.float32)], axis=0
@@ -92,23 +92,24 @@
         grid_spec=pltpu.PrefetchScalarGridSpec(
             num_scalar_prefetch=1,
             grid=(videos // step,),
-            in_specs=[block, block, block, pl.BlockSpec((step, heads, seg_len), lambda v, lens: (v, 0, 0))],
+            in_specs=[block, block, block, pl.BlockSpec((heads, videos, seg_len), lambda v, lens: (0, 0, 0))],
             out_specs=pl.BlockSpec((step, seg_len, channels + spare), lambda v, lens: (v, 0, 0)),
         ),
         out_shape=jax.ShapeDtypeStruct((videos, seg_len, channels + spare), jnp.bfloat16),
         compiler_params=pltpu.CompilerParams(vmem_limit_bytes=58 * 1024 * 1024),
         name="attention",
-    )(lens, attn_query, attn_key, attn_value, step_rate)
-
-
-def chunk_kernel(row_ref, *refs, inputs, shards, half, extra):
+    )(lens, attn_query, attn_key, attn_value, step_rate.transpose(1, 0, 2))
+
+
+def chunk_kernel(row_ref, *refs, inputs, shards, half, extra, first, last):
     x_refs, refs = refs[:inputs], refs[inputs:]
-    rate_ref, w_ref, w1_in, w2_in = refs[:4]
-    out_ref, w1_out, w2_out = refs[4 + extra : 7 + extra]
-    x_s, q_ref, k_ref, t_ref, e_ref, w1_s, w2_s = refs[7 + extra :]
+    rate_ref, w_ref, w1_in, w2_in, held_in = refs[:5]
+    out_ref, w1_out, w2_out, held_out = refs[5 + extra : 9 + extra]
+    x_s, q_ref, k_ref, t_ref, e_ref, w1_s, w2_s = refs[9 + extra :]
     tokens, depth = x_refs[0].shape
     width = 2 * half
     steps = tokens // MINI
+    skip = 1 if first else 0
     pairs = q_ref.shape[1] // width
     hidden = w1_in.shape[2]
     block_ones = half_ones(half)
@@ -135,6 +136,7 @@
     mean = jnp.sum(squares, axis=1, keepdims=True) / (shards * depth)
     inv = jnp.broadcast_to(lax.rsqrt(mean + rms_epsilon), (tokens, width))
 
+    q_ref[:MINI] = held_in[...]
     low = low_half((tokens, width), half)
     zero = jnp.zeros((tokens, width), jnp.float32)
     block = PB if pairs % PB == 0 else 1
@@ -142,17 +144,17 @@
         wide = 3 * width * block
         acc = dot_nn(x_s[...], w_ref[:, group * 3 * width : group * 3 * width + wide])
         for at in range(block):
-            first, middle, last = (
+            left, middle, right = (
                 acc[:, (3 * at + j) * width : (3 * at + j + 1) * width] * inv for j in range(3)
             )
-            query = jnp.where(low, first, middle)
-            key = pltpu.roll(jnp.where(low, last, first), half, 1)
-            target = jnp.where(low, middle, last) - key
+            query = jnp.where(low, left, middle)
+            key = pltpu.roll(jnp.where(low, right, left), half, 1)
+            target = jnp.where(low, middle, right) - key
             total_low = jnp.sum(jnp.where(low, target, zero), axis=1, keepdims=True)
             total_high = jnp.sum(jnp.where(low, zero, target), axis=1, keepdims=True)
             target = target - jnp.where(low, total_low, total_high) * (1.0 / half)
             lanes = slice((group + at) * width, (group + at + 1) * width)
-            q_ref[:, lanes] = query
+            q_ref[MINI:, lanes] = query
             k_ref[:, lanes] = key.astype(jnp.bfloat16)
             t_ref[:, lanes] = target
     head = lax.broadcasted_iota(jnp.int32, (rate_ref.shape[1], pairs * width), 0)
@@ -176,7 +178,7 @@
             for pair in group:
                 parts = []
                 if with_query:
-                    parts.append(q_ref[rows_of(step - 1), lanes[pair]].astype(jnp.bfloat16))
+                    parts.append(q_ref[rows_of(step), lanes[pair]].astype(jnp.bfloat16))
                 if with_key:
                     parts.append(k_ref[rows_of(step), lanes[pair]])
                 batch[pair] = jnp.concatenate(parts, axis=0) if len(parts) > 1 else parts[0]
@@ -202,8 +204,8 @@
                 unit[pair] = total[pair] * inverse[pair]
             if with_query:
                 for pair in group:
-                    query = q_ref[rows_of(step - 1), lanes[pair]]
-                    out_ref[rows_of(step - 1), lanes[pair]] = (query + unit[pair][:MINI]).astype(jnp.bfloat16)
+                    query = q_ref[rows_of(step), lanes[pair]]
+                    out_ref[rows_of(step - skip), lanes[pair]] = (query + unit[pair][:MINI]).astype(jnp.bfloat16)
             if not with_key:
                 continue
             rows = rows_of(step)
@@ -230,12 +232,15 @@
                 w1_out[head] = w1
                 w1_s[head, here, :] = w1.astype(jnp.bfloat16)
 
-    one(0, False, True)
-    lax.fori_loop(1, steps, lambda step, carry: (one(step, True, True), carry)[1], 0)
-    one(steps, True, False)
-
-
-def run_chunk(shards, rates, weight, row_blocks, w1, w2, half, after=()):
+    if first:
+        one(0, False, True)
+    lax.fori_loop(skip, steps, lambda step, carry: (one(step, True, True), carry)[1], 0)
+    if last:
+        one(steps, True, False)
+    held_out[...] = q_ref[tokens:]
+
+
+def run_chunk(shards, rates, weight, row_blocks, w1, w2, held, half, first, last, after=()):
     tokens, depth = shards[0].shape
     heads, _, hidden = w1.shape
     inputs = len(shards)
@@ -244,15 +249,20 @@
     inside = pl.BlockSpec(memory_space=pltpu.VMEM)
     wide = pltpu.VMEM((tokens, heads * half), jnp.float32)
     return pl.pallas_call(
-        functools.partial(chunk_kernel, inputs=inputs, shards=count, half=half, extra=len(after)),
+        functools.partial(chunk_kernel, inputs=inputs, shards=count, half=half, extra=len(after), first=first, last=last),
         in_specs=[pl.BlockSpec(memory_space=pltpu.SMEM)]
-        + [inside] * (inputs + 4)
+        + [inside] * (inputs + 5)
         + [pl.BlockSpec(memory_space=pl.ANY)] * len(after),
-        out_specs=[inside] * 3,
-        out_shape=[jax.ShapeDtypeStruct((tokens, heads * half), jnp.bfloat16), state, state],
+        out_specs=[inside] * 4,
+        out_shape=[
+            jax.ShapeDtypeStruct((tokens + MINI * (last - first), heads * half), jnp.bfloat16),
+            state,
+            state,
+            jax.ShapeDtypeStruct((MINI, heads * half), jnp.float32),
+        ],
         scratch_shapes=[
             pltpu.VMEM((tokens, count * depth), jnp.bfloat16),
-            wide,
+            pltpu.VMEM((tokens + MINI, heads * half), jnp.float32),
             pltpu.VMEM((tokens, heads * half), jnp.bfloat16),
             wide,
             wide,
@@ -261,7 +271,7 @@
         ],
         compiler_params=pltpu.CompilerParams(vmem_limit_bytes=CHUNK_VMEM),
         name="fast_weights",
-    )(row_blocks, *shards, rates, weight, w1, w2, *after)
+    )(row_blocks, *shards, rates, weight, w1, w2, held, *after)
 
 
 def normalize(values):
@@ -401,7 +411,7 @@
 CHUNK_PARTS = (3, 4, 4, 3, 2)
 LAG = 2
 AHEAD = 2
-WAT = 0
+WAT = 2
 
 
 def chunk_sizes(tokens):
@@ -423,6 +433,7 @@
     mine = mine.reshape(segments * seg_len, mixed.shape[2])
     rates = mine[:, channels:]
     w1 = init_w1
+    held = jnp.zeros((MINI, channels), jnp.float32)
     w2 = init_w2t - jnp.mean(init_w2t, axis=1, keepdims=True)
     tokens = segments * seg_len
     chunk = tokens // 4
@@ -435,11 +446,11 @@
     outs, own, far, near = [], [], [], []
 
     def send_far(c, after):
-        own.append(take(mine, ends[c] - sizes[c], sizes[c], channels, after=after))
+        own.append(take(mine, ends[c] - sizes[c], sizes[c], channels, after=after, beside=[ttt_weight] if c == WAT else []))
         far.append(lax.ppermute(own[c], "head", FAR))
 
     def send_near(c, after):
-        both = take(own[c], 0, sizes[c], channels, far[c], after, [ttt_weight] if c == WAT else [])
+        both = take(own[c], 0, sizes[c], channels, far[c], after)
         near.append(lax.ppermute(both, "head", NEAR))
         return both
 
@@ -454,8 +465,8 @@
             d = c - 1
             after = [own[c + AHEAD]] if c + AHEAD < chunks else [both] if c < chunks else []
             rate = rates[ends[d] - sizes[d] : ends[d]]
-            out, w1, w2 = run_chunk(
-                [own[d], far[d], near[d]], rate, ttt_weight, row_blocks, w1, w2, half, after
+            out, w1, w2, held = run_chunk(
+                [own[d], far[d], near[d]], rate, ttt_weight, row_blocks, w1, w2, held, half, d == 0, d + 1 == chunks, after
             )
             outs.append(out)
     result = jnp.concatenate(outs, axis=0).reshape(videos, seg_len, channels)

time: 191 us -> 188 us (0.984)
  waiting for transfers between devices: 58.3 us -> 56.3 us
    ppermute x5, waiting for transfers between devices: 26.5 us -> 21.1 us  [send_far(): far.append(lax.ppermute(own[c], 'head', FAR))]
    ppermute x5, starting transfers between devices: 9.66 us -> 13.3 us  [send_far(): far.append(lax.ppermute(own[c], 'head', FAR))]
    ppermute x5, waiting for transfers between devices: 31.8 us -> 35.2 us  [send_near(): near.append(lax.ppermute(both, 'head', NEAR))]
    ppermute x5, starting transfers between devices: 4.81 us -> 2.84 us  [send_near(): near.append(lax.ppermute(both, 'head', NEAR))]
    unnamed x16 -> x15, local copies, waits for them, and re-layouts: 7.72 us -> 6.27 us
  transfers between devices with their start and end apart: 10 -> 10, of which waited for: 5 -> 4; matrix products, arithmetic and copies ran while one was open for 0% -> 0% of each run, Pallas kernels for 23% -> 22%
where the time goes in v4:
time: 188 us
  Pallas kernels  56.4 us (30%)
  waiting for transfers between devices  56.3 us (30%)
  blocking collectives  52.4 us (28%)
  starting transfers between devices  16.1 us (9%)
  local copies, waits for them, and re-layouts  6.33 us (3%)
    pallas_call x5, Pallas kernels, run_chunk(): pl.pallas_call(functools.partial(chunk_kernel, inputs=inputs, shards=coun...  49.3 us
    ppermute x5, waiting for transfers between devices, send_near(): near.append(lax.ppermute(both, 'head', NEAR))  35.2 us
    all_to_all x1, blocking collectives, by_video(): mine = lax.all_to_all(mixed, 'seg', split_axis=0, concat_axis=0, tiled=True)  29 us
    all_to_all x1, blocking collectives, by_video(): lax.all_to_all(result, 'seg', split_axis=0, concat_axis=0, tiled=True)  23.4 us
    ppermute x5, waiting for transfers between devices, send_far(): far.append(lax.ppermute(own[c], 'head', FAR))  21.1 us
    ppermute x5, starting transfers between devices, send_far(): far.append(lax.ppermute(own[c], 'head', FAR))  13.3 us
    pallas_call x1, Pallas kernels, attention(): pl.pallas_call(functools.partial(attention_kernel, half=half), grid_spec=...  6.8 us
    unnamed x15, local copies, waits for them, and re-layouts  6.27 us
  transfers between devices with their start and end apart: 10, of which 4 were waited for; matrix products, arithmetic and copies ran while one was open for 0% of the time, Pallas kernels for 22%

profile of v4, /device:TPU:0, one launch (start us, length us, event | category | flops | bytes accessed | tf_op | source)
XLA Modules:
  0.0 187.9 jit_solution(14340476594594467531)
XLA Ops:
  0.0 6.8 %attention.1 = bf16[8,128,896]{2,1,0:T(8,128)(2,1)} custom-call(s32[8]{0:T(128)} %bitcast.14, bf16[8,128,768]{2,1,0:T(8,128)(2,1)} %q_ref.1, bf16[8,128,768]{2,1,0:T(8,128)(2,1)} %k_ref.1, bf16[8,128,768]{2,1,0:T(8,128)(2,1)} %v_ref.1, f32[12,8,128]{2,1,0:T(8,128)} %bitcast.13), custom_call_target="tpu_custom_call" | custom-call | tf_op jit(solution)/shard_map/attention/pallas_call | solution.py:90
  6.8 29.0 %all_to_all.10 = bf16[8,128,896]{2,1,0:T(8,128)(2,1)S(1)} all-to-all(bf16[8,128,896]{2,1,0:T(8,128)(2,1)} %attention.1), channel_id=1, replica_groups=mesh['seg'=8,'head'=4] {'seg'}, dimensions={0} | all-to-all | bytes 3670016 | tf_op jit(solution)/shard_map/all_to_all | solution.py:432
  35.8 0.0 copy-start.3
  35.8 2.7 %collective-permute-start = (bf16[192,768]{1,0:T(8,128)(2,1)S(1)}, bf16[192,768]{1,0:T(8,128)(2,1)S(1)}, u32[]{:S(2)}, u32[]{:S(2)}) collective-permute-start(bf16[192,768]{1,0:T(8,128)(2,1)S(1)} %take.10.refs_0_), channel_id=1, source_target_pairs={{0,2},{2,0},{1,3},{3,1},{4,6},{6,4},{5,7},{7,5},{8,10},{10,8},{9,1... | collective-permute-start | bytes 884744 | tf_op jit(solution)/shard_map/ppermute | solution.py:450
  38.4 0.0 copy-done.3
  38.4 0.1 reduce_sum.9
  38.5 1.1 collective-permute-start.2
  39.7 21.1 %collective-permute-done.refs_1_ = bf16[192,768]{1,0:T(8,128)(2,1)S(1)} collective-permute-done((bf16[192,768]{1,0:T(8,128)(2,1)S(1)}, bf16[192,768]{1,0:T(8,128)(2,1)S(1)}, u32[]{:S(2)}, u32[]{:S(2)}) %collective-permute-start) | collective-permute-done | bytes 294944 | tf_op jit(solution)/shard_map/ppermute | solution.py:450
  60.8 0.1 collective-permute-start.1
  60.9 0.1 broadcast_subtract_fusion.refs_6_
  61.0 0.0 copy-start
  61.0 5.0 %copy-done = bf16[3072,2304]{1,0:T(8,128)(2,1)S(1)} copy-done((bf16[3072,2304]{1,0:T(8,128)(2,1)S(1)}, bf16[3072,2304]{1,0:T(8,128)(2,1)}, u32[]{:S(2)}) %copy-start) | copy-done | bytes 14155800
  66.0 0.0 copy-start.1
  66.0 0.0 copy-start.4
  66.0 3.0 %collective-permute-start.4 = (bf16[256,768]{1,0:T(8,128)(2,1)S(1)}, bf16[256,768]{1,0:T(8,128)(2,1)S(1)}, u32[]{:S(2)}, u32[]{:S(2)}) collective-permute-start(bf16[256,768]{1,0:T(8,128)(2,1)S(1)} %take.15.refs_0_), channel_id=1, source_target_pairs={{0,2},{2,0},{1,3},{3,1},{4,6},{6,4},{5,7},{7,5},{8,10},{10,8},{9,1... | collective-permute-start | bytes 1179656 | tf_op jit(solution)/shard_map/ppermute | solution.py:450
  69.0 0.0 collective-permute-done.2.refs_1_
  69.0 0.1 take.13.refs_1_
  69.1 0.1 collective-permute-start.3
  69.2 0.0 copy-done.4
  69.2 0.0 copy-start.2
  69.3 19.9 %collective-permute-done.1.refs_2_ = bf16[384,768]{1,0:T(8,128)(2,1)S(1)} collective-permute-done((bf16[384,768]{1,0:T(8,128)(2,1)S(1)}, bf16[384,768]{1,0:T(8,128)(2,1)S(1)}, u32[]{:S(2)}, u32[]{:S(2)}) %collective-permute-start.1) | collective-permute-done | bytes 589856 | tf_op jit(solution)/shard_map/ppermute | solution.py:454
  89.2 0.0 copy-done.1
  89.2 0.0 copy-done.2
  89.2 8.6 %fast_weights.5 = (bf16[128,768]{1,0:T(8,128)(2,1)S(1)}, f32[12,64,256]{2,1,0:T(8,128)S(1)}, f32[12,64,256]{2,1,0:T(8,128)S(1)}, f32[64,768]{1,0:T(8,128)S(1)}) custom-call(s32[4]{0:T(128)S(1)} %broadcast_xor_fusion.row_ref, bf16[192,768]{1,0:T(8,128)(2,1)S(1)} %take.10.refs_0_, bf16[192,768]{1,0:T(8,128)(2,1)S(1)} %collective-permute-done.refs_1_, ...), custom_call_target="tpu_custom_call" | custom-call | tf_op jit(solution)/shard_map/fast_weights/pallas_call | solution.py:251
  97.8 0.0 collective-permute-done.4.refs_1_
  97.8 0.1 take.16.refs_1_
  97.9 0.1 collective-permute-start.5
  97.9 4.0 %collective-permute-start.6 = (bf16[192,768]{1,0:T(8,128)(2,1)S(1)}, bf16[192,768]{1,0:T(8,128)(2,1)S(1)}, u32[]{:S(2)}, u32[]{:S(2)}) collective-permute-start(bf16[192,768]{1,0:T(8,128)(2,1)S(1)} %take.14.refs_8_.refs_0_), channel_id=1, source_target_pairs={{0,2},{2,0},{1,3},{3,1},{4,6},{6,4},{5,7},{7,5},{8,10},{10,8},{9,1... | collective-permute-start | bytes 884744 | tf_op jit(solution)/shard_map/ppermute | solution.py:450
  102.0 10.3 %collective-permute-done.3.refs_2_ = bf16[512,768]{1,0:T(8,128)(2,1)S(1)} collective-permute-done((bf16[512,768]{1,0:T(8,128)(2,1)S(1)}, bf16[512,768]{1,0:T(8,128)(2,1)S(1)}, u32[]{:S(2)}, u32[]{:S(2)}) %collective-permute-start.3) | collective-permute-done | bytes 786464 | tf_op jit(solution)/shard_map/ppermute | solution.py:454
  112.3 12.0 %fast_weights.6 = (bf16[256,768]{1,0:T(8,128)(2,1)S(1)}, f32[12,64,256]{2,1,0:T(8,128)S(1)}, f32[12,64,256]{2,1,0:T(8,128)S(1)}, f32[64,768]{1,0:T(8,128)S(1)}) custom-call(s32[4]{0:T(128)S(1)} %broadcast_xor_fusion.row_ref, bf16[256,768]{1,0:T(8,128)(2,1)S(1)} %take.12.refs_0_, bf16[256,768]{1,0:T(8,128)(2,1)S(1)} %collective-permute-done.2.refs_1_, ...), custom_call_target="tpu_custom_call" | custom-call | tf_op jit(solution)/shard_map/fast_weights/pallas_call | solution.py:251
  124.3 0.0 collective-permute-done.6.refs_1_
  124.4 1.6 collective-permute-start.7
  126.1 2.5 %collective-permute-start.8 = (bf16[128,768]{1,0:T(8,128)(2,1)S(1)}, bf16[128,768]{1,0:T(8,128)(2,1)S(1)}, u32[]{:S(2)}, u32[]{:S(2)}) collective-permute-start(bf16[128,768]{1,0:T(8,128)(2,1)S(1)} %take.17.refs_8_.refs_0_), channel_id=1, source_target_pairs={{0,2},{2,0},{1,3},{3,1},{4,6},{6,4},{5,7},{7,5},{8,10},{10,8},{9,1... | collective-permute-start | bytes 589832 | tf_op jit(solution)/shard_map/ppermute | solution.py:450
  128.5 4.9 %collective-permute-done.5.refs_2_ = bf16[512,768]{1,0:T(8,128)(2,1)S(1)} collective-permute-done((bf16[512,768]{1,0:T(8,128)(2,1)S(1)}, bf16[512,768]{1,0:T(8,128)(2,1)S(1)}, u32[]{:S(2)}, u32[]{:S(2)}) %collective-permute-start.5) | collective-permute-done | bytes 786464 | tf_op jit(solution)/shard_map/ppermute | solution.py:454
  133.4 11.8 %fast_weights.7 = (bf16[256,768]{1,0:T(8,128)(2,1)S(1)}, f32[12,64,256]{2,1,0:T(8,128)S(1)}, f32[12,64,256]{2,1,0:T(8,128)S(1)}, f32[64,768]{1,0:T(8,128)S(1)}) custom-call(s32[4]{0:T(128)S(1)} %broadcast_xor_fusion.row_ref, bf16[256,768]{1,0:T(8,128)(2,1)S(1)} %take.15.refs_0_, bf16[256,768]{1,0:T(8,128)(2,1)S(1)} %collective-permute-done.4.refs_1_, ...), custom_call_target="tpu_custom_call" | custom-call | tf_op jit(solution)/shard_map/fast_weights/pallas_call | solution.py:251
  145.2 0.0 collective-permute-done.8.refs_1_
  145.3 1.0 collective-permute-start.9
  146.3 0.0 collective-permute-done.7.refs_2_
  146.3 9.3 %fast_weights.8 = (bf16[192,768]{1,0:T(8,128)(2,1)S(1)}, f32[12,64,256]{2,1,0:T(8,128)S(1)}, f32[12,64,256]{2,1,0:T(8,128)S(1)}, f32[64,768]{1,0:T(8,128)S(1)}) custom-call(s32[4]{0:T(128)S(1)} %broadcast_xor_fusion.row_ref, bf16[192,768]{1,0:T(8,128)(2,1)S(1)} %take.14.refs_8_.refs_0_, bf16[192,768]{1,0:T(8,128)(2,1)S(1)} %collective-permute-done.6.refs_1_, ...), custom_call_target="tpu_custom_call" | custom-call | tf_op jit(solution)/shard_map/fast_weights/pallas_call | solution.py:251
  155.7 0.0 collective-permute-done.9.refs_2_
  155.7 7.7 %fast_weights.9 = (bf16[192,768]{1,0:T(8,128)(2,1)S(1)}, f32[12,64,256]{2,1,0:T(8,128)}, f32[12,64,256]{2,1,0:T(8,128)}, f32[64,768]{1,0:T(8,128)}) custom-call(s32[4]{0:T(128)S(1)} %broadcast_xor_fusion.row_ref, bf16[128,768]{1,0:T(8,128)(2,1)S(1)} %take.17.refs_8_.refs_0_, bf16[128,768]{1,0:T(8,128)(2,1)S(1)} %collective-permute-done.8.refs_1_, ...), custom_call_target="tpu_custom_call" | custom-call | tf_op jit(solution)/shard_map/fast_weights/pallas_call | solution.py:251
  163.4 23.4 %all_to_all.11 = bf16[8,128,768]{2,1,0:T(8,128)(2,1)S(1)} all-to-all(bf16[8,128,768]{2,1,0:T(8,128)(2,1)S(1)} %bitcast.12), channel_id=1, replica_groups=mesh['seg'=8,'head'=4] {'seg'}, dimensions={0} | all-to-all | bytes 3145728 | tf_op jit(solution)/shard_map/all_to_all | solution.py:473
  186.8 1.1 copy.15
  (19 shorter events, 0.4 us)
Async XLA Ops:
  35.8 2.7 %copy-start.3 = (f32[12,64,256]{2,1,0:T(8,128)S(1)}, f32[12,64,256]{2,1,0:T(8,128)}, u32[]{:S(2)}) copy-start(f32[12,64,256]{2,1,0:T(8,128)} %param.15) | copy-start | bytes 2359300
  35.8 25.0 %collective-permute-start = (bf16[192,768]{1,0:T(8,128)(2,1)S(1)}, bf16[192,768]{1,0:T(8,128)(2,1)S(1)}, u32[]{:S(2)}, u32[]{:S(2)}) collective-permute-start(bf16[192,768]{1,0:T(8,128)(2,1)S(1)} %take.10.refs_0_), channel_id=1, source_target_pairs={{0,2},{2,0},{1,3},{3,1},{4,6},{6,4},{5,7},{7,5},{8,10},{10,8},{9,1... | collective-permute-start | bytes 884744 | tf_op jit(solution)/shard_map/ppermute | solution.py:450
  38.5 30.5 %collective-permute-start.2 = (bf16[256,768]{1,0:T(8,128)(2,1)S(1)}, bf16[256,768]{1,0:T(8,128)(2,1)S(1)}, u32[]{:S(2)}, u32[]{:S(2)}) collective-permute-start(bf16[256,768]{1,0:T(8,128)(2,1)S(1)} %take.12.refs_0_), channel_id=1, source_target_pairs={{0,2},{2,0},{1,3},{3,1},{4,6},{6,4},{5,7},{7,5},{8,10},{10,8},{9,1... | collective-permute-start | bytes 1179656 | tf_op jit(solution)/shard_map/ppermute | solution.py:450
  60.8 28.4 %collective-permute-start.1 = (bf16[384,768]{1,0:T(8,128)(2,1)S(1)}, bf16[384,768]{1,0:T(8,128)(2,1)S(1)}, u32[]{:S(2)}, u32[]{:S(2)}) collective-permute-start(bf16[384,768]{1,0:T(8,128)(2,1)S(1)} %take.11.refs_2_), channel_id=1, source_target_pairs={{0,1},{1,0},{2,3},{3,2},{4,5},{5,4},{6,7},{7,6},{8,9},{9,8},{10,11... | collective-permute-start | bytes 1769480 | tf_op jit(solution)/shard_map/ppermute | solution.py:454
  61.0 5.0 %copy-start = (bf16[3072,2304]{1,0:T(8,128)(2,1)S(1)}, bf16[3072,2304]{1,0:T(8,128)(2,1)}, u32[]{:S(2)}) copy-start(bf16[3072,2304]{1,0:T(8,128)(2,1)} %refs_4_.9) | copy-start | bytes 42467332
  66.0 23.2 %copy-start.1 = (bf16[3072,2304]{1,0:T(8,128)(2,1)S(1)}, bf16[3072,2304]{1,0:T(8,128)(2,1)}, u32[]{:S(2)}) copy-start(bf16[3072,2304]{1,0:T(8,128)(2,1)} %refs_4_.9) | copy-start | bytes 42467332
  66.0 3.2 %copy-start.4 = (s32[4]{0:T(128)S(1)}, s32[4]{0:T(128)}, u32[]{:S(2)}) copy-start(s32[4]{0:T(128)} %constant.12.clone) | copy-start | bytes 52
  66.0 31.8 %collective-permute-start.4 = (bf16[256,768]{1,0:T(8,128)(2,1)S(1)}, bf16[256,768]{1,0:T(8,128)(2,1)S(1)}, u32[]{:S(2)}, u32[]{:S(2)}) collective-permute-start(bf16[256,768]{1,0:T(8,128)(2,1)S(1)} %take.15.refs_0_), channel_id=1, source_target_pairs={{0,2},{2,0},{1,3},{3,1},{4,6},{6,4},{5,7},{7,5},{8,10},{10,8},{9,1... | collective-permute-start | bytes 1179656 | tf_op jit(solution)/shard_map/ppermute | solution.py:450
  69.1 43.2 %collective-permute-start.3 = (bf16[512,768]{1,0:T(8,128)(2,1)S(1)}, bf16[512,768]{1,0:T(8,128)(2,1)S(1)}, u32[]{:S(2)}, u32[]{:S(2)}) collective-permute-start(bf16[512,768]{1,0:T(8,128)(2,1)S(1)} %take.13.refs_1_), channel_id=1, source_target_pairs={{0,1},{1,0},{2,3},{3,2},{4,5},{5,4},{6,7},{7,6},{8,9},{9,8},{10,11... | collective-permute-start | bytes 2359304 | tf_op jit(solution)/shard_map/ppermute | solution.py:454
  69.2 20.0 %copy-start.2 = (f32[12,64,256]{2,1,0:T(8,128)S(1)}, f32[12,64,256]{2,1,0:T(8,128)}, u32[]{:S(2)}) copy-start(f32[12,64,256]{2,1,0:T(8,128)} %refs_5_.1) | copy-start | bytes 2359300
  97.9 35.6 %collective-permute-start.5 = (bf16[512,768]{1,0:T(8,128)(2,1)S(1)}, bf16[512,768]{1,0:T(8,128)(2,1)S(1)}, u32[]{:S(2)}, u32[]{:S(2)}) collective-permute-start(bf16[512,768]{1,0:T(8,128)(2,1)S(1)} %take.16.refs_1_), channel_id=1, source_target_pairs={{0,1},{1,0},{2,3},{3,2},{4,5},{5,4},{6,7},{7,6},{8,9},{9,8},{10,11... | collective-permute-start | bytes 2359304 | tf_op jit(solution)/shard_map/ppermute | solution.py:454
  97.9 26.4 %collective-permute-start.6 = (bf16[192,768]{1,0:T(8,128)(2,1)S(1)}, bf16[192,768]{1,0:T(8,128)(2,1)S(1)}, u32[]{:S(2)}, u32[]{:S(2)}) collective-permute-start(bf16[192,768]{1,0:T(8,128)(2,1)S(1)} %take.14.refs_8_.refs_0_), channel_id=1, source_target_pairs={{0,2},{2,0},{1,3},{3,1},{4,6},{6,4},{5,7},{7,5},{8,10},{10,8},{9,1... | collective-permute-start | bytes 884744 | tf_op jit(solution)/shard_map/ppermute | solution.py:450
  124.4 21.9 %collective-permute-start.7 = (bf16[384,768]{1,0:T(8,128)(2,1)S(1)}, bf16[384,768]{1,0:T(8,128)(2,1)S(1)}, u32[]{:S(2)}, u32[]{:S(2)}) collective-permute-start(bf16[384,768]{1,0:T(8,128)(2,1)S(1)} %take.18.refs_8_), channel_id=1, source_target_pairs={{0,1},{1,0},{2,3},{3,2},{4,5},{5,4},{6,7},{7,6},{8,9},{9,8},{10,11... | collective-permute-start | bytes 1769480 | tf_op jit(solution)/shard_map/ppermute | solution.py:454
  126.1 19.2 %collective-permute-start.8 = (bf16[128,768]{1,0:T(8,128)(2,1)S(1)}, bf16[128,768]{1,0:T(8,128)(2,1)S(1)}, u32[]{:S(2)}, u32[]{:S(2)}) collective-permute-start(bf16[128,768]{1,0:T(8,128)(2,1)S(1)} %take.17.refs_8_.refs_0_), channel_id=1, source_target_pairs={{0,2},{2,0},{1,3},{3,1},{4,6},{6,4},{5,7},{7,5},{8,10},{10,8},{9,1... | collective-permute-start | bytes 589832 | tf_op jit(solution)/shard_map/ppermute | solution.py:450
  145.3 10.4 %collective-permute-start.9 = (bf16[256,768]{1,0:T(8,128)(2,1)S(1)}, bf16[256,768]{1,0:T(8,128)(2,1)S(1)}, u32[]{:S(2)}, u32[]{:S(2)}) collective-permute-start(bf16[256,768]{1,0:T(8,128)(2,1)S(1)} %take.19.refs_8_), channel_id=1, source_target_pairs={{0,1},{1,0},{2,3},{3,2},{4,5},{5,4},{6,7},{7,6},{8,9},{9,8},{10,11... | collective-permute-start | bytes 1179656 | tf_op jit(solution)/shard_map/ppermute | solution.py:454

commit v5 on v4

--- a/solution.py
+++ b/solution.py
@@ -13,7 +13,7 @@
 rms_epsilon = 1e-06
 GROUP = 6
 PB = 3
-VIDEO_STEP = 2
+VIDEO_STEP = 4
 CHUNK_VMEM = 26 * 1024 * 1024
 VMEM_LIMIT = 20 * 1024 * 1024
 gelu_a = 0.7978845608028654
@@ -408,7 +408,7 @@
     )(*inputs, *beside, *after)
 
 
-CHUNK_PARTS = (3, 4, 4, 3, 2)
+CHUNK_PARTS = (4, 4, 4, 2, 2)
 LAG = 2
 AHEAD = 2
 WAT = 2

time: 188 us -> 187 us (level)
  waiting for transfers between devices: 56.3 us -> 52.5 us
    ppermute x5, waiting for transfers between devices: 35.2 us -> 19 us  [send_near(): near.append(lax.ppermute(both, 'head', NEAR))]
    ppermute x5, waiting for transfers between devices: 21.1 us -> 33.6 us  [send_far(): far.append(lax.ppermute(own[c], 'head', FAR))]
    ppermute x5, starting transfers between devices: 2.84 us -> 7.64 us  [send_near(): near.append(lax.ppermute(both, 'head', NEAR))]
    ppermute x5, starting transfers between devices: 13.3 us -> 10.3 us  [send_far(): far.append(lax.ppermute(own[c], 'head', FAR))]
    unnamed x15 -> x17, local copies, waits for them, and re-layouts: 6.27 us -> 6.27 us
  transfers between devices with their start and end apart: 10 -> 10, of which waited for: 4 -> 6; matrix products, arithmetic and copies ran while one was open for 0% -> 0% of each run, Pallas kernels for 22% -> 23%
where the time goes in v5:
time: 187 us; the launch traced here: 186 us
  Pallas kernels  56.6 us (30%)
  waiting for transfers between devices  52.5 us (28%)
  blocking collectives  52.4 us (28%)
  starting transfers between devices  17.9 us (10%)
  local copies, waits for them, and re-layouts  6.35 us (3%)
    pallas_call x5, Pallas kernels, run_chunk(): pl.pallas_call(functools.partial(chunk_kernel, inputs=inputs, shards=coun...  50.2 us
    ppermute x5, waiting for transfers between devices, send_far(): far.append(lax.ppermute(own[c], 'head', FAR))  33.6 us
    all_to_all x1, blocking collectives, by_video(): mine = lax.all_to_all(mixed, 'seg', split_axis=0, concat_axis=0, tiled=True)  29 us
    all_to_all x1, blocking collectives, by_video(): lax.all_to_all(result, 'seg', split_axis=0, concat_axis=0, tiled=True)  23.4 us
    ppermute x5, waiting for transfers between devices, send_near(): near.append(lax.ppermute(both, 'head', NEAR))  19 us
    ppermute x5, starting transfers between devices, send_far(): far.append(lax.ppermute(own[c], 'head', FAR))  10.3 us
    ppermute x5, starting transfers between devices, send_near(): near.append(lax.ppermute(both, 'head', NEAR))  7.64 us
    unnamed x17, local copies, waits for them, and re-layouts  6.27 us
  transfers between devices with their start and end apart: 10, of which 6 were waited for; matrix products, arithmetic and copies ran while one was open for 0% of the time, Pallas kernels for 23%

profile of v5, /device:TPU:0, one launch (start us, length us, event | category | flops | bytes accessed | tf_op | source)
XLA Modules:
  0.0 186.1 jit_solution(15999534217648091901)
XLA Ops:
  0.0 6.1 %attention.1 = bf16[8,128,896]{2,1,0:T(8,128)(2,1)} custom-call(s32[8]{0:T(128)} %bitcast.13, bf16[8,128,768]{2,1,0:T(8,128)(2,1)} %q_ref.1, bf16[8,128,768]{2,1,0:T(8,128)(2,1)} %k_ref.1, bf16[8,128,768]{2,1,0:T(8,128)(2,1)} %v_ref.1, f32[12,8,128]{2,1,0:T(8,128)} %bitcast.12), custom_call_target="tpu_custom_call" | custom-call | tf_op jit(solution)/shard_map/attention/pallas_call | solution.py:90
  6.1 29.0 %all_to_all.10 = bf16[8,128,896]{2,1,0:T(8,128)(2,1)S(1)} all-to-all(bf16[8,128,896]{2,1,0:T(8,128)(2,1)} %attention.1), channel_id=1, replica_groups=mesh['seg'=8,'head'=4] {'seg'}, dimensions={0} | all-to-all | bytes 3670016 | tf_op jit(solution)/shard_map/all_to_all | solution.py:432
  35.0 0.0 copy-start.3
  35.1 2.7 %collective-permute-start = (bf16[256,768]{1,0:T(8,128)(2,1)S(1)}, bf16[256,768]{1,0:T(8,128)(2,1)S(1)}, u32[]{:S(2)}, u32[]{:S(2)}) collective-permute-start(bf16[256,768]{1,0:T(8,128)(2,1)S(1)} %take.10.refs_0_), channel_id=1, source_target_pairs={{0,2},{2,0},{1,3},{3,1},{4,6},{6,4},{5,7},{7,5},{8,10},{10,8},{9,1... | collective-permute-start | bytes 1179656 | tf_op jit(solution)/shard_map/ppermute | solution.py:450
  37.7 0.0 copy-done.3
  37.7 0.1 reduce_sum.9
  37.8 16.9 %collective-permute-done.refs_1_ = bf16[256,768]{1,0:T(8,128)(2,1)S(1)} collective-permute-done((bf16[256,768]{1,0:T(8,128)(2,1)S(1)}, bf16[256,768]{1,0:T(8,128)(2,1)S(1)}, u32[]{:S(2)}, u32[]{:S(2)}) %collective-permute-start) | collective-permute-done | bytes 393248 | tf_op jit(solution)/shard_map/ppermute | solution.py:450
  54.7 0.1 take.11.refs_2_
  54.7 0.7 collective-permute-start.1
  55.5 0.0 copy-start.4
  55.5 3.4 %collective-permute-start.2 = (bf16[256,768]{1,0:T(8,128)(2,1)S(1)}, bf16[256,768]{1,0:T(8,128)(2,1)S(1)}, u32[]{:S(2)}, u32[]{:S(2)}) collective-permute-start(bf16[256,768]{1,0:T(8,128)(2,1)S(1)} %take.12.refs_0_), channel_id=1, source_target_pairs={{0,2},{2,0},{1,3},{3,1},{4,6},{6,4},{5,7},{7,5},{8,10},{10,8},{9,1... | collective-permute-start | bytes 1179656 | tf_op jit(solution)/shard_map/ppermute | solution.py:450
  58.9 0.0 copy-done.4
  58.9 0.1 broadcast_subtract_fusion.refs_6_
  59.0 0.0 copy-start
  59.0 5.0 %copy-done = bf16[3072,2304]{1,0:T(8,128)(2,1)S(1)} copy-done((bf16[3072,2304]{1,0:T(8,128)(2,1)S(1)}, bf16[3072,2304]{1,0:T(8,128)(2,1)}, u32[]{:S(2)}) %copy-start) | copy-done | bytes 14155800
  64.0 0.0 copy-start.5
  64.0 0.0 copy-start.1
  64.1 1.1 collective-permute-start.4
  65.2 0.0 copy-done.5
  65.2 16.7 %collective-permute-done.2.refs_1_ = bf16[256,768]{1,0:T(8,128)(2,1)S(1)} collective-permute-done((bf16[256,768]{1,0:T(8,128)(2,1)S(1)}, bf16[256,768]{1,0:T(8,128)(2,1)S(1)}, u32[]{:S(2)}, u32[]{:S(2)}) %collective-permute-start.2) | collective-permute-done | bytes 393248 | tf_op jit(solution)/shard_map/ppermute | solution.py:450
  81.8 0.1 take.13.refs_1_
  81.9 3.9 %collective-permute-start.3 = (bf16[512,768]{1,0:T(8,128)(2,1)S(1)}, bf16[512,768]{1,0:T(8,128)(2,1)S(1)}, u32[]{:S(2)}, u32[]{:S(2)}) collective-permute-start(bf16[512,768]{1,0:T(8,128)(2,1)S(1)} %take.13.refs_1_), channel_id=1, source_target_pairs={{0,1},{1,0},{2,3},{3,2},{4,5},{5,4},{6,7},{7,6},{8,9},{9,8},{10,11... | collective-permute-start | bytes 2359304 | tf_op jit(solution)/shard_map/ppermute | solution.py:454
  85.9 0.0 copy-start.2
  85.9 6.0 %collective-permute-done.1.refs_2_ = bf16[512,768]{1,0:T(8,128)(2,1)} collective-permute-done((bf16[512,768]{1,0:T(8,128)(2,1)S(1)}, bf16[512,768]{1,0:T(8,128)(2,1)}, u32[]{:S(2)}, u32[]{:S(2)}) %collective-permute-start.1) | collective-permute-done | bytes 786464 | tf_op jit(solution)/shard_map/ppermute | solution.py:454
  91.9 0.0 copy-done.1
  91.9 0.0 copy-done.2
  91.9 12.3 %fast_weights.5 = (bf16[192,768]{1,0:T(8,128)(2,1)S(1)}, f32[12,64,256]{2,1,0:T(8,128)S(1)}, f32[12,64,256]{2,1,0:T(8,128)S(1)}, f32[64,768]{1,0:T(8,128)S(1)}) custom-call(s32[4]{0:T(128)S(1)} %broadcast_xor_fusion.row_ref, bf16[256,768]{1,0:T(8,128)(2,1)S(1)} %take.10.refs_0_, bf16[256,768]{1,0:T(8,128)(2,1)S(1)} %collective-permute-done.refs_1_, ...), custom_call_target="tpu_custom_call" | custom-call | tf_op jit(solution)/shard_map/fast_weights/pallas_call | solution.py:251
  104.2 0.0 collective-permute-done.4.refs_1_
  104.2 0.1 take.16.refs_1_
  104.3 0.1 collective-permute-start.5
  104.4 3.0 %collective-permute-start.6 = (bf16[128,768]{1,0:T(8,128)(2,1)S(1)}, bf16[128,768]{1,0:T(8,128)(2,1)S(1)}, u32[]{:S(2)}, u32[]{:S(2)}) collective-permute-start(bf16[128,768]{1,0:T(8,128)(2,1)S(1)} %take.14.refs_8_.refs_0_), channel_id=1, source_target_pairs={{0,2},{2,0},{1,3},{3,1},{4,6},{6,4},{5,7},{7,5},{8,10},{10,8},{9,1... | collective-permute-start | bytes 589832 | tf_op jit(solution)/shard_map/ppermute | solution.py:450
  107.4 0.1 collective-permute-start.8
  107.5 9.9 %collective-permute-done.3.refs_2_ = bf16[512,768]{1,0:T(8,128)(2,1)S(1)} collective-permute-done((bf16[512,768]{1,0:T(8,128)(2,1)S(1)}, bf16[512,768]{1,0:T(8,128)(2,1)S(1)}, u32[]{:S(2)}, u32[]{:S(2)}) %collective-permute-start.3) | collective-permute-done | bytes 786464 | tf_op jit(solution)/shard_map/ppermute | solution.py:454
  117.4 11.8 %fast_weights.6 = (bf16[256,768]{1,0:T(8,128)(2,1)S(1)}, f32[12,64,256]{2,1,0:T(8,128)S(1)}, f32[12,64,256]{2,1,0:T(8,128)S(1)}, f32[64,768]{1,0:T(8,128)S(1)}) custom-call(s32[4]{0:T(128)S(1)} %broadcast_xor_fusion.row_ref, bf16[256,768]{1,0:T(8,128)(2,1)S(1)} %take.12.refs_0_, bf16[256,768]{1,0:T(8,128)(2,1)S(1)} %collective-permute-done.2.refs_1_, ...), custom_call_target="tpu_custom_call" | custom-call | tf_op jit(solution)/shard_map/fast_weights/pallas_call | solution.py:251
  129.2 0.0 collective-permute-done.6.refs_1_
  129.3 2.8 %collective-permute-start.7 = (bf16[256,768]{1,0:T(8,128)(2,1)S(1)}, bf16[256,768]{1,0:T(8,128)(2,1)S(1)}, u32[]{:S(2)}, u32[]{:S(2)}) collective-permute-start(bf16[256,768]{1,0:T(8,128)(2,1)S(1)} %take.18.refs_8_), channel_id=1, source_target_pairs={{0,1},{1,0},{2,3},{3,2},{4,5},{5,4},{6,7},{7,6},{8,9},{9,8},{10,11... | collective-permute-start | bytes 1179656 | tf_op jit(solution)/shard_map/ppermute | solution.py:454
  132.1 0.3 collective-permute-done.5.refs_2_
  132.4 12.0 %fast_weights.7 = (bf16[256,768]{1,0:T(8,128)(2,1)S(1)}, f32[12,64,256]{2,1,0:T(8,128)S(1)}, f32[12,64,256]{2,1,0:T(8,128)S(1)}, f32[64,768]{1,0:T(8,128)S(1)}) custom-call(s32[4]{0:T(128)S(1)} %broadcast_xor_fusion.row_ref, bf16[256,768]{1,0:T(8,128)(2,1)S(1)} %take.15.refs_0_, bf16[256,768]{1,0:T(8,128)(2,1)S(1)} %collective-permute-done.4.refs_1_, ...), custom_call_target="tpu_custom_call" | custom-call | tf_op jit(solution)/shard_map/fast_weights/pallas_call | solution.py:251
  144.5 0.0 collective-permute-done.8.refs_1_
  144.5 0.1 collective-permute-start.9
  144.7 0.0 collective-permute-done.7.refs_2_
  144.7 6.4 %fast_weights.8 = (bf16[128,768]{1,0:T(8,128)(2,1)S(1)}, f32[12,64,256]{2,1,0:T(8,128)S(1)}, f32[12,64,256]{2,1,0:T(8,128)S(1)}, f32[64,768]{1,0:T(8,128)S(1)}) custom-call(s32[4]{0:T(128)S(1)} %broadcast_xor_fusion.row_ref, bf16[128,768]{1,0:T(8,128)(2,1)S(1)} %take.14.refs_8_.refs_0_, bf16[128,768]{1,0:T(8,128)(2,1)S(1)} %collective-permute-done.6.refs_1_, ...), custom_call_target="tpu_custom_call" | custom-call | tf_op jit(solution)/shard_map/fast_weights/pallas_call | solution.py:251
  151.2 2.7 %collective-permute-done.9.refs_2_ = bf16[256,768]{1,0:T(8,128)(2,1)S(1)} collective-permute-done((bf16[256,768]{1,0:T(8,128)(2,1)S(1)}, bf16[256,768]{1,0:T(8,128)(2,1)S(1)}, u32[]{:S(2)}, u32[]{:S(2)}) %collective-permute-start.9) | collective-permute-done | bytes 393248 | tf_op jit(solution)/shard_map/ppermute | solution.py:454
  153.9 7.7 %fast_weights.9 = (bf16[192,768]{1,0:T(8,128)(2,1)S(1)}, f32[12,64,256]{2,1,0:T(8,128)}, f32[12,64,256]{2,1,0:T(8,128)}, f32[64,768]{1,0:T(8,128)}) custom-call(s32[4]{0:T(128)S(1)} %broadcast_xor_fusion.row_ref, bf16[128,768]{1,0:T(8,128)(2,1)S(1)} %take.17.refs_8_.refs_0_, bf16[128,768]{1,0:T(8,128)(2,1)S(1)} %collective-permute-done.8.refs_1_, ...), custom_call_target="tpu_custom_call" | custom-call | tf_op jit(solution)/shard_map/fast_weights/pallas_call | solution.py:251
  161.6 23.4 %all_to_all.11 = bf16[8,128,768]{2,1,0:T(8,128)(2,1)S(1)} all-to-all(bf16[8,128,768]{2,1,0:T(8,128)(2,1)S(1)} %bitcast.11), channel_id=1, replica_groups=mesh['seg'=8,'head'=4] {'seg'}, dimensions={0} | all-to-all | bytes 3145728 | tf_op jit(solution)/shard_map/all_to_all | solution.py:473
  185.0 1.1 copy.15
  (17 shorter events, 0.3 us)
Async XLA Ops:
  35.0 2.7 %copy-start.3 = (f32[12,64,256]{2,1,0:T(8,128)S(1)}, f32[12,64,256]{2,1,0:T(8,128)}, u32[]{:S(2)}) copy-start(f32[12,64,256]{2,1,0:T(8,128)} %param.15) | copy-start | bytes 2359300
  35.1 19.6 %collective-permute-start = (bf16[256,768]{1,0:T(8,128)(2,1)S(1)}, bf16[256,768]{1,0:T(8,128)(2,1)S(1)}, u32[]{:S(2)}, u32[]{:S(2)}) collective-permute-start(bf16[256,768]{1,0:T(8,128)(2,1)S(1)} %take.10.refs_0_), channel_id=1, source_target_pairs={{0,2},{2,0},{1,3},{3,1},{4,6},{6,4},{5,7},{7,5},{8,10},{10,8},{9,1... | collective-permute-start | bytes 1179656 | tf_op jit(solution)/shard_map/ppermute | solution.py:450
  54.7 37.2 %collective-permute-start.1 = (bf16[512,768]{1,0:T(8,128)(2,1)S(1)}, bf16[512,768]{1,0:T(8,128)(2,1)}, u32[]{:S(2)}, u32[]{:S(2)}) collective-permute-start(bf16[512,768]{1,0:T(8,128)(2,1)S(1)} %take.11.refs_2_), channel_id=1, source_target_pairs={{0,1},{1,0},{2,3},{3,2},{4,5},{5,4},{6,7},{7,6},{8,9},{9,8},{10,11... | collective-permute-start | bytes 2359304 | tf_op jit(solution)/shard_map/ppermute | solution.py:454
  55.5 3.5 %copy-start.4 = (f32[12,64,256]{2,1,0:T(8,128)S(1)}, f32[12,64,256]{2,1,0:T(8,128)}, u32[]{:S(2)}) copy-start(f32[12,64,256]{2,1,0:T(8,128)} %param.15) | copy-start | bytes 2359300
  55.5 26.4 %collective-permute-start.2 = (bf16[256,768]{1,0:T(8,128)(2,1)S(1)}, bf16[256,768]{1,0:T(8,128)(2,1)S(1)}, u32[]{:S(2)}, u32[]{:S(2)}) collective-permute-start(bf16[256,768]{1,0:T(8,128)(2,1)S(1)} %take.12.refs_0_), channel_id=1, source_target_pairs={{0,2},{2,0},{1,3},{3,1},{4,6},{6,4},{5,7},{7,5},{8,10},{10,8},{9,1... | collective-permute-start | bytes 1179656 | tf_op jit(solution)/shard_map/ppermute | solution.py:450
  59.0 5.0 %copy-start = (bf16[3072,2304]{1,0:T(8,128)(2,1)S(1)}, bf16[3072,2304]{1,0:T(8,128)(2,1)}, u32[]{:S(2)}) copy-start(bf16[3072,2304]{1,0:T(8,128)(2,1)} %refs_4_.9) | copy-start | bytes 42467332
  64.0 1.1 copy-start.5
  64.0 27.9 %copy-start.1 = (bf16[3072,2304]{1,0:T(8,128)(2,1)S(1)}, bf16[3072,2304]{1,0:T(8,128)(2,1)}, u32[]{:S(2)}) copy-start(bf16[3072,2304]{1,0:T(8,128)(2,1)} %refs_4_.9) | copy-start | bytes 42467332
  64.1 40.1 %collective-permute-start.4 = (bf16[256,768]{1,0:T(8,128)(2,1)S(1)}, bf16[256,768]{1,0:T(8,128)(2,1)S(1)}, u32[]{:S(2)}, u32[]{:S(2)}) collective-permute-start(bf16[256,768]{1,0:T(8,128)(2,1)S(1)} %take.15.refs_0_), channel_id=1, source_target_pairs={{0,2},{2,0},{1,3},{3,1},{4,6},{6,4},{5,7},{7,5},{8,10},{10,8},{9,1... | collective-permute-start | bytes 1179656 | tf_op jit(solution)/shard_map/ppermute | solution.py:450
  81.9 35.5 %collective-permute-start.3 = (bf16[512,768]{1,0:T(8,128)(2,1)S(1)}, bf16[512,768]{1,0:T(8,128)(2,1)S(1)}, u32[]{:S(2)}, u32[]{:S(2)}) collective-permute-start(bf16[512,768]{1,0:T(8,128)(2,1)S(1)} %take.13.refs_1_), channel_id=1, source_target_pairs={{0,1},{1,0},{2,3},{3,2},{4,5},{5,4},{6,7},{7,6},{8,9},{9,8},{10,11... | collective-permute-start | bytes 2359304 | tf_op jit(solution)/shard_map/ppermute | solution.py:454
  85.9 6.1 %copy-start.2 = (f32[12,64,256]{2,1,0:T(8,128)S(1)}, f32[12,64,256]{2,1,0:T(8,128)}, u32[]{:S(2)}) copy-start(f32[12,64,256]{2,1,0:T(8,128)} %refs_5_.1) | copy-start | bytes 2359300
  104.3 28.2 %collective-permute-start.5 = (bf16[512,768]{1,0:T(8,128)(2,1)S(1)}, bf16[512,768]{1,0:T(8,128)(2,1)S(1)}, u32[]{:S(2)}, u32[]{:S(2)}) collective-permute-start(bf16[512,768]{1,0:T(8,128)(2,1)S(1)} %take.16.refs_1_), channel_id=1, source_target_pairs={{0,1},{1,0},{2,3},{3,2},{4,5},{5,4},{6,7},{7,6},{8,9},{9,8},{10,11... | collective-permute-start | bytes 2359304 | tf_op jit(solution)/shard_map/ppermute | solution.py:454
  104.4 24.9 %collective-permute-start.6 = (bf16[128,768]{1,0:T(8,128)(2,1)S(1)}, bf16[128,768]{1,0:T(8,128)(2,1)S(1)}, u32[]{:S(2)}, u32[]{:S(2)}) collective-permute-start(bf16[128,768]{1,0:T(8,128)(2,1)S(1)} %take.14.refs_8_.refs_0_), channel_id=1, source_target_pairs={{0,2},{2,0},{1,3},{3,1},{4,6},{6,4},{5,7},{7,5},{8,10},{10,8},{9,1... | collective-permute-start | bytes 589832 | tf_op jit(solution)/shard_map/ppermute | solution.py:450
  107.4 37.1 %collective-permute-start.8 = (bf16[128,768]{1,0:T(8,128)(2,1)S(1)}, bf16[128,768]{1,0:T(8,128)(2,1)S(1)}, u32[]{:S(2)}, u32[]{:S(2)}) collective-permute-start(bf16[128,768]{1,0:T(8,128)(2,1)S(1)} %take.17.refs_8_.refs_0_), channel_id=1, source_target_pairs={{0,2},{2,0},{1,3},{3,1},{4,6},{6,4},{5,7},{7,5},{8,10},{10,8},{9,1... | collective-permute-start | bytes 589832 | tf_op jit(solution)/shard_map/ppermute | solution.py:450
  129.3 15.4 %collective-permute-start.7 = (bf16[256,768]{1,0:T(8,128)(2,1)S(1)}, bf16[256,768]{1,0:T(8,128)(2,1)S(1)}, u32[]{:S(2)}, u32[]{:S(2)}) collective-permute-start(bf16[256,768]{1,0:T(8,128)(2,1)S(1)} %take.18.refs_8_), channel_id=1, source_target_pairs={{0,1},{1,0},{2,3},{3,2},{4,5},{5,4},{6,7},{7,6},{8,9},{9,8},{10,11... | collective-permute-start | bytes 1179656 | tf_op jit(solution)/shard_map/ppermute | solution.py:454
  144.5 9.3 %collective-permute-start.9 = (bf16[256,768]{1,0:T(8,128)(2,1)S(1)}, bf16[256,768]{1,0:T(8,128)(2,1)S(1)}, u32[]{:S(2)}, u32[]{:S(2)}) collective-permute-start(bf16[256,768]{1,0:T(8,128)(2,1)S(1)} %take.19.refs_8_), channel_id=1, source_target_pairs={{0,1},{1,0},{2,3},{3,2},{4,5},{5,4},{6,7},{7,6},{8,9},{9,8},{10,11... | collective-permute-start | bytes 1179656 | tf_op jit(solution)/shard_map/ppermute | solution.py:454
